TPU v7x, 32 devices: a whole 2x2x4 slice. The times are simulated.
32 devices in a mesh: outer: 4 (over y, x), inner: 8 (over z, core).
Axes of the slice: x: 2, y: 2, z: 4, core: 2. Of those that a mesh axis runs over, the one named last changes fastest.
Arguments:
- frames: bfloat16 [16384, 1536], P(('outer', 'inner')), may hold values from -6 to 6
- w_qkv: bfloat16 [1536, 2304], replicated, may hold values from -64 to 64, as said below
- w_out: bfloat16 [768, 1536], replicated, may hold values from -0.21875 to 0.21875
- w_point: bfloat16 [1536, 3072], replicated, may hold values from -0.15625 to 0.15625
- conv_kernel: float32 [31, 1536], replicated, may hold values from -1 to 1
Outputs:
- block_out: bfloat16 [16384, 1536], P(('outer', 'inner'))
Inputs may be any that keep to these rules, and one draw needn't show every extreme that they name: `w_qkv`: the query, key and value projections side by side, 768 columns each.
All inputs are finite; a program needn't handle non-finite values.
Results may differ from a plain program's by a relative error of at most 0.005.
The roundings to bfloat16 on the way count: a program that leaves them out, or rounds other values in their place, can miss the bound.
Values may be sent and summed in bfloat16 or wider, within the bound.
A program may use at most 128 MiB of HBM per device.

v0:
```python
import jax
import jax.numpy as jnp
from jax import lax
from jax.sharding import PartitionSpec as P

D = 1536
HEADS = 12
HEAD_DIM = 64
KW = 31
HD = 768
WINDOW = 1024


def shifted(array, axis, by):
    peers = lax.axis_size(axis)
    pairs = [(i, i + by) for i in range(peers) if 0 <= i + by < peers]
    return lax.ppermute(array, axis, pairs)


def with_halo(cells, sides, width):
    for axis, dim in sides:
        count = lax.axis_size(axis)
        ends = count - 1
        head = lax.slice_in_dim(cells, 0, width, axis=dim)
        tail = lax.slice_in_dim(cells, cells.shape[dim] - width, cells.shape[dim], axis=dim)
        cells = jnp.concatenate(
            [
                lax.ppermute(tail, axis, [(i, (i + 1) % count) for i in range(ends)]),
                cells,
                lax.ppermute(head, axis, [((i + 1) % count, i) for i in range(ends)]),
            ],
            axis=dim,
        )
    return cells


def layer_norm(values):
    average = jnp.mean(values, -1, keepdims=True)
    centred = values - average
    return centred * lax.rsqrt(jnp.mean(centred * centred, -1, keepdims=True) + 1e-05)


def attend(queries, keyvals, query_pos, key_pos, total_frames):
    query_count = queries.shape[0]
    key_count = keyvals.shape[0]
    allowed = (
        (jnp.abs(query_pos[:, None] - key_pos[None, :]) <= WINDOW)
        & (key_pos[None, :] >= 0)
        & (key_pos[None, :] < total_frames)
    )
    head_queries = queries.reshape(query_count, HEADS, HEAD_DIM).transpose(1, 0, 2)
    head_keys = keyvals[:, :HD].reshape(key_count, HEADS, HEAD_DIM).transpose(1, 0, 2)
    head_values = keyvals[:, HD:].reshape(key_count, HEADS, HEAD_DIM).transpose(1, 0, 2)

    def one_head(operands):
        query_part, key_part, value_part = operands
        scores = jnp.dot(query_part, key_part.T, preferred_element_type=jnp.float32) * HEAD_DIM ** (
            -0.5
        )
        scores = jnp.where(allowed, scores, -1e30)
        highest = jnp.max(scores, -1, keepdims=True)
        expo = jnp.exp(scores - highest)
        totals = jnp.sum(expo, -1, keepdims=True)
        weighted = jnp.dot(
            expo.astype(jnp.bfloat16), value_part, preferred_element_type=jnp.float32
        )
        return (weighted / totals).astype(jnp.bfloat16)

    result = lax.map(one_head, (head_queries, head_keys, head_values))
    return result.transpose(1, 0, 2).reshape(query_count, HD)


def on_device(frames, w_qkv, w_out, w_point, conv_kernel):
    frame_count = frames.shape[0]
    inputs = frames.astype(jnp.float32)
    normed = layer_norm(inputs).astype(jnp.bfloat16)
    projections = jnp.dot(normed, w_qkv, preferred_element_type=jnp.float32).astype(jnp.bfloat16)
    queries = projections[:, :HD]
    keyvals = projections[:, HD:]
    block_index = lax.axis_index(("outer", "inner"))
    block_count = lax.axis_size(("outer", "inner"))

    def fetch_block(offset):
        return shifted(keyvals, ("outer", "inner"), offset)

    pieces = [fetch_block(2), fetch_block(1), keyvals, fetch_block(-1), fetch_block(-2)]
    context = jnp.concatenate(pieces, 0)
    first_row = block_index * frame_count
    query_pos = first_row + jnp.arange(frame_count, dtype=jnp.int32)
    key_pos = first_row - 2 * frame_count + jnp.arange(5 * frame_count, dtype=jnp.int32)
    attended = attend(queries, context, query_pos, key_pos, block_count * frame_count)
    after_attention = inputs + jnp.dot(attended, w_out, preferred_element_type=jnp.float32)
    normed_again = layer_norm(after_attention).astype(jnp.bfloat16)
    projected = jnp.dot(normed_again, w_point, preferred_element_type=jnp.float32)
    gated = (projected[:, :D] * jax.nn.sigmoid(projected[:, D:])).astype(jnp.bfloat16)
    half_width = (KW - 1) // 2
    gated_wide = with_halo(gated, ((("outer", "inner"), 0),), half_width)
    depthwise = jnp.zeros((frame_count, D), jnp.float32)
    for tap in range(KW):
        depthwise = depthwise + conv_kernel[tap][None, :] * gated_wide[
            tap : tap + frame_count
        ].astype(jnp.float32)
    return (after_attention + jax.nn.silu(layer_norm(depthwise))).astype(jnp.bfloat16)


def solution(mesh):
    return jax.shard_map(
        on_device,
        mesh=mesh,
        in_specs=(P(("outer", "inner"), None), P(), P(), P(), P()),
        out_specs=P(("outer", "inner"), None),
        check_vma=False,
    )
```

profile of v0, /device:TPU:4, one launch (start us, length us, event | category | flops | bytes accessed | tf_op | source)
XLA Modules:
  0.0 255.4 jit_solution(912894042791079802)
XLA Ops:
  0.0 1.8 convert_reduce_fusion
  1.9 2.0 fusion.31
  3.8 7.3 %convolution_convert_fusion = bf16[512,2304]{1,0:T(8,128)(2,1)S(1)} fusion(bf16[1536,2304]{1,0:T(8,128)(2,1)} %param.8, bf16[512,1536]{1,0:T(8,128)(2,1)S(1)} %copy-done.1, f32[512]{0:T(512)S(1)} %add_rsqrt_fusion.2, f32[512]{0:T(512)S(1)} %broadcast_multiply_fusion.2), kind=kOutput, calls=%fused_computation.53 | convolution fusion | flops 3628204032 | bytes 11014144 | tf_op jit(solution)/shard_map/dot_general | solution.py:77
  13.8 3.5 %collective-permute-start = (bf16[512,1536]{1,0:T(8,128)(2,1)}, bf16[512,1536]{1,0:T(8,128)(2,1)}, u32[]{:S(2)}, u32[]{:S(2)}) collective-permute-start(bf16[512,1536]{1,0:T(8,128)(2,1)} %slice.307), channel_id=1, source_target_pairs={{0,2},{1,3},{2,4},{3,5},{4,6},{5,7},{6,8},{7,9},{8,10},{9,11},{10,... | collective-permute-start | bytes 4718600 | tf_op jit(solution)/shard_map/ppermute | solution.py:17
  17.3 1.9 collective-permute-start.1
  19.2 7.2 %collective-permute-start.2 = (bf16[512,1536]{1,0:T(8,128)(2,1)}, bf16[512,1536]{1,0:T(8,128)(2,1)}, u32[]{:S(2)}, u32[]{:S(2)}) collective-permute-start(bf16[512,1536]{1,0:T(8,128)(2,1)} %slice.307), channel_id=1, source_target_pairs={{1,0},{2,1},{3,2},{4,3},{5,4},{6,5},{7,6},{8,7},{9,8},{10,9},{11,1... | collective-permute-start | bytes 4718600 | tf_op jit(solution)/shard_map/ppermute | solution.py:17
  26.5 2.5 collective-permute-start.3
  31.8 25.3 %collective-permute-done = bf16[512,1536]{1,0:T(8,128)(2,1)} collective-permute-done((bf16[512,1536]{1,0:T(8,128)(2,1)}, bf16[512,1536]{1,0:T(8,128)(2,1)}, u32[]{:S(2)}, u32[]{:S(2)}) %collective-permute-start) | collective-permute-done | bytes 1572896 | tf_op jit(solution)/shard_map/ppermute | solution.py:17
  57.0 1.5 constant_dynamic-update-slice_fusion.4
  58.5 29.8 %collective-permute-done.1 = bf16[512,1536]{1,0:T(8,128)(2,1)} collective-permute-done((bf16[512,1536]{1,0:T(8,128)(2,1)}, bf16[512,1536]{1,0:T(8,128)(2,1)}, u32[]{:S(2)}, u32[]{:S(2)}) %collective-permute-start.1) | collective-permute-done | bytes 1572896 | tf_op jit(solution)/shard_map/ppermute | solution.py:17
  88.3 1.5 constant_dynamic-update-slice_fusion.3
  90.0 1.5 constant_dynamic-update-slice_fusion.1
  91.5 30.8 %collective-permute-done.3 = bf16[512,1536]{1,0:T(8,128)(2,1)} collective-permute-done((bf16[512,1536]{1,0:T(8,128)(2,1)}, bf16[512,1536]{1,0:T(8,128)(2,1)}, u32[]{:S(2)}, u32[]{:S(2)}) %collective-permute-start.3) | collective-permute-done | bytes 1572896 | tf_op jit(solution)/shard_map/ppermute | solution.py:17
  122.3 1.5 constant_dynamic-update-slice_fusion
  123.8 3.5 %fusion.76 = (bf16[2560,768]{1,0:T(8,128)(2,1)}, bf16[2560,768]{1,0:T(8,128)(2,1)}) fusion(bf16[2560,1536]{1,0:T(8,128)(2,1)S(1)} %constant_dynamic-update-slice_fusion), kind=kLoop, calls=%fused_computation.168 | loop fusion | bytes 15728640 | tf_op jit(solution)/shard_map/slice | solution.py:53
  127.3 6.2 %copy.10 = bf16[2560,768]{0,1:T(8,128)(2,1)} copy(bf16[2560,768]{1,0:T(8,128)(2,1)} %get-tuple-element.125) | data formatting | bytes 7864320 | tf_op jit(solution)/shard_map/slice | solution.py:52
  133.5 6.3 %copy.11 = bf16[2560,768]{0,1:T(8,128)(2,1)} copy(bf16[2560,768]{1,0:T(8,128)(2,1)} %get-tuple-element.124) | data formatting | bytes 7864320 | tf_op jit(solution)/shard_map/slice | solution.py:53
  139.8 74.6 %while.11 = (s32[]{:T(128)}, bf16[12,512,64]{1,2,0:T(8,128)(2,1)S(1)}, bf16[12,512,64]{1,2,0:T(8,128)(2,1)}, bf16[12,2560,64]{1,2,0:T(8,128)(2,1)}, bf16[12,2560...) while((s32[]{:T(128)}, ...), condition=%wide.region_5.6_spmd.clone, body=%wide.region_2.5_spmd.clone.sunk | while | flops 351337472 | bytes 16544869 | solution.py:69
  139.8 3.4 %fusion.90 = (f32[512]{0:T(512)S(1)}, f32[512,2560]{1,0:T(8,128)S(1)}) fusion(bf16[12,2560,64]{1,2,0:T(8,128)(2,1)} %get-tuple-element.214, s32[]{:T(128)} %get-tuple-element.201, bf16[12,512,64]{1,2,0:T(8,128)(2,1)} %get-tuple-element.213, pred[2560]{0:T(1024)(128)(4,1)S(1)} %get-tuple-element.219, pred[2560]{0:T(1024)(128)(4,1)S(1)} %get-tuple-element.218, ...), kind=kOutput, calls=%fused_computation.167.clone.1 | convolution fusion | flops 178257408 | bytes 5656576 | tf_op jit(solution)/shard_map/while/body/eval_jaxpr/dot_general | solution.py:57
  144.1 2.0 fusion.92
  146.0 3.4 %fusion.90 = (f32[512]{0:T(512)S(1)}, f32[512,2560]{1,0:T(8,128)S(1)}) fusion(bf16[12,2560,64]{1,2,0:T(8,128)(2,1)} %get-tuple-element.214, s32[]{:T(128)} %get-tuple-element.201, bf16[12,512,64]{1,2,0:T(8,128)(2,1)} %get-tuple-element.213, pred[2560]{0:T(1024)(128)(4,1)S(1)} %get-tuple-element.219, pred[2560]{0:T(1024)(128)(4,1)S(1)} %get-tuple-element.218, ...), kind=kOutput, calls=%fused_computation.167.clone.1 | convolution fusion | flops 178257408 | bytes 5656576 | tf_op jit(solution)/shard_map/while/body/eval_jaxpr/dot_general | solution.py:57
  150.3 2.0 fusion.92
  152.3 3.4 %fusion.90 = (f32[512]{0:T(512)S(1)}, f32[512,2560]{1,0:T(8,128)S(1)}) fusion(bf16[12,2560,64]{1,2,0:T(8,128)(2,1)} %get-tuple-element.214, s32[]{:T(128)} %get-tuple-element.201, bf16[12,512,64]{1,2,0:T(8,128)(2,1)} %get-tuple-element.213, pred[2560]{0:T(1024)(128)(4,1)S(1)} %get-tuple-element.219, pred[2560]{0:T(1024)(128)(4,1)S(1)} %get-tuple-element.218, ...), kind=kOutput, calls=%fused_computation.167.clone.1 | convolution fusion | flops 178257408 | bytes 5656576 | tf_op jit(solution)/shard_map/while/body/eval_jaxpr/dot_general | solution.py:57
  156.5 2.0 fusion.92
  158.5 3.4 %fusion.90 = (f32[512]{0:T(512)S(1)}, f32[512,2560]{1,0:T(8,128)S(1)}) fusion(bf16[12,2560,64]{1,2,0:T(8,128)(2,1)} %get-tuple-element.214, s32[]{:T(128)} %get-tuple-element.201, bf16[12,512,64]{1,2,0:T(8,128)(2,1)} %get-tuple-element.213, pred[2560]{0:T(1024)(128)(4,1)S(1)} %get-tuple-element.219, pred[2560]{0:T(1024)(128)(4,1)S(1)} %get-tuple-element.218, ...), kind=kOutput, calls=%fused_computation.167.clone.1 | convolution fusion | flops 178257408 | bytes 5656576 | tf_op jit(solution)/shard_map/while/body/eval_jaxpr/dot_general | solution.py:57
  162.7 2.0 fusion.92
  164.7 3.4 %fusion.90 = (f32[512]{0:T(512)S(1)}, f32[512,2560]{1,0:T(8,128)S(1)}) fusion(bf16[12,2560,64]{1,2,0:T(8,128)(2,1)} %get-tuple-element.214, s32[]{:T(128)} %get-tuple-element.201, bf16[12,512,64]{1,2,0:T(8,128)(2,1)} %get-tuple-element.213, pred[2560]{0:T(1024)(128)(4,1)S(1)} %get-tuple-element.219, pred[2560]{0:T(1024)(128)(4,1)S(1)} %get-tuple-element.218, ...), kind=kOutput, calls=%fused_computation.167.clone.1 | convolution fusion | flops 178257408 | bytes 5656576 | tf_op jit(solution)/shard_map/while/body/eval_jaxpr/dot_general | solution.py:57
  168.9 2.0 fusion.92
  170.9 3.4 %fusion.90 = (f32[512]{0:T(512)S(1)}, f32[512,2560]{1,0:T(8,128)S(1)}) fusion(bf16[12,2560,64]{1,2,0:T(8,128)(2,1)} %get-tuple-element.214, s32[]{:T(128)} %get-tuple-element.201, bf16[12,512,64]{1,2,0:T(8,128)(2,1)} %get-tuple-element.213, pred[2560]{0:T(1024)(128)(4,1)S(1)} %get-tuple-element.219, pred[2560]{0:T(1024)(128)(4,1)S(1)} %get-tuple-element.218, ...), kind=kOutput, calls=%fused_computation.167.clone.1 | convolution fusion | flops 178257408 | bytes 5656576 | tf_op jit(solution)/shard_map/while/body/eval_jaxpr/dot_general | solution.py:57
  175.2 2.0 fusion.92
  177.1 3.4 %fusion.90 = (f32[512]{0:T(512)S(1)}, f32[512,2560]{1,0:T(8,128)S(1)}) fusion(bf16[12,2560,64]{1,2,0:T(8,128)(2,1)} %get-tuple-element.214, s32[]{:T(128)} %get-tuple-element.201, bf16[12,512,64]{1,2,0:T(8,128)(2,1)} %get-tuple-element.213, pred[2560]{0:T(1024)(128)(4,1)S(1)} %get-tuple-element.219, pred[2560]{0:T(1024)(128)(4,1)S(1)} %get-tuple-element.218, ...), kind=kOutput, calls=%fused_computation.167.clone.1 | convolution fusion | flops 178257408 | bytes 5656576 | tf_op jit(solution)/shard_map/while/body/eval_jaxpr/dot_general | solution.py:57
  181.4 2.0 fusion.92
  183.4 3.4 %fusion.90 = (f32[512]{0:T(512)S(1)}, f32[512,2560]{1,0:T(8,128)S(1)}) fusion(bf16[12,2560,64]{1,2,0:T(8,128)(2,1)} %get-tuple-element.214, s32[]{:T(128)} %get-tuple-element.201, bf16[12,512,64]{1,2,0:T(8,128)(2,1)} %get-tuple-element.213, pred[2560]{0:T(1024)(128)(4,1)S(1)} %get-tuple-element.219, pred[2560]{0:T(1024)(128)(4,1)S(1)} %get-tuple-element.218, ...), kind=kOutput, calls=%fused_computation.167.clone.1 | convolution fusion | flops 178257408 | bytes 5656576 | tf_op jit(solution)/shard_map/while/body/eval_jaxpr/dot_general | solution.py:57
  187.6 2.0 fusion.92
  189.6 3.4 %fusion.90 = (f32[512]{0:T(512)S(1)}, f32[512,2560]{1,0:T(8,128)S(1)}) fusion(bf16[12,2560,64]{1,2,0:T(8,128)(2,1)} %get-tuple-element.214, s32[]{:T(128)} %get-tuple-element.201, bf16[12,512,64]{1,2,0:T(8,128)(2,1)} %get-tuple-element.213, pred[2560]{0:T(1024)(128)(4,1)S(1)} %get-tuple-element.219, pred[2560]{0:T(1024)(128)(4,1)S(1)} %get-tuple-element.218, ...), kind=kOutput, calls=%fused_computation.167.clone.1 | convolution fusion | flops 178257408 | bytes 5656576 | tf_op jit(solution)/shard_map/while/body/eval_jaxpr/dot_general | solution.py:57
  193.8 2.0 fusion.92
  195.8 3.4 %fusion.90 = (f32[512]{0:T(512)S(1)}, f32[512,2560]{1,0:T(8,128)S(1)}) fusion(bf16[12,2560,64]{1,2,0:T(8,128)(2,1)} %get-tuple-element.214, s32[]{:T(128)} %get-tuple-element.201, bf16[12,512,64]{1,2,0:T(8,128)(2,1)} %get-tuple-element.213, pred[2560]{0:T(1024)(128)(4,1)S(1)} %get-tuple-element.219, pred[2560]{0:T(1024)(128)(4,1)S(1)} %get-tuple-element.218, ...), kind=kOutput, calls=%fused_computation.167.clone.1 | convolution fusion | flops 178257408 | bytes 5656576 | tf_op jit(solution)/shard_map/while/body/eval_jaxpr/dot_general | solution.py:57
  200.0 2.0 fusion.92
  202.0 3.4 %fusion.90 = (f32[512]{0:T(512)S(1)}, f32[512,2560]{1,0:T(8,128)S(1)}) fusion(bf16[12,2560,64]{1,2,0:T(8,128)(2,1)} %get-tuple-element.214, s32[]{:T(128)} %get-tuple-element.201, bf16[12,512,64]{1,2,0:T(8,128)(2,1)} %get-tuple-element.213, pred[2560]{0:T(1024)(128)(4,1)S(1)} %get-tuple-element.219, pred[2560]{0:T(1024)(128)(4,1)S(1)} %get-tuple-element.218, ...), kind=kOutput, calls=%fused_computation.167.clone.1 | convolution fusion | flops 178257408 | bytes 5656576 | tf_op jit(solution)/shard_map/while/body/eval_jaxpr/dot_general | solution.py:57
  206.3 2.0 fusion.92
  208.3 3.4 %fusion.90 = (f32[512]{0:T(512)S(1)}, f32[512,2560]{1,0:T(8,128)S(1)}) fusion(bf16[12,2560,64]{1,2,0:T(8,128)(2,1)} %get-tuple-element.214, s32[]{:T(128)} %get-tuple-element.201, bf16[12,512,64]{1,2,0:T(8,128)(2,1)} %get-tuple-element.213, pred[2560]{0:T(1024)(128)(4,1)S(1)} %get-tuple-element.219, pred[2560]{0:T(1024)(128)(4,1)S(1)} %get-tuple-element.218, ...), kind=kOutput, calls=%fused_computation.167.clone.1 | convolution fusion | flops 178257408 | bytes 5656576 | tf_op jit(solution)/shard_map/while/body/eval_jaxpr/dot_general | solution.py:57
  212.5 2.0 fusion.92
  214.5 3.0 %fusion.78 = (f32[512]{0:T(512)S(1)}, f32[512,1536]{1,0:T(8,128)S(1)}) fusion(bf16[512,768]{0,1:T(8,128)(2,1)S(1)} %bitcast.46, bf16[768,1536]{1,0:T(8,128)(2,1)S(1)} %copy-done, bf16[512,1536]{1,0:T(8,128)(2,1)} %param.7), kind=kOutput, calls=%fused_computation.170 | convolution fusion | flops 1210318336 | bytes 7866368 | tf_op jit(solution)/shard_map/dot_general | solution.py:92
  217.9 7.8 %fusion.38 = f32[512,3072]{1,0:T(8,128)S(1)} fusion(bf16[1536,3072]{1,0:T(8,128)(2,1)} %param.10, f32[512,1536]{1,0:T(8,128)S(1)} %get-tuple-element.129, f32[512]{0:T(512)S(1)} %add_rsqrt_fusion.1, f32[512]{0:T(512)S(1)} %broadcast_multiply_fusion.1), kind=kOutput, calls=%fused_computation.69 | convolution fusion | flops 4834197504 | bytes 18878464 | tf_op jit(solution)/shard_map/dot_general | solution.py:94
  226.5 1.9 collective-permute-start.4
  228.5 7.5 %collective-permute-start.5 = (bf16[15,1536]{1,0:T(8,128)(2,1)S(1)}, bf16[15,1536]{1,0:T(8,128)(2,1)S(1)}, u32[]{:S(2)}, u32[]{:S(2)}) collective-permute-start(bf16[15,1536]{1,0:T(8,128)(2,1)S(1)} %get-tuple-element.127), channel_id=1, source_target_pairs={{1,0},{2,1},{3,2},{4,3},{5,4},{6,5},{7,6},{8,7},{9,8},{10,9},{11,1... | collective-permute-start | bytes 138248 | tf_op jit(solution)/shard_map/ppermute | solution.py:30
  237.5 15.2 %fusion.74 = (f32[512]{0:T(512)S(1)}, f32[512,1536]{1,0:T(8,128)S(1)}) fusion(bf16[15,1536]{1,0:T(8,128)(2,1)S(1)} %collective-permute-done.5, bf16[512,1536]{1,0:T(8,128)(2,1)S(1)} %fusion.37, f32[1536]{0:T(1024)S(1)} %get-tuple-element.100, f32[1536]{0:T(1024)S(1)} %get-tuple-element.101, f32[1536]{0:T(1024)S(1)} %get-tuple-element.72, ...), kind=kLoop, calls=%fused_computation.166 | loop fusion | flops 143916544 | bytes 5003264 | tf_op jit(solution)/shard_map/reduce_sum | solution.py:38
  253.2 2.2 add_convert_fusion
  (47 shorter events, 18.9 us)
Async XLA Ops:
  0.0 214.5 %copy-start = (bf16[768,1536]{1,0:T(8,128)(2,1)S(1)}, bf16[768,1536]{1,0:T(8,128)(2,1)}, u32[]{:S(2)}) copy-start(bf16[768,1536]{1,0:T(8,128)(2,1)} %param.9) | copy-start | bytes 7077892
  0.0 3.8 %copy-start.1 = (bf16[512,1536]{1,0:T(8,128)(2,1)S(1)}, bf16[512,1536]{1,0:T(8,128)(2,1)}, u32[]{:S(2)}) copy-start(bf16[512,1536]{1,0:T(8,128)(2,1)} %param.7) | copy-start | bytes 4718596
  11.1 1.4 copy-start.2
  12.5 18.9 %copy-start.5 = (f32[31,1536]{1,0:T(8,128)S(1)}, f32[31,1536]{1,0:T(8,128)}, u32[]{:S(2)}) copy-start(f32[31,1536]{1,0:T(8,128)} %param.11) | copy-start | bytes 571396
  13.8 43.2 %collective-permute-start = (bf16[512,1536]{1,0:T(8,128)(2,1)}, bf16[512,1536]{1,0:T(8,128)(2,1)}, u32[]{:S(2)}, u32[]{:S(2)}) collective-permute-start(bf16[512,1536]{1,0:T(8,128)(2,1)} %slice.307), channel_id=1, source_target_pairs={{0,2},{1,3},{2,4},{3,5},{4,6},{5,7},{6,8},{7,9},{8,10},{9,11},{10,... | collective-permute-start | bytes 4718600 | tf_op jit(solution)/shard_map/ppermute | solution.py:17
  17.3 71.0 %collective-permute-start.1 = (bf16[512,1536]{1,0:T(8,128)(2,1)}, bf16[512,1536]{1,0:T(8,128)(2,1)}, u32[]{:S(2)}, u32[]{:S(2)}) collective-permute-start(bf16[512,1536]{1,0:T(8,128)(2,1)} %slice.307), channel_id=1, source_target_pairs={{0,1},{1,2},{2,3},{3,4},{4,5},{5,6},{6,7},{7,8},{8,9},{9,10},{10,1... | collective-permute-start | bytes 4718600 | tf_op jit(solution)/shard_map/ppermute | solution.py:17
  19.2 70.8 %collective-permute-start.2 = (bf16[512,1536]{1,0:T(8,128)(2,1)}, bf16[512,1536]{1,0:T(8,128)(2,1)}, u32[]{:S(2)}, u32[]{:S(2)}) collective-permute-start(bf16[512,1536]{1,0:T(8,128)(2,1)} %slice.307), channel_id=1, source_target_pairs={{1,0},{2,1},{3,2},{4,3},{5,4},{6,5},{7,6},{8,7},{9,8},{10,9},{11,1... | collective-permute-start | bytes 4718600 | tf_op jit(solution)/shard_map/ppermute | solution.py:17
  26.5 95.8 %collective-permute-start.3 = (bf16[512,1536]{1,0:T(8,128)(2,1)}, bf16[512,1536]{1,0:T(8,128)(2,1)}, u32[]{:S(2)}, u32[]{:S(2)}) collective-permute-start(bf16[512,1536]{1,0:T(8,128)(2,1)} %slice.307), channel_id=1, source_target_pairs={{2,0},{3,1},{4,2},{5,3},{6,4},{7,5},{8,6},{9,7},{10,8},{11,9},{12,... | collective-permute-start | bytes 4718600 | tf_op jit(solution)/shard_map/ppermute | solution.py:17
  31.7 58.1 %copy-start.3 = (bf16[512,2304]{1,0:T(8,128)(2,1)S(1)}, bf16[512,2304]{1,0:T(8,128)(2,1)}, u32[]{:S(2)}) copy-start(bf16[512,2304]{1,0:T(8,128)(2,1)} %copy-done.2) | copy-start | bytes 7077892
  133.5 6.3 %copy-start.4 = (bf16[12,512,64]{1,2,0:T(8,128)(2,1)S(1)}, bf16[12,512,64]{1,2,0:T(8,128)(2,1)}, u32[]{:S(2)}) copy-start(bf16[12,512,64]{1,2,0:T(8,128)(2,1)} %custom-call.1) | copy-start | bytes 2359300
  226.5 9.6 %collective-permute-start.4 = (bf16[15,1536]{1,0:T(8,128)(2,1)S(1)}, bf16[15,1536]{1,0:T(8,128)(2,1)S(1)}, u32[]{:S(2)}, u32[]{:S(2)}) collective-permute-start(bf16[15,1536]{1,0:T(8,128)(2,1)S(1)} %get-tuple-element.126), channel_id=1, source_target_pairs={{0,1},{1,2},{2,3},{3,4},{4,5},{5,6},{6,7},{7,8},{8,9},{9,10},{10,1... | collective-permute-start | bytes 138248 | tf_op jit(solution)/shard_map/ppermute | solution.py:28
  228.5 9.0 %collective-permute-start.5 = (bf16[15,1536]{1,0:T(8,128)(2,1)S(1)}, bf16[15,1536]{1,0:T(8,128)(2,1)S(1)}, u32[]{:S(2)}, u32[]{:S(2)}) collective-permute-start(bf16[15,1536]{1,0:T(8,128)(2,1)S(1)} %get-tuple-element.127), channel_id=1, source_target_pairs={{1,0},{2,1},{3,2},{4,3},{5,4},{6,5},{7,6},{8,7},{9,8},{10,9},{11,1... | collective-permute-start | bytes 138248 | tf_op jit(solution)/shard_map/ppermute | solution.py:30
where the time goes:
time: 258 us; the launch traced here: 255 us
  waiting for transfers between devices  87.1 us (34%)
  matrix products  82.4 us (32%)
  other arithmetic  33.2 us (13%)
  local copies, waits for them, and re-layouts  27.7 us (11%)
  starting transfers between devices  24.6 us (10%)
    ppermute x4, waiting for transfers between devices, shifted(): return lax.ppermute(array, axis, pairs)  85.8 us
    dot_general x12, matrix products, one_head(): jnp.dot(query_part, key_part.T, preferred_element_type=jnp.float32)  40.7 us
    dot_general x12, matrix products, one_head(): jnp.dot(expo.astype(jnp.bfloat16), value_part, preferred_element_type=jnp...  23.7 us
    reduce_sum x2, other arithmetic, layer_norm(): average = jnp.mean(values, -1, keepdims=True)  17.1 us
    ppermute x4, starting transfers between devices, shifted(): return lax.ppermute(array, axis, pairs)  15.2 us
    reduce_sum x12, other arithmetic, one_head(): totals = jnp.sum(expo, -1, keepdims=True)  10.2 us
    slice x2, local copies, waits for them, and re-layouts, attend(): keyvals[:, HD:].reshape(key_count, HEADS, HEAD_DIM).transpose(1, 0, 2)  9.81 us
    dot_general x1, matrix products, on_device(): jnp.dot(normed_again, w_point, preferred_element_type=jnp.float32)  7.78 us
  transfers between devices with their start and end apart: 6, of which 4 were waited for; matrix products, arithmetic and copies ran while one was open for 3% of the time, Pallas kernels for 0%

commit v1 on v0

v1 whole, which is shorter than its diff:
```python
import functools

import jax
import jax.numpy as jnp
from jax import lax
from jax.experimental import pallas as pl
from jax.experimental.pallas import tpu as pltpu
from jax.sharding import PartitionSpec as P

D = 1536
HEADS = 12
HEAD_DIM = 64
KW = 31
HD = 768
AXES = ("outer", "inner")
LANES = 128
PAIRS = HD // LANES
NEG = -1e30


def layer_norm(values):
    average = jnp.mean(values, -1, keepdims=True)
    centred = values - average
    return centred * lax.rsqrt(jnp.mean(centred * centred, -1, keepdims=True) + 1e-05)


def scores_of(queries, keys):
    return lax.dot_general(
        queries, keys, (((1,), (1,)), ((), ())), preferred_element_type=jnp.float32
    )


def head_queries(pair, lane, head):
    picked = jnp.where((lane >= HEAD_DIM) == (head == 1), pair * HEAD_DIM**-0.5, 0.0)
    return picked.astype(jnp.bfloat16)


def softmax_parts(scores, values, highest):
    for part in scores:
        highest = jnp.maximum(highest, jnp.max(part, -1, keepdims=True))
    totals = 0.0
    weighted = 0.0
    for part, value in zip(scores, values):
        expo = jnp.exp(part - highest)
        totals = totals + jnp.sum(expo, -1, keepdims=True)
        weighted = weighted + jnp.dot(
            expo.astype(jnp.bfloat16), value, preferred_element_type=jnp.float32
        )
    return highest, totals, weighted


def near_kernel(rows, q_ref, k0_ref, k1_ref, v0_ref, v1_ref, acc_ref, high_ref, total_ref):
    lane = lax.broadcasted_iota(jnp.int32, (rows, LANES), 1)
    for start in range(0, q_ref.shape[0], rows):
        here = pl.ds(start, rows)
        pair = q_ref[here, :].astype(jnp.float32)
        found = []
        for head in range(2):
            queries = head_queries(pair, lane, head)
            scores = [scores_of(queries, ref[...]) for ref in (k0_ref, k1_ref)]
            found.append(softmax_parts(scores, (v0_ref[...], v1_ref[...]), NEG))
        second = lane >= HEAD_DIM
        high_ref[here, :] = jnp.where(second, found[1][0], found[0][0])
        total_ref[here, :] = jnp.where(second, found[1][1], found[0][1])
        acc_ref[here, :] = jnp.where(second, found[1][2], found[0][2])


def far_kernel(
    rows, lim_ref, q_ref, ka_ref, kb_ref, kc_ref, va_ref, vb_ref, vc_ref,
    acc_ref, high_ref, total_ref, out_ref,
):
    lane = lax.broadcasted_iota(jnp.int32, (rows, LANES), 1)
    count = q_ref.shape[0]
    for start in range(0, count, rows):
        here = pl.ds(start, rows)
        pair = q_ref[here, :].astype(jnp.float32)
        before = pl.ds(start, count - start)
        after = pl.ds(0, start + rows)
        gap_a = lax.broadcasted_iota(jnp.int32, (rows, count - start), 1) - (
            lax.broadcasted_iota(jnp.int32, (rows, count - start), 0)
        )
        gap_c = lax.broadcasted_iota(jnp.int32, (rows, start + rows), 1) - (
            lax.broadcasted_iota(jnp.int32, (rows, start + rows), 0) + start
        )
        in_a = gap_a >= lim_ref[0]
        in_c = gap_c <= lim_ref[2]
        bias_b = jnp.where(lim_ref[1] > 0, 0.0, NEG)
        found = []
        for head in range(2):
            queries = head_queries(pair, lane, head)
            scores = [
                jnp.where(in_a, scores_of(queries, ka_ref[before, :]), NEG),
                scores_of(queries, kb_ref[...]) + bias_b,
                jnp.where(in_c, scores_of(queries, kc_ref[after, :]), NEG),
            ]
            values = (va_ref[before, :], vb_ref[...], vc_ref[after, :])
            old = high_ref[here, :][:, head * HEAD_DIM : head * HEAD_DIM + 1]
            found.append(softmax_parts(scores, values, old))
        second = lane >= HEAD_DIM
        highest = jnp.where(second, found[1][0], found[0][0])
        scale = jnp.exp(high_ref[here, :] - highest)
        totals = jnp.where(second, found[1][1], found[0][1]) + scale * total_ref[here, :]
        weighted = jnp.where(second, found[1][2], found[0][2]) + scale * acc_ref[here, :]
        out_ref[here, :] = (weighted / totals).astype(jnp.bfloat16)


def conv_kernel_body(
    rows, gated_ref, left_ref, right_ref, after_ref, taps_ref, out_ref, wide_ref, sum_ref
):
    count = gated_ref.shape[0]
    halo = left_ref.shape[0]
    step = pl.program_id(0)
    blocks = D // LANES

    @pl.when(step == 0)
    def _():
        for block in range(blocks):
            cols = pl.ds(block * LANES, LANES)
            wide_ref[block, :halo, :] = left_ref[:, cols].astype(jnp.float32)
            wide_ref[block, pl.ds(halo, count), :] = gated_ref[:, cols].astype(jnp.float32)
            wide_ref[block, pl.ds(halo + count, halo), :] = right_ref[:, cols].astype(jnp.float32)

    first = pl.multiple_of(step * rows, rows)
    lead = halo - (KW - 1) // 2
    for block in range(blocks):
        cols = pl.ds(block * LANES, LANES)
        total = jnp.zeros((rows, LANES), jnp.float32)
        for tap in range(KW):
            total = total + taps_ref[pl.ds(tap, 1), cols] * (
                wide_ref[block, pl.ds(first + (lead + tap), rows), :]
            )
        sum_ref[:, cols] = total
    normed = layer_norm(sum_ref[...])
    out_ref[...] = (after_ref[...] + normed / (1.0 + jnp.exp(-normed))).astype(jnp.bfloat16)


def call_near(queries, own, other):
    count = queries.shape[0]
    key = pl.BlockSpec((count, LANES), lambda i: (0, i))
    value = pl.BlockSpec((count, LANES), lambda i: (0, i + PAIRS))
    state = jax.ShapeDtypeStruct((count, HD), jnp.float32)
    return pl.pallas_call(
        functools.partial(near_kernel, count // 2),
        grid=(PAIRS,),
        in_specs=[key, key, key, value, value],
        out_specs=[key] * 3,
        out_shape=[state] * 3,
        compiler_params=pltpu.CompilerParams(vmem_limit_bytes=40 << 20),
        cost_estimate=pl.CostEstimate(
            flops=HEADS * 2 * 2 * count * 2 * count * 256,
            bytes_accessed=12 << 20,
            transcendentals=HEADS * count * 2 * count,
        ),
        name="near_attention",
    )(queries, own, other, own, other)


def call_far(limits, queries, a, b, c, state):
    count = queries.shape[0]
    key = pl.BlockSpec((count, LANES), lambda i: (0, i))
    value = pl.BlockSpec((count, LANES), lambda i: (0, i + PAIRS))
    return pl.pallas_call(
        functools.partial(far_kernel, count // 2),
        grid=(PAIRS,),
        in_specs=[pl.BlockSpec(memory_space=pltpu.SMEM)]
        + [key] * 4 + [value] * 3 + [key] * 3,
        out_specs=key,
        out_shape=jax.ShapeDtypeStruct((count, HD), jnp.bfloat16),
        compiler_params=pltpu.CompilerParams(vmem_limit_bytes=40 << 20),
        cost_estimate=pl.CostEstimate(
            flops=HEADS * 2 * 2 * count * 3 * count * 256,
            bytes_accessed=12 << 20,
            transcendentals=HEADS * count * 3 * count,
        ),
        name="far_attention",
    )(limits, queries, a, b, c, a, b, c, *state)


def call_conv(gated, left, right, after, taps):
    count = gated.shape[0]
    halo = left.shape[0]
    rows = 64
    whole = lambda array: pl.BlockSpec(array.shape, lambda i: (0, 0))
    block = pl.BlockSpec((rows, D), lambda i: (i, 0))
    return pl.pallas_call(
        functools.partial(conv_kernel_body, rows),
        grid=(count // rows,),
        in_specs=[whole(gated), whole(left), whole(right), block, whole(taps)],
        out_specs=block,
        out_shape=jax.ShapeDtypeStruct((count, D), jnp.bfloat16),
        scratch_shapes=[
            pltpu.VMEM((D // LANES, count + 2 * halo, LANES), jnp.float32),
            pltpu.VMEM((rows, D), jnp.float32),
        ],
        compiler_params=pltpu.CompilerParams(vmem_limit_bytes=40 << 20),
        name="conv_tail",
    )(gated, left, right, after, taps)


def on_device(frames, w_qkv, w_out, w_point, conv_kernel):
    index = lax.axis_index(AXES)
    total = lax.axis_size(AXES)

    def shifted(array, by):
        pairs = [(i, i + by) for i in range(total) if 0 <= i + by < total]
        return lax.ppermute(array, AXES, pairs)

    def swapped(array):
        return lax.ppermute(array, AXES, [(i, i ^ 1) for i in range(total)])

    inputs = frames.astype(jnp.float32)
    normed = layer_norm(inputs).astype(jnp.bfloat16)
    keyvals = jnp.dot(normed, w_qkv[:, HD:], preferred_element_type=jnp.float32).astype(
        jnp.bfloat16
    )
    from_before = shifted(keyvals, 2)
    from_after = shifted(keyvals, -2)
    other = swapped(keyvals)
    queries = jnp.dot(normed, w_qkv[:, :HD], preferred_element_type=jnp.float32).astype(
        jnp.bfloat16
    )
    even = index % 2 == 0
    state = call_near(queries, keyvals, other)
    from_before, from_after, state = lax.optimization_barrier((from_before, from_after, state))
    bridge = swapped(jnp.where(even, from_after, from_before))
    big = 1 << 20
    limits = jnp.stack([
        jnp.where(index >= 2, 0, big),
        jnp.where(jnp.where(even, index >= 1, index + 1 < total), 1, 0),
        jnp.where(index + 2 < total, 0, -big),
    ]).astype(jnp.int32)
    attended = call_far(limits, queries, from_before, bridge, from_after, state)
    after_attention = inputs + jnp.dot(attended, w_out, preferred_element_type=jnp.float32)
    normed_again = layer_norm(after_attention).astype(jnp.bfloat16)
    projected = jnp.dot(normed_again, w_point, preferred_element_type=jnp.float32)
    gated = (projected[:, :D] * jax.nn.sigmoid(projected[:, D:])).astype(jnp.bfloat16)
    left = shifted(gated[-16:], 1)
    right = shifted(gated[:16], -1)
    return call_conv(gated, left, right, after_attention, conv_kernel)


def solution(mesh):
    return jax.shard_map(
        on_device,
        mesh=mesh,
        in_specs=(P(AXES, None), P(), P(), P(), P()),
        out_specs=P(AXES, None),
        check_vma=False,
    )
```

time: 258 us -> 152 us (0.59)
  matrix products: 82.4 us -> 16.4 us
  Pallas kernels: 0 us -> 45.1 us
  waiting for transfers between devices: 87.1 us -> 57.1 us
  other arithmetic: 33.2 us -> 7.92 us
  local copies, waits for them, and re-layouts: 27.7 us -> 9.51 us
  starting transfers between devices: 24.6 us -> 15.2 us
    dot_general x25 -> x2, matrix products: 71.6 us -> 9.8 us  [the longest x1 6.23 us: on_device(): jnp.dot(normed, w_qkv[:, HD:], preferred_element_type=jnp.float32)]
    pallas_call x0 -> x3, Pallas kernels: none -> 45.1 us  [the longest x1 19.9 us: call_far(): pl.pallas_call(functools.partial(far_kernel, count // 2), grid=(PAIRS,),...]
    ppermute x6, waiting for transfers between devices: 87.1 us -> 57.1 us  [the longest x4 53.4 us: shifted(): return lax.ppermute(array, AXES, pairs)]
    slice x9 -> x1, local copies, waits for them, and re-layouts: 20.2 us -> 0.01 us  [on_device(): right = shifted(gated[:16], -1)]
    reduce_sum x2 -> x1, other arithmetic: 17.1 us -> 1.84 us  [layer_norm(): average = jnp.mean(values, -1, keepdims=True)]
    reduce_sum x12 -> x0, other arithmetic: 10.2 us -> none  [one_head(): totals = jnp.sum(expo, -1, keepdims=True)]
    ppermute x6, starting transfers between devices: 24.6 us -> 15.2 us  [the longest x4 15.2 us: shifted(): return lax.ppermute(array, AXES, pairs)]
    unnamed x16 -> x22, local copies, waits for them, and re-layouts: 6.07 us -> 9.5 us
  transfers between devices with their start and end apart: 6 -> 6, of which waited for: 4 -> 5; matrix products, arithmetic and copies ran while one was open for 3% -> 2% of each run, Pallas kernels for 0% -> 9%
where the time goes in v1:
time: 152 us; the launch traced here: 151 us
  waiting for transfers between devices  57.1 us (38%)
  Pallas kernels  45.1 us (30%)
  matrix products  16.4 us (11%)
  starting transfers between devices  15.2 us (10%)
  local copies, waits for them, and re-layouts  9.51 us (6%)
  other arithmetic  7.92 us (5%)
    ppermute x4, waiting for transfers between devices, shifted(): return lax.ppermute(array, AXES, pairs)  53.4 us
    pallas_call x1, Pallas kernels, call_far(): pl.pallas_call(functools.partial(far_kernel, count // 2), grid=(PAIRS,),...  19.9 us
    ppermute x4, starting transfers between devices, shifted(): return lax.ppermute(array, AXES, pairs)  15.2 us
    pallas_call x1, Pallas kernels, call_near(): pl.pallas_call(functools.partial(near_kernel, count // 2), grid=(PAIRS,),...  13.8 us
    pallas_call x1, Pallas kernels, call_conv(): pl.pallas_call(functools.partial(conv_kernel_body, rows), grid=(count //...  11.5 us
    unnamed x22, local copies, waits for them, and re-layouts  9.5 us
    dot_general x1, matrix products, on_device(): jnp.dot(normed, w_qkv[:, HD:], preferred_element_type=jnp.float32)  6.23 us
    dot_general x1, matrix products, on_device(): jnp.dot(normed_again, w_point, preferred_element_type=jnp.float32)  5.09 us
  transfers between devices with their start and end apart: 6, of which 5 were waited for; matrix products, arithmetic and copies ran while one was open for 2% of the time, Pallas kernels for 9%

profile of v1, /device:TPU:4, one launch (start us, length us, event | category | flops | bytes accessed | tf_op | source)
XLA Modules:
  0.0 151.4 jit_solution(942178658427086347)
XLA Ops:
  0.0 0.0 copy-start
  0.0 0.0 copy-start.8
  0.0 1.8 %convert_reduce_fusion = f32[512]{0:T(512)S(1)} fusion(bf16[512,1536]{1,0:T(8,128)(2,1)} %param.5), kind=kLoop, calls=%fused_computation.2 | loop fusion | flops 1572352 | bytes 1574912 | tf_op jit(solution)/shard_map/reduce_sum | solution.py:22
  1.9 2.0 %fusion.4 = f32[512]{0:T(512)S(1)} fusion(bf16[512,1536]{1,0:T(8,128)(2,1)} %param.5, f32[512]{0:T(512)S(1)} %broadcast_multiply_fusion.1), kind=kLoop, calls=%fused_computation.7 | loop fusion | flops 3145216 | bytes 1576960 | tf_op jit(solution)/shard_map/reduce_sum | solution.py:24
  3.8 0.0 copy-done.8
  3.8 6.2 %fusion.11.k0_ref.v0_ref = bf16[512,1536]{1,0:T(8,128)(2,1)} fusion(bf16[1536,2304]{1,0:T(8,128)(2,1)} %param.6, bf16[512,1536]{1,0:T(8,128)(2,1)S(1)} %copy-done.8, f32[512]{0:T(512)S(1)} %add_rsqrt_fusion.1, f32[512]{0:T(512)S(1)} %broadcast_multiply_fusion.1), kind=kOutput, calls=%fused_computation.17 | convolution fusion | flops 2419851264 | bytes 7868416 | tf_op jit(solution)/shard_map/dot_general | solution.py:213
  10.1 0.0 collective-permute-start.2
  10.1 6.4 %collective-permute-start.1 = (bf16[512,1536]{1,0:T(8,128)(2,1)}, bf16[512,1536]{1,0:T(8,128)(2,1)}, u32[]{:S(2)}, u32[]{:S(2)}) collective-permute-start(bf16[512,1536]{1,0:T(8,128)(2,1)} %fusion.11.k0_ref.v0_ref), channel_id=1, source_target_pairs={{2,0},{3,1},{4,2},{5,3},{6,4},{7,5},{8,6},{9,7},{10,8},{11,9},{12,... | collective-permute-start | bytes 4718600 | tf_op jit(solution)/shard_map/ppermute | solution.py:206
  16.4 1.9 %collective-permute-start = (bf16[512,1536]{1,0:T(8,128)(2,1)}, bf16[512,1536]{1,0:T(8,128)(2,1)}, u32[]{:S(2)}, u32[]{:S(2)}) collective-permute-start(bf16[512,1536]{1,0:T(8,128)(2,1)} %fusion.11.k0_ref.v0_ref), channel_id=1, source_target_pairs={{0,2},{1,3},{2,4},{3,5},{4,6},{5,7},{6,8},{7,9},{8,10},{9,11},{10,... | collective-permute-start | bytes 4718600 | tf_op jit(solution)/shard_map/ppermute | solution.py:206
  18.4 3.6 %fusion.19.q_ref = bf16[512,768]{1,0:T(8,128)(2,1)S(1)} fusion(bf16[1536,2304]{1,0:T(8,128)(2,1)} %param.6, bf16[512,1536]{1,0:T(8,128)(2,1)} %param.5, f32[512]{0:T(512)S(1)} %add_rsqrt_fusion.1, f32[512]{0:T(512)S(1)} %broadcast_multiply_fusion.1), kind=kOutput, calls=%fused_computation.24 | convolution fusion | flops 1211498496 | bytes 4722688 | tf_op jit(solution)/shard_map/dot_general | solution.py:219
  22.0 0.0 collective-permute-done.2.k1_ref.v1_ref
  22.0 13.8 %near_attention.1 = (f32[512,768]{1,0:T(8,128)S(1)}, f32[512,768]{1,0:T(8,128)S(1)}, f32[512,768]{1,0:T(8,128)S(1)}) custom-call(bf16[512,768]{1,0:T(8,128)(2,1)S(1)} %fusion.19.q_ref, bf16[512,1536]{1,0:T(8,128)(2,1)} %fusion.11.k0_ref.v0_ref, bf16[512,1536]{1,0:T(8,128)(2,1)} %collective-permute-done.2.k1_ref.v1_ref, ...), custom_call_target="tpu_custom_call" | custom-call | flops 6442450944 | bytes 12582912 | tf_op jit(solution)/shard_map/near_attention/pallas_call | solution.py:142
  35.8 0.0 copy-start.2
  35.8 1.2 copy-done.2
  36.9 0.0 copy-start.4
  36.9 1.1 copy-done.4
  38.1 0.0 copy-start.6
  38.1 1.2 copy-done.6
  39.3 12.2 %collective-permute-done.1.kc_ref.vc_ref = bf16[512,1536]{1,0:T(8,128)(2,1)} collective-permute-done((bf16[512,1536]{1,0:T(8,128)(2,1)}, bf16[512,1536]{1,0:T(8,128)(2,1)}, u32[]{:S(2)}, u32[]{:S(2)}) %collective-permute-start.1) | collective-permute-done | bytes 1572896 | tf_op jit(solution)/shard_map/ppermute | solution.py:206
  51.5 34.2 %collective-permute-done.ka_ref.va_ref = bf16[512,1536]{1,0:T(8,128)(2,1)} collective-permute-done((bf16[512,1536]{1,0:T(8,128)(2,1)}, bf16[512,1536]{1,0:T(8,128)(2,1)}, u32[]{:S(2)}, u32[]{:S(2)}) %collective-permute-start) | collective-permute-done | bytes 1572896 | tf_op jit(solution)/shard_map/ppermute | solution.py:206
  85.7 2.7 %broadcast_select_fusion = bf16[512,1536]{1,0:T(8,128)(2,1)} fusion(bf16[512,1536]{1,0:T(8,128)(2,1)} %collective-permute-done.1.kc_ref.vc_ref, bf16[512,1536]{1,0:T(8,128)(2,1)} %collective-permute-done.ka_ref.va_ref, pred[]{:T(512)S(6)} %eq.5), kind=kLoop, calls=%fused_computation.23 | loop fusion | flops 786432 | bytes 4718593 | tf_op jit(solution)/shard_map/jit(_where)/select_n | solution.py:225
  88.4 0.0 collective-permute-start.3
  88.4 0.1 pad_add_fusion.lim_ref
  88.5 3.7 %collective-permute-done.3.kb_ref.vb_ref = bf16[512,1536]{1,0:T(8,128)(2,1)} collective-permute-done((bf16[512,1536]{1,0:T(8,128)(2,1)}, bf16[512,1536]{1,0:T(8,128)(2,1)}, u32[]{:S(2)}, u32[]{:S(2)}) %collective-permute-start.3) | collective-permute-done | bytes 1572896 | tf_op jit(solution)/shard_map/ppermute | solution.py:209
  92.1 0.0 copy-start.3
  92.1 1.4 copy-done.3
  93.6 0.0 copy-start.5
  93.6 1.4 copy-done.5
  95.0 0.0 copy-start.7
  95.0 1.4 copy-done.7
  96.4 0.0 copy-start.9
  96.4 19.9 %far_attention.1 = bf16[512,768]{1,0:T(8,128)(2,1)S(1)} custom-call(s32[3]{0:T(128)S(1)} %pad_add_fusion.lim_ref, bf16[512,768]{1,0:T(8,128)(2,1)S(1)} %fusion.19.q_ref, bf16[512,1536]{1,0:T(8,128)(2,1)} %collective-permute-done.ka_ref.va_ref, bf16[512,1536]{1,0:T(8,128)(2,1)} %collective-permute-done.3.kb_ref.vb_ref, ...), custom_call_target="tpu_custom_call" | custom-call | flops 9663676416 | bytes 12582912 | tf_op jit(solution)/shard_map/far_attention/pallas_call | solution.py:162
  116.2 0.0 copy-done
  116.2 0.0 copy-done.9
  116.3 0.0 copy-start.10
  116.3 1.5 fusion.25
  117.7 0.5 multiply_reduce_fusion
  118.2 1.7 %copy-done.10 = bf16[1536,3072]{1,0:T(8,128)(2,1)S(1)} copy-done((bf16[1536,3072]{1,0:T(8,128)(2,1)S(1)}, bf16[1536,3072]{1,0:T(8,128)(2,1)}, u32[]{:S(2)}) %copy-start.10) | copy-done | bytes 9437208
  119.9 5.1 %fusion.16 = f32[512,3072]{1,0:T(8,128)S(1)} fusion(bf16[1536,3072]{1,0:T(8,128)(2,1)S(1)} %copy-done.10, f32[512,1536]{1,0:T(8,128)S(1)} %get-tuple-element.24.after_ref, f32[512]{0:T(512)S(1)} %add_rsqrt_fusion, f32[512]{0:T(512)S(1)} %broadcast_multiply_fusion), kind=kOutput, calls=%fused_computation.20 | convolution fusion | flops 4834197504 | bytes 18878464 | tf_op jit(solution)/shard_map/dot_general | solution.py:235
  125.0 0.0 copy-start.1
  125.0 0.8 fusion.10.gated_ref
  125.9 5.0 %collective-permute-start.5 = (bf16[16,1536]{1,0:T(8,128)(2,1)S(1)}, bf16[16,1536]{1,0:T(8,128)(2,1)S(1)}, u32[]{:S(2)}, u32[]{:S(2)}) collective-permute-start(bf16[16,1536]{1,0:T(8,128)(2,1)S(1)} %get-tuple-element.21), channel_id=1, source_target_pairs={{1,0},{2,1},{3,2},{4,3},{5,4},{6,5},{7,6},{8,7},{9,8},{10,9},{11,1... | collective-permute-start | bytes 147464 | tf_op jit(solution)/shard_map/ppermute | solution.py:206
  130.9 1.9 %collective-permute-start.4 = (bf16[16,1536]{1,0:T(8,128)(2,1)S(1)}, bf16[16,1536]{1,0:T(8,128)(2,1)S(1)}, u32[]{:S(2)}, u32[]{:S(2)}) collective-permute-start(bf16[16,1536]{1,0:T(8,128)(2,1)S(1)} %get-tuple-element.22), channel_id=1, source_target_pairs={{0,1},{1,2},{2,3},{3,4},{4,5},{5,6},{6,7},{7,8},{8,9},{9,10},{10,1... | collective-permute-start | bytes 147464 | tf_op jit(solution)/shard_map/ppermute | solution.py:206
  132.9 0.2 collective-permute-done.5.right_ref
  133.0 6.9 %collective-permute-done.4.left_ref = bf16[16,1536]{1,0:T(8,128)(2,1)S(1)} collective-permute-done((bf16[16,1536]{1,0:T(8,128)(2,1)S(1)}, bf16[16,1536]{1,0:T(8,128)(2,1)S(1)}, u32[]{:S(2)}, u32[]{:S(2)}) %collective-permute-start.4) | collective-permute-done | bytes 49184 | tf_op jit(solution)/shard_map/ppermute | solution.py:206
  139.9 0.0 copy-done.1
  139.9 11.5 %conv_tail.1 = bf16[512,1536]{1,0:T(8,128)(2,1)} custom-call(bf16[512,1536]{1,0:T(8,128)(2,1)S(1)} %fusion.10.gated_ref, bf16[16,1536]{1,0:T(8,128)(2,1)S(1)} %collective-permute-done.4.left_ref, bf16[16,1536]{1,0:T(8,128)(2,1)S(1)} %collective-permute-done.5.right_ref, f32[512,1536]{1,0:T(8,128)S(1)} %get-tuple-element.24.after_ref, f32[31,1536]{1,0:T(8,128)S(1)} %copy-done.1), custom_call_target="tpu_custom_call" | custom-call | tf_op jit(solution)/shard_map/conv_tail/pallas_call | solution.py:185
  (5 shorter events, 0.0 us)
Async XLA Ops:
  0.0 116.2 %copy-start = (bf16[768,1536]{1,0:T(8,128)(2,1)S(1)}, bf16[768,1536]{1,0:T(8,128)(2,1)}, u32[]{:S(2)}) copy-start(bf16[768,1536]{1,0:T(8,128)(2,1)} %param.7) | copy-start | bytes 7077892
  0.0 3.8 %copy-start.8 = (bf16[512,1536]{1,0:T(8,128)(2,1)S(1)}, bf16[512,1536]{1,0:T(8,128)(2,1)}, u32[]{:S(2)}) copy-start(bf16[512,1536]{1,0:T(8,128)(2,1)} %param.5) | copy-start | bytes 4718596
  10.1 11.9 %collective-permute-start.2 = (bf16[512,1536]{1,0:T(8,128)(2,1)}, bf16[512,1536]{1,0:T(8,128)(2,1)}, u32[]{:S(2)}, u32[]{:S(2)}) collective-permute-start(bf16[512,1536]{1,0:T(8,128)(2,1)} %fusion.11.k0_ref.v0_ref), channel_id=1, source_target_pairs={{0,1},{1,0},{2,3},{3,2},{4,5},{5,4},{6,7},{7,6},{8,9},{9,8},{10,11... | collective-permute-start | bytes 4718600 | tf_op jit(solution)/shard_map/ppermute | solution.py:209
  10.1 41.4 %collective-permute-start.1 = (bf16[512,1536]{1,0:T(8,128)(2,1)}, bf16[512,1536]{1,0:T(8,128)(2,1)}, u32[]{:S(2)}, u32[]{:S(2)}) collective-permute-start(bf16[512,1536]{1,0:T(8,128)(2,1)} %fusion.11.k0_ref.v0_ref), channel_id=1, source_target_pairs={{2,0},{3,1},{4,2},{5,3},{6,4},{7,5},{8,6},{9,7},{10,8},{11,9},{12,... | collective-permute-start | bytes 4718600 | tf_op jit(solution)/shard_map/ppermute | solution.py:206
  16.4 69.2 %collective-permute-start = (bf16[512,1536]{1,0:T(8,128)(2,1)}, bf16[512,1536]{1,0:T(8,128)(2,1)}, u32[]{:S(2)}, u32[]{:S(2)}) collective-permute-start(bf16[512,1536]{1,0:T(8,128)(2,1)} %fusion.11.k0_ref.v0_ref), channel_id=1, source_target_pairs={{0,2},{1,3},{2,4},{3,5},{4,6},{5,7},{6,8},{7,9},{8,10},{9,11},{10,... | collective-permute-start | bytes 4718600 | tf_op jit(solution)/shard_map/ppermute | solution.py:206
  35.8 1.2 copy-start.2
  36.9 1.1 copy-start.4
  38.1 1.2 copy-start.6
  88.4 3.8 %collective-permute-start.3 = (bf16[512,1536]{1,0:T(8,128)(2,1)}, bf16[512,1536]{1,0:T(8,128)(2,1)}, u32[]{:S(2)}, u32[]{:S(2)}) collective-permute-start(bf16[512,1536]{1,0:T(8,128)(2,1)} %broadcast_select_fusion), channel_id=1, source_target_pairs={{0,1},{1,0},{2,3},{3,2},{4,5},{5,4},{6,7},{7,6},{8,9},{9,8},{10,11... | collective-permute-start | bytes 4718600 | tf_op jit(solution)/shard_map/ppermute | solution.py:209
  92.1 1.4 copy-start.3
  93.6 1.4 copy-start.5
  95.0 1.4 copy-start.7
  96.4 19.9 %copy-start.9 = (bf16[512,1536]{1,0:T(8,128)(2,1)S(1)}, bf16[512,1536]{1,0:T(8,128)(2,1)}, u32[]{:S(2)}) copy-start(bf16[512,1536]{1,0:T(8,128)(2,1)} %param.5) | copy-start | bytes 4718596
  116.3 3.7 %copy-start.10 = (bf16[1536,3072]{1,0:T(8,128)(2,1)S(1)}, bf16[1536,3072]{1,0:T(8,128)(2,1)}, u32[]{:S(2)}) copy-start(bf16[1536,3072]{1,0:T(8,128)(2,1)} %param.8) | copy-start | bytes 28311556
  125.0 14.9 %copy-start.1 = (f32[31,1536]{1,0:T(8,128)S(1)}, f32[31,1536]{1,0:T(8,128)}, u32[]{:S(2)}) copy-start(f32[31,1536]{1,0:T(8,128)} %taps_ref.1) | copy-start | bytes 571396
  125.9 7.1 %collective-permute-start.5 = (bf16[16,1536]{1,0:T(8,128)(2,1)S(1)}, bf16[16,1536]{1,0:T(8,128)(2,1)S(1)}, u32[]{:S(2)}, u32[]{:S(2)}) collective-permute-start(bf16[16,1536]{1,0:T(8,128)(2,1)S(1)} %get-tuple-element.21), channel_id=1, source_target_pairs={{1,0},{2,1},{3,2},{4,3},{5,4},{6,5},{7,6},{8,7},{9,8},{10,9},{11,1... | collective-permute-start | bytes 147464 | tf_op jit(solution)/shard_map/ppermute | solution.py:206
  130.9 9.0 %collective-permute-start.4 = (bf16[16,1536]{1,0:T(8,128)(2,1)S(1)}, bf16[16,1536]{1,0:T(8,128)(2,1)S(1)}, u32[]{:S(2)}, u32[]{:S(2)}) collective-permute-start(bf16[16,1536]{1,0:T(8,128)(2,1)S(1)} %get-tuple-element.22), channel_id=1, source_target_pairs={{0,1},{1,2},{2,3},{3,4},{4,5},{5,6},{6,7},{7,8},{8,9},{9,10},{10,1... | collective-permute-start | bytes 147464 | tf_op jit(solution)/shard_map/ppermute | solution.py:206

commit v2 on v1

--- a/solution.py
+++ b/solution.py
@@ -14,7 +14,7 @@
 HD = 768
 AXES = ("outer", "inner")
 LANES = 128
-PAIRS = HD // LANES
+SPLIT = 512
 NEG = -1e30
 
 
@@ -135,42 +135,44 @@
 
 
 def call_near(queries, own, other):
-    count = queries.shape[0]
+    count, width = queries.shape
+    pairs = width // LANES
     key = pl.BlockSpec((count, LANES), lambda i: (0, i))
-    value = pl.BlockSpec((count, LANES), lambda i: (0, i + PAIRS))
-    state = jax.ShapeDtypeStruct((count, HD), jnp.float32)
+    value = pl.BlockSpec((count, LANES), lambda i: (0, i + pairs))
+    state = jax.ShapeDtypeStruct((count, width), jnp.float32)
     return pl.pallas_call(
         functools.partial(near_kernel, count // 2),
-        grid=(PAIRS,),
+        grid=(pairs,),
         in_specs=[key, key, key, value, value],
         out_specs=[key] * 3,
         out_shape=[state] * 3,
         compiler_params=pltpu.CompilerParams(vmem_limit_bytes=40 << 20),
         cost_estimate=pl.CostEstimate(
-            flops=HEADS * 2 * 2 * count * 2 * count * 256,
+            flops=2 * pairs * 2 * 2 * count * 2 * count * 256,
             bytes_accessed=12 << 20,
-            transcendentals=HEADS * count * 2 * count,
+            transcendentals=2 * pairs * count * 2 * count,
         ),
         name="near_attention",
     )(queries, own, other, own, other)
 
 
 def call_far(limits, queries, a, b, c, state):
-    count = queries.shape[0]
+    count, width = queries.shape
+    pairs = width // LANES
     key = pl.BlockSpec((count, LANES), lambda i: (0, i))
-    value = pl.BlockSpec((count, LANES), lambda i: (0, i + PAIRS))
+    value = pl.BlockSpec((count, LANES), lambda i: (0, i + pairs))
     return pl.pallas_call(
         functools.partial(far_kernel, count // 2),
-        grid=(PAIRS,),
+        grid=(pairs,),
         in_specs=[pl.BlockSpec(memory_space=pltpu.SMEM)]
         + [key] * 4 + [value] * 3 + [key] * 3,
         out_specs=key,
-        out_shape=jax.ShapeDtypeStruct((count, HD), jnp.bfloat16),
+        out_shape=jax.ShapeDtypeStruct((count, width), jnp.bfloat16),
         compiler_params=pltpu.CompilerParams(vmem_limit_bytes=40 << 20),
         cost_estimate=pl.CostEstimate(
-            flops=HEADS * 2 * 2 * count * 3 * count * 256,
+            flops=2 * pairs * 2 * 2 * count * 3 * count * 256,
             bytes_accessed=12 << 20,
-            transcendentals=HEADS * count * 3 * count,
+            transcendentals=2 * pairs * count * 3 * count,
         ),
         name="far_attention",
     )(limits, queries, a, b, c, a, b, c, *state)
@@ -210,26 +212,49 @@
 
     inputs = frames.astype(jnp.float32)
     normed = layer_norm(inputs).astype(jnp.bfloat16)
-    keyvals = jnp.dot(normed, w_qkv[:, HD:], preferred_element_type=jnp.float32).astype(
-        jnp.bfloat16
-    )
-    from_before = shifted(keyvals, 2)
-    from_after = shifted(keyvals, -2)
-    other = swapped(keyvals)
-    queries = jnp.dot(normed, w_qkv[:, :HD], preferred_element_type=jnp.float32).astype(
-        jnp.bfloat16
-    )
+    def project(start, stop):
+        return jnp.dot(
+            normed, w_qkv[:, start:stop], preferred_element_type=jnp.float32
+        ).astype(jnp.bfloat16)
+
+    def keyvals_of(start, stop):
+        return jnp.concatenate(
+            [project(HD + start, HD + stop), project(2 * HD + start, 2 * HD + stop)], 1
+        )
+
+    big = 1 << 20
     even = index % 2 == 0
-    state = call_near(queries, keyvals, other)
-    from_before, from_after, state = lax.optimization_barrier((from_before, from_after, state))
-    bridge = swapped(jnp.where(even, from_after, from_before))
-    big = 1 << 20
     limits = jnp.stack([
         jnp.where(index >= 2, 0, big),
         jnp.where(jnp.where(even, index >= 1, index + 1 < total), 1, 0),
         jnp.where(index + 2 < total, 0, -big),
     ]).astype(jnp.int32)
-    attended = call_far(limits, queries, from_before, bridge, from_after, state)
+
+    wait = lax.optimization_barrier
+    kv_1 = keyvals_of(0, SPLIT)
+    before_1, after_1 = shifted(kv_1, 2), shifted(kv_1, -2)
+    other_1 = swapped(kv_1)
+    kv_2 = keyvals_of(SPLIT, HD)
+    other_2 = swapped(kv_2)
+    queries = project(0, HD)
+    queries_1, queries_2 = queries[:, :SPLIT], queries[:, SPLIT:]
+    acc_1, high_1, sum_1 = call_near(queries_1, kv_1, other_1)
+    acc_2, high_2, sum_2 = call_near(queries_2, kv_2, other_2)
+    kv_up, kv_down = kv_2, kv_2
+    kv_down, after_1, sum_1, sum_2 = wait((kv_down, after_1, sum_1, sum_2))
+    after_2 = shifted(kv_down, -2)
+    kv_up, before_1, sum_1 = wait((kv_up, before_1, sum_1))
+    before_2 = shifted(kv_up, 2)
+    bridge_1 = swapped(jnp.where(even, after_1, before_1))
+    attended_1 = call_far(
+        limits, queries_1, before_1, bridge_1, after_1, (acc_1, high_1, sum_1)
+    )
+    before_2, after_2, attended_1 = wait((before_2, after_2, attended_1))
+    bridge_2 = swapped(jnp.where(even, after_2, before_2))
+    attended_2 = call_far(
+        limits, queries_2, before_2, bridge_2, after_2, (acc_2, high_2, sum_2)
+    )
+    attended = jnp.concatenate([attended_1, attended_2], 1)
     after_attention = inputs + jnp.dot(attended, w_out, preferred_element_type=jnp.float32)
     normed_again = layer_norm(after_attention).astype(jnp.bfloat16)
     projected = jnp.dot(normed_again, w_point, preferred_element_type=jnp.float32)

time: 152 us -> 142 us (0.934)
  waiting for transfers between devices: 57.1 us -> 27.8 us
  starting transfers between devices: 15.2 us -> 25.8 us
  local copies, waits for them, and re-layouts: 9.51 us -> 12.7 us
  matrix products: 16.4 us -> 18.8 us
  Pallas kernels: 45.1 us -> 47 us
    ppermute x4 -> x6, waiting for transfers between devices: 53.4 us -> 25.9 us  [shifted(): return lax.ppermute(array, AXES, pairs)]
    ppermute x4 -> x6, starting transfers between devices: 15.2 us -> 24.8 us  [shifted(): return lax.ppermute(array, AXES, pairs)]
    dot_general x2 -> x5, matrix products: 9.8 us -> 12.3 us  [project(): jnp.dot(normed, w_qkv[:, start:stop], preferred_element_type=jnp.float32)]
    concatenate x0 -> x2, other arithmetic: none -> 1.95 us  [keyvals_of(): jnp.concatenate([project(HD + start, HD + stop), project(2 * HD + start,...]
    pallas_call x2 -> x4, Pallas kernels: 33.6 us -> 35.6 us  [the longest x2 20.6 us: call_far(): pl.pallas_call(functools.partial(far_kernel, count // 2), grid=(pairs,),...]
    ppermute x2 -> x4, waiting for transfers between devices: 3.68 us -> 1.9 us  [swapped(): return lax.ppermute(array, AXES, [(i, i ^ 1) for i in range(total)])]
    unnamed x22 -> x48, local copies, waits for them, and re-layouts: 9.5 us -> 11.1 us
    select_n x1 -> x2, other arithmetic: 2.72 us -> 1.14 us  [the longest x1 1.08 us: on_device(): bridge_1 = swapped(jnp.where(even, after_1, before_1))]
  transfers between devices with their start and end apart: 6 -> 10, of which waited for: 5 -> 5; matrix products, arithmetic and copies ran while one was open for 2% -> 7% of each run, Pallas kernels for 9% -> 20%
where the time goes in v2:
time: 142 us; the launch traced here: 141 us
  Pallas kernels  47 us (33%)
  waiting for transfers between devices  27.8 us (20%)
  starting transfers between devices  25.8 us (18%)
  matrix products  18.8 us (13%)
  local copies, waits for them, and re-layouts  12.7 us (9%)
  other arithmetic  8.73 us (6%)
    ppermute x6, waiting for transfers between devices, shifted(): return lax.ppermute(array, AXES, pairs)  25.9 us
    ppermute x6, starting transfers between devices, shifted(): return lax.ppermute(array, AXES, pairs)  24.8 us
    pallas_call x2, Pallas kernels, call_far(): pl.pallas_call(functools.partial(far_kernel, count // 2), grid=(pairs,),...  20.6 us
    pallas_call x2, Pallas kernels, call_near(): pl.pallas_call(functools.partial(near_kernel, count // 2), grid=(pairs,),...  14.9 us
    dot_general x5, matrix products, project(): jnp.dot(normed, w_qkv[:, start:stop], preferred_element_type=jnp.float32)  12.3 us
    pallas_call x1, Pallas kernels, call_conv(): pl.pallas_call(functools.partial(conv_kernel_body, rows), grid=(count //...  11.5 us
    unnamed x48, local copies, waits for them, and re-layouts  11.1 us
    dot_general x1, matrix products, on_device(): jnp.dot(normed_again, w_point, preferred_element_type=jnp.float32)  5.1 us
  transfers between devices with their start and end apart: 10, of which 5 were waited for; matrix products, arithmetic and copies ran while one was open for 7% of the time, Pallas kernels for 20%

profile of v2, /device:TPU:4, one launch (start us, length us, event | category | flops | bytes accessed | tf_op | source)
XLA Modules:
  0.0 141.2 jit_solution(17638228414155147551)
XLA Ops:
  0.0 1.8 %convert_reduce_fusion = f32[512]{0:T(512)S(1)} fusion(bf16[512,1536]{1,0:T(8,128)(2,1)} %param.5), kind=kLoop, calls=%fused_computation.2 | loop fusion | flops 1572352 | bytes 1574912 | tf_op jit(solution)/shard_map/reduce_sum | solution.py:22
  1.9 2.0 %fusion.2 = f32[512]{0:T(512)S(1)} fusion(bf16[512,1536]{1,0:T(8,128)(2,1)} %param.5, f32[512]{0:T(512)S(1)} %broadcast_multiply_fusion.1), kind=kLoop, calls=%fused_computation.5 | loop fusion | flops 3145216 | bytes 1576960 | tf_op jit(solution)/shard_map/reduce_sum | solution.py:24
  3.8 0.4 fusion.3
  4.3 3.0 %fusion.24 = bf16[512,512]{1,0:T(8,128)(2,1)S(1)} fusion(bf16[512,1536]{1,0:T(8,128)(2,1)S(1)} %fusion.3, bf16[1536,2304]{1,0:T(8,128)(2,1)} %param.6), kind=kOutput, calls=%fused_computation.26 | convolution fusion | flops 805568512 | bytes 3670016 | tf_op jit(solution)/shard_map/dot_general | solution.py:216
  7.2 2.4 %fusion.21 = bf16[512,512]{1,0:T(8,128)(2,1)S(1)} fusion(bf16[512,1536]{1,0:T(8,128)(2,1)S(1)} %fusion.3, bf16[1536,2304]{1,0:T(8,128)(2,1)} %param.6), kind=kOutput, calls=%fused_computation.25 | convolution fusion | flops 805568512 | bytes 3670016 | tf_op jit(solution)/shard_map/dot_general | solution.py:216
  9.6 1.1 pad_maximum_fusion.k0_ref.v0_ref
  10.7 1.7 %convolution_convert_fusion = bf16[512,256]{1,0:T(8,128)(2,1)S(1)} fusion(bf16[512,1536]{1,0:T(8,128)(2,1)S(1)} %fusion.3, bf16[1536,2304]{1,0:T(8,128)(2,1)} %param.6), kind=kOutput, calls=%fused_computation.27 | convolution fusion | flops 402784256 | bytes 2621440 | tf_op jit(solution)/shard_map/dot_general | solution.py:216
  12.5 1.7 %convolution_convert_fusion.1 = bf16[512,256]{1,0:T(8,128)(2,1)S(1)} fusion(bf16[512,1536]{1,0:T(8,128)(2,1)S(1)} %fusion.3, bf16[1536,2304]{1,0:T(8,128)(2,1)} %param.6), kind=kOutput, calls=%fused_computation.28 | convolution fusion | flops 402784256 | bytes 2621440 | tf_op jit(solution)/shard_map/dot_general | solution.py:216
  14.2 0.8 pad_maximum_fusion.1.k0_ref.v0_ref
  15.0 0.5 collective-permute-start.3
  15.5 6.4 %collective-permute-start.1 = (bf16[512,1024]{1,0:T(8,128)(2,1)}, bf16[512,1024]{1,0:T(8,128)(2,1)S(1)}, u32[]{:S(2)}, u32[]{:S(2)}) collective-permute-start(bf16[512,1024]{1,0:T(8,128)(2,1)} %pad_maximum_fusion.k0_ref.v0_ref), channel_id=1, source_target_pairs={{2,0},{3,1},{4,2},{5,3},{6,4},{7,5},{8,6},{9,7},{10,8},{11,9},{12,... | collective-permute-start | bytes 3145736 | tf_op jit(solution)/shard_map/ppermute | solution.py:208
  21.9 1.9 %collective-permute-start = (bf16[512,1024]{1,0:T(8,128)(2,1)}, bf16[512,1024]{1,0:T(8,128)(2,1)}, u32[]{:S(2)}, u32[]{:S(2)}) collective-permute-start(bf16[512,1024]{1,0:T(8,128)(2,1)} %pad_maximum_fusion.k0_ref.v0_ref), channel_id=1, source_target_pairs={{0,2},{1,3},{2,4},{3,5},{4,6},{5,7},{6,8},{7,9},{8,10},{9,11},{10,... | collective-permute-start | bytes 3145736 | tf_op jit(solution)/shard_map/ppermute | solution.py:208
  23.8 3.5 %fusion.18 = bf16[512,768]{1,0:T(8,128)(2,1)S(1)} fusion(bf16[512,1536]{1,0:T(8,128)(2,1)} %copy-done.20, bf16[1536,2304]{1,0:T(8,128)(2,1)} %param.6), kind=kOutput, calls=%fused_computation.24 | convolution fusion | flops 1208352768 | bytes 4718592 | tf_op jit(solution)/shard_map/dot_general | solution.py:216
  27.4 0.7 slice.45.q_ref
  28.1 0.8 slice.44.q_ref
  29.0 1.0 copy-done.3
  30.0 5.3 %near_attention.3 = (f32[512,256]{1,0:T(8,128)S(1)}, f32[512,256]{1,0:T(8,128)S(1)}, f32[512,256]{1,0:T(8,128)S(1)}) custom-call(bf16[512,256]{1,0:T(8,128)(2,1)S(1)} %copy-done.3, bf16[512,512]{1,0:T(8,128)(2,1)} %pad_maximum_fusion.1.k0_ref.v0_ref, bf16[512,512]{1,0:T(8,128)(2,1)} %collective-permute-done.3.k1_ref.v1_ref, ...), custom_call_target="tpu_custom_call" | custom-call | flops 2147483648 | bytes 12582912 | tf_op jit(solution)/shard_map/near_attention/pallas_call | solution.py:143
  35.3 0.8 copy-done.6
  36.1 0.8 copy-done.8
  36.9 0.8 copy-done.10
  37.7 9.7 %near_attention.2 = (f32[512,512]{1,0:T(8,128)S(1)}, f32[512,512]{1,0:T(8,128)S(1)}, f32[512,512]{1,0:T(8,128)S(1)}) custom-call(bf16[512,512]{1,0:T(8,128)(2,1)S(1)} %copy-done.1, bf16[512,1024]{1,0:T(8,128)(2,1)} %pad_maximum_fusion.k0_ref.v0_ref, bf16[512,1024]{1,0:T(8,128)(2,1)} %collective-permute-done.2.k1_ref.v1_ref, ...), custom_call_target="tpu_custom_call" | custom-call | flops 4294967296 | bytes 12582912 | tf_op jit(solution)/shard_map/near_attention/pallas_call | solution.py:143
  47.4 1.0 copy-done.12
  48.3 1.0 copy-done.14
  49.3 1.0 copy-done.16
  50.3 17.9 %collective-permute-done.ka_ref.va_ref = bf16[512,1024]{1,0:T(8,128)(2,1)} collective-permute-done((bf16[512,1024]{1,0:T(8,128)(2,1)}, bf16[512,1024]{1,0:T(8,128)(2,1)}, u32[]{:S(2)}, u32[]{:S(2)}) %collective-permute-start) | collective-permute-done | bytes 1048608 | tf_op jit(solution)/shard_map/ppermute | solution.py:208
  68.2 1.1 broadcast_select_fusion
  69.2 0.4 collective-permute-start.6
  69.6 0.1 pad_add_fusion.lim_ref
  69.7 3.5 %collective-permute-start.4 = (bf16[512,512]{1,0:T(8,128)(2,1)}, bf16[512,512]{1,0:T(8,128)(2,1)S(1)}, u32[]{:S(2)}, u32[]{:S(2)}) collective-permute-start(bf16[512,512]{1,0:T(8,128)(2,1)} %pad_maximum_fusion.1.k0_ref.v0_ref), channel_id=1, source_target_pairs={{0,2},{1,3},{2,4},{3,5},{4,6},{5,7},{6,8},{7,9},{8,10},{9,11},{10,... | collective-permute-start | bytes 1572872 | tf_op jit(solution)/shard_map/ppermute | solution.py:208
  73.2 6.1 %collective-permute-start.5 = (bf16[512,512]{1,0:T(8,128)(2,1)}, bf16[512,512]{1,0:T(8,128)(2,1)S(1)}, u32[]{:S(2)}, u32[]{:S(2)}) collective-permute-start(bf16[512,512]{1,0:T(8,128)(2,1)} %pad_maximum_fusion.1.k0_ref.v0_ref), channel_id=1, source_target_pairs={{2,0},{3,1},{4,2},{5,3},{6,4},{7,5},{8,6},{9,7},{10,8},{11,9},{12,... | collective-permute-start | bytes 1572872 | tf_op jit(solution)/shard_map/ppermute | solution.py:208
  79.3 1.0 copy-done.2
  80.4 1.2 copy-done.13
  81.6 1.2 copy-done.15
  82.8 1.2 copy-done.17
  84.1 13.8 %far_attention.2 = bf16[512,512]{1,0:T(8,128)(2,1)S(1)} custom-call(s32[3]{0:T(128)S(1)} %pad_add_fusion.lim_ref, bf16[512,512]{1,0:T(8,128)(2,1)S(1)} %copy-done.2, bf16[512,1024]{1,0:T(8,128)(2,1)} %collective-permute-done.ka_ref.va_ref, bf16[512,1024]{1,0:T(8,128)(2,1)} %collective-permute-done.6.kb_ref.vb_ref, ...), custom_call_target="tpu_custom_call" | custom-call | flops 6442450944 | bytes 12582912 | tf_op jit(solution)/shard_map/far_attention/pallas_call | solution.py:164
  97.9 0.9 collective-permute-done.5.kc_ref.vc_ref
  98.9 0.1 collective-permute-start.7
  99.0 1.9 %collective-permute-done.7.kb_ref.vb_ref = bf16[512,512]{1,0:T(8,128)(2,1)S(1)} collective-permute-done((bf16[512,512]{1,0:T(8,128)(2,1)S(1)}, bf16[512,512]{1,0:T(8,128)(2,1)S(1)}, u32[]{:S(2)}, u32[]{:S(2)}) %collective-permute-start.7) | collective-permute-done | bytes 524320 | tf_op jit(solution)/shard_map/ppermute | solution.py:211
  100.9 6.8 %far_attention.3 = bf16[512,256]{1,0:T(8,128)(2,1)S(1)} custom-call(s32[3]{0:T(128)S(1)} %pad_add_fusion.lim_ref, bf16[512,256]{1,0:T(8,128)(2,1)S(1)} %copy-done.4, bf16[512,512]{1,0:T(8,128)(2,1)S(1)} %collective-permute-done.4.ka_ref.va_ref, bf16[512,512]{1,0:T(8,128)(2,1)S(1)} %collective-permute-done.7.kb_ref.vb_ref, ...), custom_call_target="tpu_custom_call" | custom-call | flops 3221225472 | bytes 12582912 | tf_op jit(solution)/shard_map/far_attention/pallas_call | solution.py:164
  107.8 1.5 %fusion.34 = (f32[512]{0:T(512)S(1)}, f32[512,1536]{1,0:T(8,128)S(1)}) fusion(bf16[768,1536]{1,0:T(8,128)(2,1)S(1)} %copy-done, bf16[512,256]{1,0:T(8,128)(2,1)S(1)} %far_attention.3, bf16[512,512]{1,0:T(8,128)(2,1)S(1)} %far_attention.2, bf16[512,1536]{1,0:T(8,128)(2,1)S(1)} %copy-done.19), kind=kOutput, calls=%fused_computation.45 | convolution fusion | flops 1211891200 | bytes 7866368 | tf_op jit(solution)/shard_map/dot_general | solution.py:258
  109.2 0.5 multiply_reduce_fusion
  109.7 5.1 %fusion.11 = f32[512,3072]{1,0:T(8,128)S(1)} fusion(bf16[1536,3072]{1,0:T(8,128)(2,1)S(1)} %bitcast.11, f32[512,1536]{1,0:T(8,128)S(1)} %get-tuple-element.40.after_ref, f32[512]{0:T(512)S(1)} %add_rsqrt_fusion, f32[512]{0:T(512)S(1)} %broadcast_multiply_fusion), kind=kOutput, calls=%fused_computation.17 | convolution fusion | flops 4834197504 | bytes 18878464 | tf_op jit(solution)/shard_map/dot_general | solution.py:260
  114.9 0.8 fusion.8.gated_ref
  115.7 5.0 %collective-permute-start.9 = (bf16[16,1536]{1,0:T(8,128)(2,1)S(1)}, bf16[16,1536]{1,0:T(8,128)(2,1)S(1)}, u32[]{:S(2)}, u32[]{:S(2)}) collective-permute-start(bf16[16,1536]{1,0:T(8,128)(2,1)S(1)} %get-tuple-element.37), channel_id=1, source_target_pairs={{1,0},{2,1},{3,2},{4,3},{5,4},{6,5},{7,6},{8,7},{9,8},{10,9},{11,1... | collective-permute-start | bytes 147464 | tf_op jit(solution)/shard_map/ppermute | solution.py:208
  120.8 1.9 %collective-permute-start.8 = (bf16[16,1536]{1,0:T(8,128)(2,1)S(1)}, bf16[16,1536]{1,0:T(8,128)(2,1)S(1)}, u32[]{:S(2)}, u32[]{:S(2)}) collective-permute-start(bf16[16,1536]{1,0:T(8,128)(2,1)S(1)} %get-tuple-element.38), channel_id=1, source_target_pairs={{0,1},{1,2},{2,3},{3,4},{4,5},{5,6},{6,7},{7,8},{8,9},{9,10},{10,1... | collective-permute-start | bytes 147464 | tf_op jit(solution)/shard_map/ppermute | solution.py:208
  122.7 0.2 collective-permute-done.9.right_ref
  122.9 6.9 %collective-permute-done.8.left_ref = bf16[16,1536]{1,0:T(8,128)(2,1)S(1)} collective-permute-done((bf16[16,1536]{1,0:T(8,128)(2,1)S(1)}, bf16[16,1536]{1,0:T(8,128)(2,1)S(1)}, u32[]{:S(2)}, u32[]{:S(2)}) %collective-permute-start.8) | collective-permute-done | bytes 49184 | tf_op jit(solution)/shard_map/ppermute | solution.py:208
  129.8 11.5 %conv_tail.1 = bf16[512,1536]{1,0:T(8,128)(2,1)} custom-call(bf16[512,1536]{1,0:T(8,128)(2,1)S(1)} %fusion.8.gated_ref, bf16[16,1536]{1,0:T(8,128)(2,1)S(1)} %collective-permute-done.8.left_ref, bf16[16,1536]{1,0:T(8,128)(2,1)S(1)} %collective-permute-done.9.right_ref, f32[512,1536]{1,0:T(8,128)S(1)} %get-tuple-element.40.after_ref, f32[31,1536]{1,0:T(8,128)S(1)} %copy-done.5), custom_call_target="tpu_custom_call" | custom-call | tf_op jit(solution)/shard_map/conv_tail/pallas_call | solution.py:187
  (50 shorter events, 0.2 us)
Async XLA Ops:
  0.0 107.7 %copy-start = (bf16[768,1536]{1,0:T(8,128)(2,1)S(1)}, bf16[768,1536]{1,0:T(8,128)(2,1)}, u32[]{:S(2)}) copy-start(bf16[768,1536]{1,0:T(8,128)(2,1)} %param.7) | copy-start | bytes 7077892
  0.0 3.8 %copy-start.18 = (bf16[512,1536]{1,0:T(8,128)(2,1)S(1)}, bf16[512,1536]{1,0:T(8,128)(2,1)}, u32[]{:S(2)}) copy-start(bf16[512,1536]{1,0:T(8,128)(2,1)} %param.5) | copy-start | bytes 4718596
  4.3 8.2 %copy-start.20 = (bf16[512,1536]{1,0:T(8,128)(2,1)}, bf16[512,1536]{1,0:T(8,128)(2,1)S(1)}, u32[]{:S(2)}) copy-start(bf16[512,1536]{1,0:T(8,128)(2,1)S(1)} %fusion.3) | copy-start | bytes 4718596
  10.7 26.9 %collective-permute-start.2 = (bf16[512,1024]{1,0:T(8,128)(2,1)}, bf16[512,1024]{1,0:T(8,128)(2,1)}, u32[]{:S(2)}, u32[]{:S(2)}) collective-permute-start(bf16[512,1024]{1,0:T(8,128)(2,1)} %pad_maximum_fusion.k0_ref.v0_ref), channel_id=1, source_target_pairs={{0,1},{1,0},{2,3},{3,2},{4,5},{5,4},{6,7},{7,6},{8,9},{9,8},{10,11... | collective-permute-start | bytes 3145736 | tf_op jit(solution)/shard_map/ppermute | solution.py:211
  15.0 13.9 %collective-permute-start.3 = (bf16[512,512]{1,0:T(8,128)(2,1)}, bf16[512,512]{1,0:T(8,128)(2,1)}, u32[]{:S(2)}, u32[]{:S(2)}) collective-permute-start(bf16[512,512]{1,0:T(8,128)(2,1)} %pad_maximum_fusion.1.k0_ref.v0_ref), channel_id=1, source_target_pairs={{0,1},{1,0},{2,3},{3,2},{4,5},{5,4},{6,7},{7,6},{8,9},{9,8},{10,11... | collective-permute-start | bytes 1572872 | tf_op jit(solution)/shard_map/ppermute | solution.py:211
  15.5 34.8 %collective-permute-start.1 = (bf16[512,1024]{1,0:T(8,128)(2,1)}, bf16[512,1024]{1,0:T(8,128)(2,1)S(1)}, u32[]{:S(2)}, u32[]{:S(2)}) collective-permute-start(bf16[512,1024]{1,0:T(8,128)(2,1)} %pad_maximum_fusion.k0_ref.v0_ref), channel_id=1, source_target_pairs={{2,0},{3,1},{4,2},{5,3},{6,4},{7,5},{8,6},{9,7},{10,8},{11,9},{12,... | collective-permute-start | bytes 3145736 | tf_op jit(solution)/shard_map/ppermute | solution.py:208
  21.9 46.3 %collective-permute-start = (bf16[512,1024]{1,0:T(8,128)(2,1)}, bf16[512,1024]{1,0:T(8,128)(2,1)}, u32[]{:S(2)}, u32[]{:S(2)}) collective-permute-start(bf16[512,1024]{1,0:T(8,128)(2,1)} %pad_maximum_fusion.k0_ref.v0_ref), channel_id=1, source_target_pairs={{0,2},{1,3},{2,4},{3,5},{4,6},{5,7},{6,8},{7,9},{8,10},{9,11},{10,... | collective-permute-start | bytes 3145736 | tf_op jit(solution)/shard_map/ppermute | solution.py:208
  28.9 8.7 %copy-start.1 = (bf16[512,512]{1,0:T(8,128)(2,1)S(1)}, bf16[512,512]{1,0:T(8,128)(2,1)}, u32[]{:S(2)}) copy-start(bf16[512,512]{1,0:T(8,128)(2,1)} %slice.44.q_ref) | copy-start | bytes 1572868
  29.0 1.0 copy-start.3
  35.3 0.8 copy-start.6
  36.1 0.8 copy-start.8
  36.9 0.8 copy-start.10
  47.3 1.0 copy-start.12
  48.3 1.0 copy-start.14
  49.3 1.0 copy-start.16
  69.2 10.1 %collective-permute-start.6 = (bf16[512,1024]{1,0:T(8,128)(2,1)}, bf16[512,1024]{1,0:T(8,128)(2,1)}, u32[]{:S(2)}, u32[]{:S(2)}) collective-permute-start(bf16[512,1024]{1,0:T(8,128)(2,1)} %broadcast_select_fusion), channel_id=1, source_target_pairs={{0,1},{1,0},{2,3},{3,2},{4,5},{5,4},{6,7},{7,6},{8,9},{9,8},{10,11... | collective-permute-start | bytes 3145736 | tf_op jit(solution)/shard_map/ppermute | solution.py:211
  69.7 28.2 %collective-permute-start.4 = (bf16[512,512]{1,0:T(8,128)(2,1)}, bf16[512,512]{1,0:T(8,128)(2,1)S(1)}, u32[]{:S(2)}, u32[]{:S(2)}) collective-permute-start(bf16[512,512]{1,0:T(8,128)(2,1)} %pad_maximum_fusion.1.k0_ref.v0_ref), channel_id=1, source_target_pairs={{0,2},{1,3},{2,4},{3,5},{4,6},{5,7},{6,8},{7,9},{8,10},{9,11},{10,... | collective-permute-start | bytes 1572872 | tf_op jit(solution)/shard_map/ppermute | solution.py:208
  73.2 25.6 %collective-permute-start.5 = (bf16[512,512]{1,0:T(8,128)(2,1)}, bf16[512,512]{1,0:T(8,128)(2,1)S(1)}, u32[]{:S(2)}, u32[]{:S(2)}) collective-permute-start(bf16[512,512]{1,0:T(8,128)(2,1)} %pad_maximum_fusion.1.k0_ref.v0_ref), channel_id=1, source_target_pairs={{2,0},{3,1},{4,2},{5,3},{6,4},{7,5},{8,6},{9,7},{10,8},{11,9},{12,... | collective-permute-start | bytes 1572872 | tf_op jit(solution)/shard_map/ppermute | solution.py:208
  79.3 1.0 copy-start.2
  80.4 1.2 copy-start.13
  81.6 1.2 copy-start.15
  82.8 1.2 copy-start.17
  84.0 16.8 %copy-start.4 = (bf16[512,256]{1,0:T(8,128)(2,1)S(1)}, bf16[512,256]{1,0:T(8,128)(2,1)}, u32[]{:S(2)}) copy-start(bf16[512,256]{1,0:T(8,128)(2,1)} %slice.45.q_ref) | copy-start | bytes 786436
  84.0 16.8 %copy-start.7 = (f32[512,256]{1,0:T(8,128)S(1)}, f32[512,256]{1,0:T(8,128)}, u32[]{:S(2)}) copy-start(f32[512,256]{1,0:T(8,128)} %copy-done.6) | copy-start | bytes 1572868
  84.0 16.8 %copy-start.9 = (f32[512,256]{1,0:T(8,128)S(1)}, f32[512,256]{1,0:T(8,128)}, u32[]{:S(2)}) copy-start(f32[512,256]{1,0:T(8,128)} %copy-done.8) | copy-start | bytes 1572868
  84.0 16.8 %copy-start.11 = (f32[512,256]{1,0:T(8,128)S(1)}, f32[512,256]{1,0:T(8,128)}, u32[]{:S(2)}) copy-start(f32[512,256]{1,0:T(8,128)} %copy-done.10) | copy-start | bytes 1572868
  98.9 2.0 %collective-permute-start.7 = (bf16[512,512]{1,0:T(8,128)(2,1)S(1)}, bf16[512,512]{1,0:T(8,128)(2,1)S(1)}, u32[]{:S(2)}, u32[]{:S(2)}) collective-permute-start(bf16[512,512]{1,0:T(8,128)(2,1)S(1)} %broadcast_select_fusion.1), channel_id=1, source_target_pairs={{0,1},{1,0},{2,3},{3,2},{4,5},{5,4},{6,7},{7,6},{8,9},{9,8},{10,11... | collective-permute-start | bytes 1572872 | tf_op jit(solution)/shard_map/ppermute | solution.py:211
  100.9 6.9 %copy-start.19 = (bf16[512,1536]{1,0:T(8,128)(2,1)S(1)}, bf16[512,1536]{1,0:T(8,128)(2,1)}, u32[]{:S(2)}) copy-start(bf16[512,1536]{1,0:T(8,128)(2,1)} %param.5) | copy-start | bytes 4718596
  100.9 8.8 %slice-start = ((s8[9437184]{0:T(1024)(128)(4,1)}), s8[4194304]{0:T(1024)(128)(4,1)S(1)}, s32[]{:S(2)}) async-start(s8[9437184]{0:T(1024)(128)(4,1)} %bitcast.10), calls=%async_computation | async-start | bytes 8388608
  100.9 8.8 %slice-start.1 = ((s8[9437184]{0:T(1024)(128)(4,1)}), s8[4194304]{0:T(1024)(128)(4,1)S(1)}, s32[]{:S(2)}) async-start(s8[9437184]{0:T(1024)(128)(4,1)} %bitcast.10), calls=%async_computation.1 | async-start | bytes 8388608
  107.7 2.0 %slice-start.2 = ((s8[9437184]{0:T(1024)(128)(4,1)}), s8[1048576]{0:T(1024)(128)(4,1)S(1)}, s32[]{:S(2)}) async-start(s8[9437184]{0:T(1024)(128)(4,1)} %bitcast.10), calls=%async_computation.2 | async-start | bytes 2097152
  114.8 14.9 %copy-start.5 = (f32[31,1536]{1,0:T(8,128)S(1)}, f32[31,1536]{1,0:T(8,128)}, u32[]{:S(2)}) copy-start(f32[31,1536]{1,0:T(8,128)} %taps_ref.1) | copy-start | bytes 571396
  115.7 7.1 %collective-permute-start.9 = (bf16[16,1536]{1,0:T(8,128)(2,1)S(1)}, bf16[16,1536]{1,0:T(8,128)(2,1)S(1)}, u32[]{:S(2)}, u32[]{:S(2)}) collective-permute-start(bf16[16,1536]{1,0:T(8,128)(2,1)S(1)} %get-tuple-element.37), channel_id=1, source_target_pairs={{1,0},{2,1},{3,2},{4,3},{5,4},{6,5},{7,6},{8,7},{9,8},{10,9},{11,1... | collective-permute-start | bytes 147464 | tf_op jit(solution)/shard_map/ppermute | solution.py:208
  120.8 9.0 %collective-permute-start.8 = (bf16[16,1536]{1,0:T(8,128)(2,1)S(1)}, bf16[16,1536]{1,0:T(8,128)(2,1)S(1)}, u32[]{:S(2)}, u32[]{:S(2)}) collective-permute-start(bf16[16,1536]{1,0:T(8,128)(2,1)S(1)} %get-tuple-element.38), channel_id=1, source_target_pairs={{0,1},{1,2},{2,3},{3,4},{4,5},{5,6},{6,7},{7,8},{8,9},{9,10},{10,1... | collective-permute-start | bytes 147464 | tf_op jit(solution)/shard_map/ppermute | solution.py:208

commit v3 on v2

--- a/solution.py
+++ b/solution.py
@@ -148,9 +148,9 @@
         out_shape=[state] * 3,
         compiler_params=pltpu.CompilerParams(vmem_limit_bytes=40 << 20),
         cost_estimate=pl.CostEstimate(
-            flops=2 * pairs * 2 * 2 * count * 2 * count * 256,
-            bytes_accessed=12 << 20,
-            transcendentals=2 * pairs * count * 2 * count,
+            flops=pairs * count * 2 * count,
+            bytes_accessed=1 << 20,
+            transcendentals=0,
         ),
         name="near_attention",
     )(queries, own, other, own, other)
@@ -170,9 +170,9 @@
         out_shape=jax.ShapeDtypeStruct((count, width), jnp.bfloat16),
         compiler_params=pltpu.CompilerParams(vmem_limit_bytes=40 << 20),
         cost_estimate=pl.CostEstimate(
-            flops=2 * pairs * 2 * 2 * count * 3 * count * 256,
-            bytes_accessed=12 << 20,
-            transcendentals=2 * pairs * count * 3 * count,
+            flops=pairs * count * 3 * count,
+            bytes_accessed=1 << 20,
+            transcendentals=0,
         ),
         name="far_attention",
     )(limits, queries, a, b, c, a, b, c, *state)

time: 142 us -> 138 us (0.972)
  waiting for transfers between devices: 27.8 us -> 25.6 us
  local copies, waits for them, and re-layouts: 12.7 us -> 10.9 us
    ppermute x6, waiting for transfers between devices: 25.9 us -> 23.7 us  [shifted(): return lax.ppermute(array, AXES, pairs)]
    unnamed x48, local copies, waits for them, and re-layouts: 11.1 us -> 9.23 us
  transfers between devices with their start and end apart: 10 -> 10, of which waited for: 5 -> 5; matrix products, arithmetic and copies ran while one was open for 7% -> 7% of each run, Pallas kernels for 20% -> 21%
where the time goes in v3:
time: 138 us; the launch traced here: 137 us
  Pallas kernels  47 us (34%)
  waiting for transfers between devices  25.6 us (19%)
  starting transfers between devices  25.2 us (18%)
  matrix products  18.8 us (14%)
  local copies, waits for them, and re-layouts  10.9 us (8%)
  other arithmetic  8.97 us (7%)
    ppermute x6, starting transfers between devices, shifted(): return lax.ppermute(array, AXES, pairs)  24.9 us
    ppermute x6, waiting for transfers between devices, shifted(): return lax.ppermute(array, AXES, pairs)  23.7 us
    pallas_call x2, Pallas kernels, call_far(): pl.pallas_call(functools.partial(far_kernel, count // 2), grid=(pairs,),...  20.6 us
    pallas_call x2, Pallas kernels, call_near(): pl.pallas_call(functools.partial(near_kernel, count // 2), grid=(pairs,),...  15 us
    dot_general x5, matrix products, project(): jnp.dot(normed, w_qkv[:, start:stop], preferred_element_type=jnp.float32)  12.3 us
    pallas_call x1, Pallas kernels, call_conv(): pl.pallas_call(functools.partial(conv_kernel_body, rows), grid=(count //...  11.5 us
    unnamed x48, local copies, waits for them, and re-layouts  9.23 us
    dot_general x1, matrix products, on_device(): jnp.dot(normed_again, w_point, preferred_element_type=jnp.float32)  5.1 us
  transfers between devices with their start and end apart: 10, of which 5 were waited for; matrix products, arithmetic and copies ran while one was open for 7% of the time, Pallas kernels for 21%

profile of v3, /device:TPU:4, one launch (start us, length us, event | category | flops | bytes accessed | tf_op | source)
XLA Modules:
  0.0 137.0 jit_solution(7495188401317368981)
XLA Ops:
  0.0 1.8 %convert_reduce_fusion = f32[512]{0:T(512)S(1)} fusion(bf16[512,1536]{1,0:T(8,128)(2,1)} %param.5), kind=kLoop, calls=%fused_computation.2 | loop fusion | flops 1572352 | bytes 1574912 | tf_op jit(solution)/shard_map/reduce_sum | solution.py:22
  1.9 2.0 %fusion.2 = f32[512]{0:T(512)S(1)} fusion(bf16[512,1536]{1,0:T(8,128)(2,1)} %param.5, f32[512]{0:T(512)S(1)} %broadcast_multiply_fusion.1), kind=kLoop, calls=%fused_computation.5 | loop fusion | flops 3145216 | bytes 1576960 | tf_op jit(solution)/shard_map/reduce_sum | solution.py:24
  3.8 0.4 fusion.3
  4.3 3.0 %fusion.24 = bf16[512,512]{1,0:T(8,128)(2,1)S(1)} fusion(bf16[512,1536]{1,0:T(8,128)(2,1)S(1)} %fusion.3, bf16[1536,2304]{1,0:T(8,128)(2,1)} %param.6), kind=kOutput, calls=%fused_computation.26 | convolution fusion | flops 805568512 | bytes 3670016 | tf_op jit(solution)/shard_map/dot_general | solution.py:216
  7.2 2.4 %fusion.21 = bf16[512,512]{1,0:T(8,128)(2,1)S(1)} fusion(bf16[512,1536]{1,0:T(8,128)(2,1)S(1)} %fusion.3, bf16[1536,2304]{1,0:T(8,128)(2,1)} %param.6), kind=kOutput, calls=%fused_computation.25 | convolution fusion | flops 805568512 | bytes 3670016 | tf_op jit(solution)/shard_map/dot_general | solution.py:216
  9.6 0.1 pad_maximum_fusion.k0_ref.v0_ref
  9.8 0.1 collective-permute-start.2
  9.8 6.4 %collective-permute-start.1 = (bf16[512,1024]{1,0:T(8,128)(2,1)S(1)}, bf16[512,1024]{1,0:T(8,128)(2,1)}, u32[]{:S(2)}, u32[]{:S(2)}) collective-permute-start(bf16[512,1024]{1,0:T(8,128)(2,1)S(1)} %pad_maximum_fusion.k0_ref.v0_ref), channel_id=1, source_target_pairs={{2,0},{3,1},{4,2},{5,3},{6,4},{7,5},{8,6},{9,7},{10,8},{11,9},{12,... | collective-permute-start | bytes 3145736 | tf_op jit(solution)/shard_map/ppermute | solution.py:208
  16.2 1.9 %collective-permute-start = (bf16[512,1024]{1,0:T(8,128)(2,1)S(1)}, bf16[512,1024]{1,0:T(8,128)(2,1)}, u32[]{:S(2)}, u32[]{:S(2)}) collective-permute-start(bf16[512,1024]{1,0:T(8,128)(2,1)S(1)} %pad_maximum_fusion.k0_ref.v0_ref), channel_id=1, source_target_pairs={{0,2},{1,3},{2,4},{3,5},{4,6},{5,7},{6,8},{7,9},{8,10},{9,11},{10,... | collective-permute-start | bytes 3145736 | tf_op jit(solution)/shard_map/ppermute | solution.py:208
  18.2 1.7 %convolution_convert_fusion = bf16[512,256]{1,0:T(8,128)(2,1)S(1)} fusion(bf16[512,1536]{1,0:T(8,128)(2,1)S(1)} %fusion.3, bf16[1536,2304]{1,0:T(8,128)(2,1)} %param.6), kind=kOutput, calls=%fused_computation.27 | convolution fusion | flops 402784256 | bytes 2621440 | tf_op jit(solution)/shard_map/dot_general | solution.py:216
  19.9 1.7 %convolution_convert_fusion.1 = bf16[512,256]{1,0:T(8,128)(2,1)S(1)} fusion(bf16[512,1536]{1,0:T(8,128)(2,1)S(1)} %fusion.3, bf16[1536,2304]{1,0:T(8,128)(2,1)} %param.6), kind=kOutput, calls=%fused_computation.28 | convolution fusion | flops 402784256 | bytes 2621440 | tf_op jit(solution)/shard_map/dot_general | solution.py:216
  21.6 0.9 pad_maximum_fusion.1.k0_ref.v0_ref
  22.4 0.2 collective-permute-start.3
  22.6 3.5 %fusion.18 = bf16[512,768]{1,0:T(8,128)(2,1)S(1)} fusion(bf16[512,1536]{1,0:T(8,128)(2,1)} %copy-done.20, bf16[1536,2304]{1,0:T(8,128)(2,1)} %param.6), kind=kOutput, calls=%fused_computation.24 | convolution fusion | flops 1208352768 | bytes 4718592 | tf_op jit(solution)/shard_map/dot_general | solution.py:216
  26.2 0.7 slice.45.q_ref
  26.9 0.9 slice.44.q_ref
  27.8 0.9 copy-done.3
  28.8 5.3 %near_attention.3 = (f32[512,256]{1,0:T(8,128)S(1)}, f32[512,256]{1,0:T(8,128)S(1)}, f32[512,256]{1,0:T(8,128)S(1)}) custom-call(bf16[512,256]{1,0:T(8,128)(2,1)S(1)} %copy-done.3, bf16[512,512]{1,0:T(8,128)(2,1)} %pad_maximum_fusion.1.k0_ref.v0_ref, bf16[512,512]{1,0:T(8,128)(2,1)} %collective-permute-done.3.k1_ref.v1_ref, ...), custom_call_target="tpu_custom_call" | custom-call | flops 1048576 | bytes 1048576 | tf_op jit(solution)/shard_map/near_attention/pallas_call | solution.py:143
  34.1 0.8 copy-done.11
  34.9 0.8 copy-done.13
  35.7 0.9 copy-done.15
  36.5 1.0 copy-done.1
  37.6 9.7 %near_attention.2 = (f32[512,512]{1,0:T(8,128)S(1)}, f32[512,512]{1,0:T(8,128)S(1)}, f32[512,512]{1,0:T(8,128)S(1)}) custom-call(bf16[512,512]{1,0:T(8,128)(2,1)S(1)} %copy-done.1, bf16[512,1024]{1,0:T(8,128)(2,1)S(1)} %pad_maximum_fusion.k0_ref.v0_ref, bf16[512,1024]{1,0:T(8,128)(2,1)} %collective-permute-done.2.k1_ref.v1_ref, ...), custom_call_target="tpu_custom_call" | custom-call | flops 2097152 | bytes 1048576 | tf_op jit(solution)/shard_map/near_attention/pallas_call | solution.py:143
  47.3 15.5 %collective-permute-done.ka_ref.va_ref = bf16[512,1024]{1,0:T(8,128)(2,1)} collective-permute-done((bf16[512,1024]{1,0:T(8,128)(2,1)S(1)}, bf16[512,1024]{1,0:T(8,128)(2,1)}, u32[]{:S(2)}, u32[]{:S(2)}) %collective-permute-start) | collective-permute-done | bytes 1048608 | tf_op jit(solution)/shard_map/ppermute | solution.py:208
  62.8 2.3 %broadcast_select_fusion = bf16[512,1024]{1,0:T(8,128)(2,1)} fusion(bf16[512,1024]{1,0:T(8,128)(2,1)} %collective-permute-done.1.kc_ref.vc_ref, bf16[512,1024]{1,0:T(8,128)(2,1)} %collective-permute-done.ka_ref.va_ref, pred[]{:T(512)S(6)} %eq.5), kind=kLoop, calls=%fused_computation.30 | loop fusion | flops 524288 | bytes 3145729 | tf_op jit(solution)/shard_map/jit(_where)/select_n | solution.py:248
  65.1 3.5 %collective-permute-start.4 = (bf16[512,512]{1,0:T(8,128)(2,1)}, bf16[512,512]{1,0:T(8,128)(2,1)S(1)}, u32[]{:S(2)}, u32[]{:S(2)}) collective-permute-start(bf16[512,512]{1,0:T(8,128)(2,1)} %pad_maximum_fusion.1.k0_ref.v0_ref), channel_id=1, source_target_pairs={{0,2},{1,3},{2,4},{3,5},{4,6},{5,7},{6,8},{7,9},{8,10},{9,11},{10,... | collective-permute-start | bytes 1572872 | tf_op jit(solution)/shard_map/ppermute | solution.py:208
  68.6 6.1 %collective-permute-start.5 = (bf16[512,512]{1,0:T(8,128)(2,1)}, bf16[512,512]{1,0:T(8,128)(2,1)S(1)}, u32[]{:S(2)}, u32[]{:S(2)}) collective-permute-start(bf16[512,512]{1,0:T(8,128)(2,1)} %pad_maximum_fusion.1.k0_ref.v0_ref), channel_id=1, source_target_pairs={{2,0},{3,1},{4,2},{5,3},{6,4},{7,5},{8,6},{9,7},{10,8},{11,9},{12,... | collective-permute-start | bytes 1572872 | tf_op jit(solution)/shard_map/ppermute | solution.py:208
  74.7 0.1 pad_add_fusion.lim_ref
  74.8 1.0 copy-done.2
  75.9 1.2 copy-done.6
  77.1 1.2 copy-done.8
  78.3 1.2 copy-done.10
  79.5 13.8 %far_attention.2 = bf16[512,512]{1,0:T(8,128)(2,1)S(1)} custom-call(s32[3]{0:T(128)S(1)} %pad_add_fusion.lim_ref, bf16[512,512]{1,0:T(8,128)(2,1)S(1)} %copy-done.2, bf16[512,1024]{1,0:T(8,128)(2,1)} %collective-permute-done.ka_ref.va_ref, bf16[512,1024]{1,0:T(8,128)(2,1)} %collective-permute-done.6.kb_ref.vb_ref, ...), custom_call_target="tpu_custom_call" | custom-call | flops 3145728 | bytes 1048576 | tf_op jit(solution)/shard_map/far_attention/pallas_call | solution.py:164
  93.3 1.2 collective-permute-done.5.kc_ref.vc_ref
  94.6 0.1 broadcast_select_fusion.1
  94.6 0.1 collective-permute-start.7
  94.7 1.9 %collective-permute-done.7.kb_ref.vb_ref = bf16[512,512]{1,0:T(8,128)(2,1)S(1)} collective-permute-done((bf16[512,512]{1,0:T(8,128)(2,1)S(1)}, bf16[512,512]{1,0:T(8,128)(2,1)S(1)}, u32[]{:S(2)}, u32[]{:S(2)}) %collective-permute-start.7) | collective-permute-done | bytes 524320 | tf_op jit(solution)/shard_map/ppermute | solution.py:211
  96.6 0.0 slice-start.1
  96.6 6.8 %far_attention.3 = bf16[512,256]{1,0:T(8,128)(2,1)S(1)} custom-call(s32[3]{0:T(128)S(1)} %pad_add_fusion.lim_ref, bf16[512,256]{1,0:T(8,128)(2,1)S(1)} %copy-done.4, bf16[512,512]{1,0:T(8,128)(2,1)S(1)} %collective-permute-done.4.ka_ref.va_ref, bf16[512,512]{1,0:T(8,128)(2,1)S(1)} %collective-permute-done.7.kb_ref.vb_ref, ...), custom_call_target="tpu_custom_call" | custom-call | flops 1572864 | bytes 1048576 | tf_op jit(solution)/shard_map/far_attention/pallas_call | solution.py:164
  103.5 1.5 %fusion.34 = (f32[512]{0:T(512)S(1)}, f32[512,1536]{1,0:T(8,128)S(1)}) fusion(bf16[768,1536]{1,0:T(8,128)(2,1)S(1)} %copy-done, bf16[512,256]{1,0:T(8,128)(2,1)S(1)} %far_attention.3, bf16[512,512]{1,0:T(8,128)(2,1)S(1)} %far_attention.2, bf16[512,1536]{1,0:T(8,128)(2,1)S(1)} %copy-done.19), kind=kOutput, calls=%fused_computation.45 | convolution fusion | flops 1211891200 | bytes 7866368 | tf_op jit(solution)/shard_map/dot_general | solution.py:258
  105.0 0.5 multiply_reduce_fusion
  105.5 5.1 %fusion.11 = f32[512,3072]{1,0:T(8,128)S(1)} fusion(bf16[1536,3072]{1,0:T(8,128)(2,1)S(1)} %bitcast.11, f32[512,1536]{1,0:T(8,128)S(1)} %get-tuple-element.40.after_ref, f32[512]{0:T(512)S(1)} %add_rsqrt_fusion, f32[512]{0:T(512)S(1)} %broadcast_multiply_fusion), kind=kOutput, calls=%fused_computation.17 | convolution fusion | flops 4834197504 | bytes 18878464 | tf_op jit(solution)/shard_map/dot_general | solution.py:260
  110.6 0.8 fusion.8.gated_ref
  111.4 5.0 %collective-permute-start.9 = (bf16[16,1536]{1,0:T(8,128)(2,1)S(1)}, bf16[16,1536]{1,0:T(8,128)(2,1)S(1)}, u32[]{:S(2)}, u32[]{:S(2)}) collective-permute-start(bf16[16,1536]{1,0:T(8,128)(2,1)S(1)} %get-tuple-element.37), channel_id=1, source_target_pairs={{1,0},{2,1},{3,2},{4,3},{5,4},{6,5},{7,6},{8,7},{9,8},{10,9},{11,1... | collective-permute-start | bytes 147464 | tf_op jit(solution)/shard_map/ppermute | solution.py:208
  116.5 1.9 %collective-permute-start.8 = (bf16[16,1536]{1,0:T(8,128)(2,1)S(1)}, bf16[16,1536]{1,0:T(8,128)(2,1)S(1)}, u32[]{:S(2)}, u32[]{:S(2)}) collective-permute-start(bf16[16,1536]{1,0:T(8,128)(2,1)S(1)} %get-tuple-element.38), channel_id=1, source_target_pairs={{0,1},{1,2},{2,3},{3,4},{4,5},{5,6},{6,7},{7,8},{8,9},{9,10},{10,1... | collective-permute-start | bytes 147464 | tf_op jit(solution)/shard_map/ppermute | solution.py:208
  118.4 0.2 collective-permute-done.9.right_ref
  118.6 6.9 %collective-permute-done.8.left_ref = bf16[16,1536]{1,0:T(8,128)(2,1)S(1)} collective-permute-done((bf16[16,1536]{1,0:T(8,128)(2,1)S(1)}, bf16[16,1536]{1,0:T(8,128)(2,1)S(1)}, u32[]{:S(2)}, u32[]{:S(2)}) %collective-permute-start.8) | collective-permute-done | bytes 49184 | tf_op jit(solution)/shard_map/ppermute | solution.py:208
  125.5 11.5 %conv_tail.1 = bf16[512,1536]{1,0:T(8,128)(2,1)} custom-call(bf16[512,1536]{1,0:T(8,128)(2,1)S(1)} %fusion.8.gated_ref, bf16[16,1536]{1,0:T(8,128)(2,1)S(1)} %collective-permute-done.8.left_ref, bf16[16,1536]{1,0:T(8,128)(2,1)S(1)} %collective-permute-done.9.right_ref, f32[512,1536]{1,0:T(8,128)S(1)} %get-tuple-element.40.after_ref, f32[31,1536]{1,0:T(8,128)S(1)} %copy-done.17), custom_call_target="tpu_custom_call" | custom-call | tf_op jit(solution)/shard_map/conv_tail/pallas_call | solution.py:187
  (50 shorter events, 0.1 us)
Async XLA Ops:
  0.0 103.5 %copy-start = (bf16[768,1536]{1,0:T(8,128)(2,1)S(1)}, bf16[768,1536]{1,0:T(8,128)(2,1)}, u32[]{:S(2)}) copy-start(bf16[768,1536]{1,0:T(8,128)(2,1)} %param.7) | copy-start | bytes 7077892
  0.0 3.8 %copy-start.18 = (bf16[512,1536]{1,0:T(8,128)(2,1)S(1)}, bf16[512,1536]{1,0:T(8,128)(2,1)}, u32[]{:S(2)}) copy-start(bf16[512,1536]{1,0:T(8,128)(2,1)} %param.5) | copy-start | bytes 4718596
  4.3 15.6 %copy-start.20 = (bf16[512,1536]{1,0:T(8,128)(2,1)}, bf16[512,1536]{1,0:T(8,128)(2,1)S(1)}, u32[]{:S(2)}) copy-start(bf16[512,1536]{1,0:T(8,128)(2,1)S(1)} %fusion.3) | copy-start | bytes 4718596
  9.8 26.8 %collective-permute-start.2 = (bf16[512,1024]{1,0:T(8,128)(2,1)S(1)}, bf16[512,1024]{1,0:T(8,128)(2,1)}, u32[]{:S(2)}, u32[]{:S(2)}) collective-permute-start(bf16[512,1024]{1,0:T(8,128)(2,1)S(1)} %pad_maximum_fusion.k0_ref.v0_ref), channel_id=1, source_target_pairs={{0,1},{1,0},{2,3},{3,2},{4,5},{5,4},{6,7},{7,6},{8,9},{9,8},{10,11... | collective-permute-start | bytes 3145736 | tf_op jit(solution)/shard_map/ppermute | solution.py:211
  9.8 37.5 %collective-permute-start.1 = (bf16[512,1024]{1,0:T(8,128)(2,1)S(1)}, bf16[512,1024]{1,0:T(8,128)(2,1)}, u32[]{:S(2)}, u32[]{:S(2)}) collective-permute-start(bf16[512,1024]{1,0:T(8,128)(2,1)S(1)} %pad_maximum_fusion.k0_ref.v0_ref), channel_id=1, source_target_pairs={{2,0},{3,1},{4,2},{5,3},{6,4},{7,5},{8,6},{9,7},{10,8},{11,9},{12,... | collective-permute-start | bytes 3145736 | tf_op jit(solution)/shard_map/ppermute | solution.py:208
  16.2 46.5 %collective-permute-start = (bf16[512,1024]{1,0:T(8,128)(2,1)S(1)}, bf16[512,1024]{1,0:T(8,128)(2,1)}, u32[]{:S(2)}, u32[]{:S(2)}) collective-permute-start(bf16[512,1024]{1,0:T(8,128)(2,1)S(1)} %pad_maximum_fusion.k0_ref.v0_ref), channel_id=1, source_target_pairs={{0,2},{1,3},{2,4},{3,5},{4,6},{5,7},{6,8},{7,9},{8,10},{9,11},{10,... | collective-permute-start | bytes 3145736 | tf_op jit(solution)/shard_map/ppermute | solution.py:208
  22.4 5.4 %collective-permute-start.3 = (bf16[512,512]{1,0:T(8,128)(2,1)}, bf16[512,512]{1,0:T(8,128)(2,1)}, u32[]{:S(2)}, u32[]{:S(2)}) collective-permute-start(bf16[512,512]{1,0:T(8,128)(2,1)} %pad_maximum_fusion.1.k0_ref.v0_ref), channel_id=1, source_target_pairs={{0,1},{1,0},{2,3},{3,2},{4,5},{5,4},{6,7},{7,6},{8,9},{9,8},{10,11... | collective-permute-start | bytes 1572872 | tf_op jit(solution)/shard_map/ppermute | solution.py:211
  27.8 1.0 copy-start.3
  34.1 0.8 copy-start.11
  34.9 0.8 copy-start.13
  35.7 0.9 copy-start.15
  36.5 1.0 copy-start.1
  47.3 17.8 %copy-start.5 = (f32[512,512]{1,0:T(8,128)}, f32[512,512]{1,0:T(8,128)S(1)}, u32[]{:S(2)}) copy-start(f32[512,512]{1,0:T(8,128)S(1)} %get-tuple-element.28.acc_ref) | copy-start | bytes 3145732
  47.3 21.3 %copy-start.7 = (f32[512,512]{1,0:T(8,128)}, f32[512,512]{1,0:T(8,128)S(1)}, u32[]{:S(2)}) copy-start(f32[512,512]{1,0:T(8,128)S(1)} %get-tuple-element.29.high_ref) | copy-start | bytes 3145732
  47.3 21.3 %copy-start.9 = (f32[512,512]{1,0:T(8,128)}, f32[512,512]{1,0:T(8,128)S(1)}, u32[]{:S(2)}) copy-start(f32[512,512]{1,0:T(8,128)S(1)} %get-tuple-element.30.total_ref) | copy-start | bytes 3145732
  65.1 9.8 %collective-permute-start.6 = (bf16[512,1024]{1,0:T(8,128)(2,1)}, bf16[512,1024]{1,0:T(8,128)(2,1)}, u32[]{:S(2)}, u32[]{:S(2)}) collective-permute-start(bf16[512,1024]{1,0:T(8,128)(2,1)} %broadcast_select_fusion), channel_id=1, source_target_pairs={{0,1},{1,0},{2,3},{3,2},{4,5},{5,4},{6,7},{7,6},{8,9},{9,8},{10,11... | collective-permute-start | bytes 3145736 | tf_op jit(solution)/shard_map/ppermute | solution.py:211
  65.1 28.3 %collective-permute-start.4 = (bf16[512,512]{1,0:T(8,128)(2,1)}, bf16[512,512]{1,0:T(8,128)(2,1)S(1)}, u32[]{:S(2)}, u32[]{:S(2)}) collective-permute-start(bf16[512,512]{1,0:T(8,128)(2,1)} %pad_maximum_fusion.1.k0_ref.v0_ref), channel_id=1, source_target_pairs={{0,2},{1,3},{2,4},{3,5},{4,6},{5,7},{6,8},{7,9},{8,10},{9,11},{10,... | collective-permute-start | bytes 1572872 | tf_op jit(solution)/shard_map/ppermute | solution.py:208
  68.6 25.9 %collective-permute-start.5 = (bf16[512,512]{1,0:T(8,128)(2,1)}, bf16[512,512]{1,0:T(8,128)(2,1)S(1)}, u32[]{:S(2)}, u32[]{:S(2)}) collective-permute-start(bf16[512,512]{1,0:T(8,128)(2,1)} %pad_maximum_fusion.1.k0_ref.v0_ref), channel_id=1, source_target_pairs={{2,0},{3,1},{4,2},{5,3},{6,4},{7,5},{8,6},{9,7},{10,8},{11,9},{12,... | collective-permute-start | bytes 1572872 | tf_op jit(solution)/shard_map/ppermute | solution.py:208
  74.8 1.0 copy-start.2
  75.9 1.2 copy-start.6
  77.1 1.2 copy-start.8
  78.3 1.2 copy-start.10
  79.5 17.1 %copy-start.4 = (bf16[512,256]{1,0:T(8,128)(2,1)S(1)}, bf16[512,256]{1,0:T(8,128)(2,1)}, u32[]{:S(2)}) copy-start(bf16[512,256]{1,0:T(8,128)(2,1)} %slice.45.q_ref) | copy-start | bytes 786436
  79.5 17.1 %copy-start.12 = (f32[512,256]{1,0:T(8,128)S(1)}, f32[512,256]{1,0:T(8,128)}, u32[]{:S(2)}) copy-start(f32[512,256]{1,0:T(8,128)} %copy-done.11) | copy-start | bytes 1572868
  79.5 17.1 %copy-start.14 = (f32[512,256]{1,0:T(8,128)S(1)}, f32[512,256]{1,0:T(8,128)}, u32[]{:S(2)}) copy-start(f32[512,256]{1,0:T(8,128)} %copy-done.13) | copy-start | bytes 1572868
  79.5 17.1 %copy-start.16 = (f32[512,256]{1,0:T(8,128)S(1)}, f32[512,256]{1,0:T(8,128)}, u32[]{:S(2)}) copy-start(f32[512,256]{1,0:T(8,128)} %copy-done.15) | copy-start | bytes 1572868
  93.3 10.1 %copy-start.19 = (bf16[512,1536]{1,0:T(8,128)(2,1)S(1)}, bf16[512,1536]{1,0:T(8,128)(2,1)}, u32[]{:S(2)}) copy-start(bf16[512,1536]{1,0:T(8,128)(2,1)} %param.5) | copy-start | bytes 4718596
  94.6 10.9 %slice-start = ((s8[9437184]{0:T(1024)(128)(4,1)}), s8[4194304]{0:T(1024)(128)(4,1)S(1)}, s32[]{:S(2)}) async-start(s8[9437184]{0:T(1024)(128)(4,1)} %bitcast.10), calls=%async_computation | async-start | bytes 8388608
  94.6 2.0 %collective-permute-start.7 = (bf16[512,512]{1,0:T(8,128)(2,1)S(1)}, bf16[512,512]{1,0:T(8,128)(2,1)S(1)}, u32[]{:S(2)}, u32[]{:S(2)}) collective-permute-start(bf16[512,512]{1,0:T(8,128)(2,1)S(1)} %broadcast_select_fusion.1), channel_id=1, source_target_pairs={{0,1},{1,0},{2,3},{3,2},{4,5},{5,4},{6,7},{7,6},{8,9},{9,8},{10,11... | collective-permute-start | bytes 1572872 | tf_op jit(solution)/shard_map/ppermute | solution.py:211
  96.6 8.8 %slice-start.1 = ((s8[9437184]{0:T(1024)(128)(4,1)}), s8[4194304]{0:T(1024)(128)(4,1)S(1)}, s32[]{:S(2)}) async-start(s8[9437184]{0:T(1024)(128)(4,1)} %bitcast.10), calls=%async_computation.1 | async-start | bytes 8388608
  103.5 2.0 %slice-start.2 = ((s8[9437184]{0:T(1024)(128)(4,1)}), s8[1048576]{0:T(1024)(128)(4,1)S(1)}, s32[]{:S(2)}) async-start(s8[9437184]{0:T(1024)(128)(4,1)} %bitcast.10), calls=%async_computation.2 | async-start | bytes 2097152
  110.6 14.9 %copy-start.17 = (f32[31,1536]{1,0:T(8,128)S(1)}, f32[31,1536]{1,0:T(8,128)}, u32[]{:S(2)}) copy-start(f32[31,1536]{1,0:T(8,128)} %taps_ref.1) | copy-start | bytes 571396
  111.4 7.2 %collective-permute-start.9 = (bf16[16,1536]{1,0:T(8,128)(2,1)S(1)}, bf16[16,1536]{1,0:T(8,128)(2,1)S(1)}, u32[]{:S(2)}, u32[]{:S(2)}) collective-permute-start(bf16[16,1536]{1,0:T(8,128)(2,1)S(1)} %get-tuple-element.37), channel_id=1, source_target_pairs={{1,0},{2,1},{3,2},{4,3},{5,4},{6,5},{7,6},{8,7},{9,8},{10,9},{11,1... | collective-permute-start | bytes 147464 | tf_op jit(solution)/shard_map/ppermute | solution.py:208
  116.5 9.0 %collective-permute-start.8 = (bf16[16,1536]{1,0:T(8,128)(2,1)S(1)}, bf16[16,1536]{1,0:T(8,128)(2,1)S(1)}, u32[]{:S(2)}, u32[]{:S(2)}) collective-permute-start(bf16[16,1536]{1,0:T(8,128)(2,1)S(1)} %get-tuple-element.38), channel_id=1, source_target_pairs={{0,1},{1,2},{2,3},{3,4},{4,5},{5,6},{6,7},{7,8},{8,9},{9,10},{10,1... | collective-permute-start | bytes 147464 | tf_op jit(solution)/shard_map/ppermute | solution.py:208

commit v4 on v3

--- a/solution.py
+++ b/solution.py
@@ -240,11 +240,8 @@
     queries_1, queries_2 = queries[:, :SPLIT], queries[:, SPLIT:]
     acc_1, high_1, sum_1 = call_near(queries_1, kv_1, other_1)
     acc_2, high_2, sum_2 = call_near(queries_2, kv_2, other_2)
-    kv_up, kv_down = kv_2, kv_2
-    kv_down, after_1, sum_1, sum_2 = wait((kv_down, after_1, sum_1, sum_2))
-    after_2 = shifted(kv_down, -2)
-    kv_up, before_1, sum_1 = wait((kv_up, before_1, sum_1))
-    before_2 = shifted(kv_up, 2)
+    kv_far, sum_1, sum_2 = wait((kv_2, sum_1, sum_2))
+    before_2, after_2 = shifted(kv_far, 2), shifted(kv_far, -2)
     bridge_1 = swapped(jnp.where(even, after_1, before_1))
     attended_1 = call_far(
         limits, queries_1, before_1, bridge_1, after_1, (acc_1, high_1, sum_1)

time: 138 us -> 158 us (1.14)
  waiting for transfers between devices: 25.6 us -> 41.4 us
  starting transfers between devices: 25.2 us -> 28.9 us
    ppermute x6, waiting for transfers between devices: 23.7 us -> 39.5 us  [shifted(): return lax.ppermute(array, AXES, pairs)]
    ppermute x6, starting transfers between devices: 24.9 us -> 28.2 us  [shifted(): return lax.ppermute(array, AXES, pairs)]
    slice x2, local copies, waits for them, and re-layouts: 1.64 us -> 0.05 us  [on_device(): queries_1, queries_2 = (queries[:, :SPLIT], queries[:, SPLIT:])]
    unnamed x48 -> x50, local copies, waits for them, and re-layouts: 9.23 us -> 10.2 us
  transfers between devices with their start and end apart: 10 -> 10, of which waited for: 5 -> 4; matrix products, arithmetic and copies ran while one was open for 7% -> 6% of each run, Pallas kernels for 21% -> 19%
where the time goes in v4:
time: 158 us; the launch traced here: 155 us
  Pallas kernels  47.2 us (30%)
  waiting for transfers between devices  41.4 us (26%)
  starting transfers between devices  28.9 us (18%)
  matrix products  18.4 us (12%)
  local copies, waits for them, and re-layouts  10.3 us (7%)
  other arithmetic  8.96 us (6%)
    ppermute x6, waiting for transfers between devices, shifted(): return lax.ppermute(array, AXES, pairs)  39.5 us
    ppermute x6, starting transfers between devices, shifted(): return lax.ppermute(array, AXES, pairs)  28.2 us
    pallas_call x2, Pallas kernels, call_far(): pl.pallas_call(functools.partial(far_kernel, count // 2), grid=(pairs,),...  20.6 us
    pallas_call x2, Pallas kernels, call_near(): pl.pallas_call(functools.partial(near_kernel, count // 2), grid=(pairs,),...  15.1 us
    dot_general x5, matrix products, project(): jnp.dot(normed, w_qkv[:, start:stop], preferred_element_type=jnp.float32)  11.8 us
    pallas_call x1, Pallas kernels, call_conv(): pl.pallas_call(functools.partial(conv_kernel_body, rows), grid=(count //...  11.5 us
    unnamed x50, local copies, waits for them, and re-layouts  10.2 us
    dot_general x1, matrix products, on_device(): jnp.dot(normed_again, w_point, preferred_element_type=jnp.float32)  5.1 us
  transfers between devices with their start and end apart: 10, of which 4 were waited for; matrix products, arithmetic and copies ran while one was open for 6% of the time, Pallas kernels for 19%

profile of v4, /device:TPU:4, one launch (start us, length us, event | category | flops | bytes accessed | tf_op | source)
XLA Modules:
  0.0 155.5 jit_solution(17021721599056586872)
XLA Ops:
  0.0 1.8 %convert_reduce_fusion = f32[512]{0:T(512)S(1)} fusion(bf16[512,1536]{1,0:T(8,128)(2,1)} %param.5), kind=kLoop, calls=%fused_computation.2 | loop fusion | flops 1572352 | bytes 1574912 | tf_op jit(solution)/shard_map/reduce_sum | solution.py:22
  1.9 2.0 %fusion.2 = f32[512]{0:T(512)S(1)} fusion(bf16[512,1536]{1,0:T(8,128)(2,1)} %param.5, f32[512]{0:T(512)S(1)} %broadcast_multiply_fusion.1), kind=kLoop, calls=%fused_computation.5 | loop fusion | flops 3145216 | bytes 1576960 | tf_op jit(solution)/shard_map/reduce_sum | solution.py:24
  3.8 0.4 fusion.3
  4.3 3.0 %fusion.24 = bf16[512,512]{1,0:T(8,128)(2,1)S(1)} fusion(bf16[512,1536]{1,0:T(8,128)(2,1)S(1)} %fusion.3, bf16[1536,2304]{1,0:T(8,128)(2,1)} %param.6), kind=kOutput, calls=%fused_computation.26 | convolution fusion | flops 805568512 | bytes 3670016 | tf_op jit(solution)/shard_map/dot_general | solution.py:216
  7.2 2.4 %fusion.21 = bf16[512,512]{1,0:T(8,128)(2,1)S(1)} fusion(bf16[512,1536]{1,0:T(8,128)(2,1)S(1)} %fusion.3, bf16[1536,2304]{1,0:T(8,128)(2,1)} %param.6), kind=kOutput, calls=%fused_computation.25 | convolution fusion | flops 805568512 | bytes 3670016 | tf_op jit(solution)/shard_map/dot_general | solution.py:216
  9.6 0.1 pad_maximum_fusion.k0_ref.v0_ref
  9.8 3.5 %collective-permute-start.4 = (bf16[512,1024]{1,0:T(8,128)(2,1)S(1)}, bf16[512,1024]{1,0:T(8,128)(2,1)}, u32[]{:S(2)}, u32[]{:S(2)}) collective-permute-start(bf16[512,1024]{1,0:T(8,128)(2,1)S(1)} %pad_maximum_fusion.k0_ref.v0_ref), channel_id=1, source_target_pairs={{0,2},{1,3},{2,4},{3,5},{4,6},{5,7},{6,8},{7,9},{8,10},{9,11},{10,... | collective-permute-start | bytes 3145736 | tf_op jit(solution)/shard_map/ppermute | solution.py:208
  13.3 6.0 %collective-permute-start.5 = (bf16[512,1024]{1,0:T(8,128)(2,1)S(1)}, bf16[512,1024]{1,0:T(8,128)(2,1)}, u32[]{:S(2)}, u32[]{:S(2)}) collective-permute-start(bf16[512,1024]{1,0:T(8,128)(2,1)S(1)} %pad_maximum_fusion.k0_ref.v0_ref), channel_id=1, source_target_pairs={{2,0},{3,1},{4,2},{5,3},{6,4},{7,5},{8,6},{9,7},{10,8},{11,9},{12,... | collective-permute-start | bytes 3145736 | tf_op jit(solution)/shard_map/ppermute | solution.py:208
  19.2 0.1 collective-permute-start
  19.3 1.7 %convolution_convert_fusion = bf16[512,256]{1,0:T(8,128)(2,1)S(1)} fusion(bf16[512,1536]{1,0:T(8,128)(2,1)S(1)} %fusion.3, bf16[1536,2304]{1,0:T(8,128)(2,1)} %param.6), kind=kOutput, calls=%fused_computation.27 | convolution fusion | flops 402784256 | bytes 2621440 | tf_op jit(solution)/shard_map/dot_general | solution.py:216
  21.0 1.7 %convolution_convert_fusion.1 = bf16[512,256]{1,0:T(8,128)(2,1)S(1)} fusion(bf16[512,1536]{1,0:T(8,128)(2,1)S(1)} %fusion.3, bf16[1536,2304]{1,0:T(8,128)(2,1)} %param.6), kind=kOutput, calls=%fused_computation.28 | convolution fusion | flops 402784256 | bytes 2621440 | tf_op jit(solution)/shard_map/dot_general | solution.py:216
  22.7 0.9 pad_maximum_fusion.1.k0_ref.v0_ref
  23.6 0.5 collective-permute-start.1
  24.1 17.4 %collective-permute-done.4.ka_ref.va_ref = bf16[512,1024]{1,0:T(8,128)(2,1)} collective-permute-done((bf16[512,1024]{1,0:T(8,128)(2,1)S(1)}, bf16[512,1024]{1,0:T(8,128)(2,1)}, u32[]{:S(2)}, u32[]{:S(2)}) %collective-permute-start.4) | collective-permute-done | bytes 1048608 | tf_op jit(solution)/shard_map/ppermute | solution.py:208
  41.4 20.4 %collective-permute-done.5.kc_ref.vc_ref = bf16[512,1024]{1,0:T(8,128)(2,1)} collective-permute-done((bf16[512,1024]{1,0:T(8,128)(2,1)S(1)}, bf16[512,1024]{1,0:T(8,128)(2,1)}, u32[]{:S(2)}, u32[]{:S(2)}) %collective-permute-start.5) | collective-permute-done | bytes 1048608 | tf_op jit(solution)/shard_map/ppermute | solution.py:208
  61.9 2.3 %broadcast_select_fusion = bf16[512,1024]{1,0:T(8,128)(2,1)} fusion(bf16[512,1024]{1,0:T(8,128)(2,1)} %collective-permute-done.5.kc_ref.vc_ref, bf16[512,1024]{1,0:T(8,128)(2,1)} %collective-permute-done.4.ka_ref.va_ref, pred[]{:T(512)S(6)} %eq.5), kind=kLoop, calls=%fused_computation.30 | loop fusion | flops 524288 | bytes 3145729 | tf_op jit(solution)/shard_map/jit(_where)/select_n | solution.py:245
  64.2 0.0 collective-permute-start.6
  64.2 3.0 %fusion.18 = bf16[512,768]{1,0:T(8,128)(2,1)S(1)} fusion(bf16[512,1536]{1,0:T(8,128)(2,1)S(1)} %copy-done.21, bf16[1536,2304]{1,0:T(8,128)(2,1)} %param.6), kind=kOutput, calls=%fused_computation.24 | convolution fusion | flops 1208352768 | bytes 4718592 | tf_op jit(solution)/shard_map/dot_general | solution.py:216
  67.3 5.5 %near_attention.3 = (f32[512,256]{1,0:T(8,128)S(1)}, f32[512,256]{1,0:T(8,128)S(1)}, f32[512,256]{1,0:T(8,128)S(1)}) custom-call(bf16[512,256]{1,0:T(8,128)(2,1)S(1)} %slice.45.q_ref, bf16[512,512]{1,0:T(8,128)(2,1)} %pad_maximum_fusion.1.k0_ref.v0_ref, bf16[512,512]{1,0:T(8,128)(2,1)} %collective-permute-done.1.k1_ref.v1_ref, ...), custom_call_target="tpu_custom_call" | custom-call | flops 1048576 | bytes 1048576 | tf_op jit(solution)/shard_map/near_attention/pallas_call | solution.py:143
  72.8 0.8 copy-done.11
  73.6 0.8 copy-done.13
  74.4 0.9 copy-done.15
  75.3 9.7 %near_attention.2 = (f32[512,512]{1,0:T(8,128)S(1)}, f32[512,512]{1,0:T(8,128)S(1)}, f32[512,512]{1,0:T(8,128)S(1)}) custom-call(bf16[512,512]{1,0:T(8,128)(2,1)S(1)} %slice.44.q_ref, bf16[512,1024]{1,0:T(8,128)(2,1)S(1)} %pad_maximum_fusion.k0_ref.v0_ref, bf16[512,1024]{1,0:T(8,128)(2,1)} %collective-permute-done.k1_ref.v1_ref, ...), custom_call_target="tpu_custom_call" | custom-call | flops 2097152 | bytes 1048576 | tf_op jit(solution)/shard_map/near_attention/pallas_call | solution.py:143
  85.0 1.0 copy-done.5
  86.0 1.0 copy-done.7
  87.0 1.0 copy-done.9
  87.9 2.5 %collective-permute-start.2 = (bf16[512,512]{1,0:T(8,128)(2,1)}, bf16[512,512]{1,0:T(8,128)(2,1)S(1)}, u32[]{:S(2)}, u32[]{:S(2)}) collective-permute-start(bf16[512,512]{1,0:T(8,128)(2,1)} %pad_maximum_fusion.1.k0_ref.v0_ref), channel_id=1, source_target_pairs={{0,2},{1,3},{2,4},{3,5},{4,6},{5,7},{6,8},{7,9},{8,10},{9,11},{10,... | collective-permute-start | bytes 1572872 | tf_op jit(solution)/shard_map/ppermute | solution.py:208
  90.4 7.1 %collective-permute-start.3 = (bf16[512,512]{1,0:T(8,128)(2,1)}, bf16[512,512]{1,0:T(8,128)(2,1)S(1)}, u32[]{:S(2)}, u32[]{:S(2)}) collective-permute-start(bf16[512,512]{1,0:T(8,128)(2,1)} %pad_maximum_fusion.1.k0_ref.v0_ref), channel_id=1, source_target_pairs={{2,0},{3,1},{4,2},{5,3},{6,4},{7,5},{8,6},{9,7},{10,8},{11,9},{12,... | collective-permute-start | bytes 1572872 | tf_op jit(solution)/shard_map/ppermute | solution.py:208
  97.6 0.1 pad_add_fusion.lim_ref
  97.7 1.0 copy-done.2
  98.7 1.2 copy-done.6
  99.9 1.2 copy-done.8
  101.2 1.2 copy-done.10
  102.4 13.8 %far_attention.2 = bf16[512,512]{1,0:T(8,128)(2,1)S(1)} custom-call(s32[3]{0:T(128)S(1)} %pad_add_fusion.lim_ref, bf16[512,512]{1,0:T(8,128)(2,1)S(1)} %copy-done.2, bf16[512,1024]{1,0:T(8,128)(2,1)} %collective-permute-done.4.ka_ref.va_ref, bf16[512,1024]{1,0:T(8,128)(2,1)} %collective-permute-done.6.kb_ref.vb_ref, ...), custom_call_target="tpu_custom_call" | custom-call | flops 3145728 | bytes 1048576 | tf_op jit(solution)/shard_map/far_attention/pallas_call | solution.py:164
  116.2 0.1 broadcast_select_fusion.1
  116.3 0.1 collective-permute-start.7
  116.4 1.9 %collective-permute-done.7.kb_ref.vb_ref = bf16[512,512]{1,0:T(8,128)(2,1)S(1)} collective-permute-done((bf16[512,512]{1,0:T(8,128)(2,1)S(1)}, bf16[512,512]{1,0:T(8,128)(2,1)S(1)}, u32[]{:S(2)}, u32[]{:S(2)}) %collective-permute-start.7) | collective-permute-done | bytes 524320 | tf_op jit(solution)/shard_map/ppermute | solution.py:211
  118.3 0.0 slice-start.1
  118.3 6.8 %far_attention.3 = bf16[512,256]{1,0:T(8,128)(2,1)S(1)} custom-call(s32[3]{0:T(128)S(1)} %pad_add_fusion.lim_ref, bf16[512,256]{1,0:T(8,128)(2,1)S(1)} %copy-done.4, bf16[512,512]{1,0:T(8,128)(2,1)S(1)} %collective-permute-done.2.ka_ref.va_ref, bf16[512,512]{1,0:T(8,128)(2,1)S(1)} %collective-permute-done.7.kb_ref.vb_ref, ...), custom_call_target="tpu_custom_call" | custom-call | flops 1572864 | bytes 1048576 | tf_op jit(solution)/shard_map/far_attention/pallas_call | solution.py:164
  125.1 0.0 slice-start.2
  125.1 1.5 fusion.34
  126.6 0.5 multiply_reduce_fusion
  127.1 5.1 %fusion.11 = f32[512,3072]{1,0:T(8,128)S(1)} fusion(bf16[1536,3072]{1,0:T(8,128)(2,1)S(1)} %bitcast.11, f32[512,1536]{1,0:T(8,128)S(1)} %get-tuple-element.32.after_ref, f32[512]{0:T(512)S(1)} %add_rsqrt_fusion, f32[512]{0:T(512)S(1)} %broadcast_multiply_fusion), kind=kOutput, calls=%fused_computation.17 | convolution fusion | flops 4834197504 | bytes 18878464 | tf_op jit(solution)/shard_map/dot_general | solution.py:257
  132.2 0.8 fusion.8.gated_ref
  133.1 2.0 %collective-permute-start.8 = (bf16[16,1536]{1,0:T(8,128)(2,1)S(1)}, bf16[16,1536]{1,0:T(8,128)(2,1)S(1)}, u32[]{:S(2)}, u32[]{:S(2)}) collective-permute-start(bf16[16,1536]{1,0:T(8,128)(2,1)S(1)} %get-tuple-element.30), channel_id=1, source_target_pairs={{0,1},{1,2},{2,3},{3,4},{4,5},{5,6},{6,7},{7,8},{8,9},{9,10},{10,1... | collective-permute-start | bytes 147464 | tf_op jit(solution)/shard_map/ppermute | solution.py:208
  135.2 7.1 %collective-permute-start.9 = (bf16[16,1536]{1,0:T(8,128)(2,1)S(1)}, bf16[16,1536]{1,0:T(8,128)(2,1)S(1)}, u32[]{:S(2)}, u32[]{:S(2)}) collective-permute-start(bf16[16,1536]{1,0:T(8,128)(2,1)S(1)} %get-tuple-element.29), channel_id=1, source_target_pairs={{1,0},{2,1},{3,2},{4,3},{5,4},{6,5},{7,6},{8,7},{9,8},{10,9},{11,1... | collective-permute-start | bytes 147464 | tf_op jit(solution)/shard_map/ppermute | solution.py:208
  142.3 1.7 %collective-permute-done.9.right_ref = bf16[16,1536]{1,0:T(8,128)(2,1)S(1)} collective-permute-done((bf16[16,1536]{1,0:T(8,128)(2,1)S(1)}, bf16[16,1536]{1,0:T(8,128)(2,1)S(1)}, u32[]{:S(2)}, u32[]{:S(2)}) %collective-permute-start.9) | collective-permute-done | bytes 49184 | tf_op jit(solution)/shard_map/ppermute | solution.py:208
  144.0 11.5 %conv_tail.1 = bf16[512,1536]{1,0:T(8,128)(2,1)} custom-call(bf16[512,1536]{1,0:T(8,128)(2,1)S(1)} %fusion.8.gated_ref, bf16[16,1536]{1,0:T(8,128)(2,1)S(1)} %collective-permute-done.8.left_ref, bf16[16,1536]{1,0:T(8,128)(2,1)S(1)} %collective-permute-done.9.right_ref, f32[512,1536]{1,0:T(8,128)S(1)} %get-tuple-element.32.after_ref, f32[31,1536]{1,0:T(8,128)S(1)} %copy-done.17), custom_call_target="tpu_custom_call" | custom-call | tf_op jit(solution)/shard_map/conv_tail/pallas_call | solution.py:187
  (52 shorter events, 0.2 us)
Async XLA Ops:
  0.0 125.1 %copy-start = (bf16[768,1536]{1,0:T(8,128)(2,1)S(1)}, bf16[768,1536]{1,0:T(8,128)(2,1)}, u32[]{:S(2)}) copy-start(bf16[768,1536]{1,0:T(8,128)(2,1)} %param.7) | copy-start | bytes 7077892
  0.0 3.8 %copy-start.18 = (bf16[512,1536]{1,0:T(8,128)(2,1)S(1)}, bf16[512,1536]{1,0:T(8,128)(2,1)}, u32[]{:S(2)}) copy-start(bf16[512,1536]{1,0:T(8,128)(2,1)} %param.5) | copy-start | bytes 4718596
  4.3 16.7 %copy-start.20 = (bf16[512,1536]{1,0:T(8,128)(2,1)}, bf16[512,1536]{1,0:T(8,128)(2,1)S(1)}, u32[]{:S(2)}) copy-start(bf16[512,1536]{1,0:T(8,128)(2,1)S(1)} %fusion.3) | copy-start | bytes 4718596
  9.8 31.7 %collective-permute-start.4 = (bf16[512,1024]{1,0:T(8,128)(2,1)S(1)}, bf16[512,1024]{1,0:T(8,128)(2,1)}, u32[]{:S(2)}, u32[]{:S(2)}) collective-permute-start(bf16[512,1024]{1,0:T(8,128)(2,1)S(1)} %pad_maximum_fusion.k0_ref.v0_ref), channel_id=1, source_target_pairs={{0,2},{1,3},{2,4},{3,5},{4,6},{5,7},{6,8},{7,9},{8,10},{9,11},{10,... | collective-permute-start | bytes 3145736 | tf_op jit(solution)/shard_map/ppermute | solution.py:208
  13.3 48.6 %collective-permute-start.5 = (bf16[512,1024]{1,0:T(8,128)(2,1)S(1)}, bf16[512,1024]{1,0:T(8,128)(2,1)}, u32[]{:S(2)}, u32[]{:S(2)}) collective-permute-start(bf16[512,1024]{1,0:T(8,128)(2,1)S(1)} %pad_maximum_fusion.k0_ref.v0_ref), channel_id=1, source_target_pairs={{2,0},{3,1},{4,2},{5,3},{6,4},{7,5},{8,6},{9,7},{10,8},{11,9},{12,... | collective-permute-start | bytes 3145736 | tf_op jit(solution)/shard_map/ppermute | solution.py:208
  19.2 56.1 %collective-permute-start = (bf16[512,1024]{1,0:T(8,128)(2,1)S(1)}, bf16[512,1024]{1,0:T(8,128)(2,1)}, u32[]{:S(2)}, u32[]{:S(2)}) collective-permute-start(bf16[512,1024]{1,0:T(8,128)(2,1)S(1)} %pad_maximum_fusion.k0_ref.v0_ref), channel_id=1, source_target_pairs={{0,1},{1,0},{2,3},{3,2},{4,5},{5,4},{6,7},{7,6},{8,9},{9,8},{10,11... | collective-permute-start | bytes 3145736 | tf_op jit(solution)/shard_map/ppermute | solution.py:211
  23.6 43.7 %collective-permute-start.1 = (bf16[512,512]{1,0:T(8,128)(2,1)}, bf16[512,512]{1,0:T(8,128)(2,1)}, u32[]{:S(2)}, u32[]{:S(2)}) collective-permute-start(bf16[512,512]{1,0:T(8,128)(2,1)} %pad_maximum_fusion.1.k0_ref.v0_ref), channel_id=1, source_target_pairs={{0,1},{1,0},{2,3},{3,2},{4,5},{5,4},{6,7},{7,6},{8,9},{9,8},{10,11... | collective-permute-start | bytes 1572872 | tf_op jit(solution)/shard_map/ppermute | solution.py:211
  24.1 40.1 %copy-start.21 = (bf16[512,1536]{1,0:T(8,128)(2,1)S(1)}, bf16[512,1536]{1,0:T(8,128)(2,1)}, u32[]{:S(2)}) copy-start(bf16[512,1536]{1,0:T(8,128)(2,1)} %copy-done.20) | copy-start | bytes 4718596
  64.2 33.5 %collective-permute-start.6 = (bf16[512,1024]{1,0:T(8,128)(2,1)}, bf16[512,1024]{1,0:T(8,128)(2,1)}, u32[]{:S(2)}, u32[]{:S(2)}) collective-permute-start(bf16[512,1024]{1,0:T(8,128)(2,1)} %broadcast_select_fusion), channel_id=1, source_target_pairs={{0,1},{1,0},{2,3},{3,2},{4,5},{5,4},{6,7},{7,6},{8,9},{9,8},{10,11... | collective-permute-start | bytes 3145736 | tf_op jit(solution)/shard_map/ppermute | solution.py:211
  67.3 17.7 %copy-start.3 = (bf16[512,256]{1,0:T(8,128)(2,1)}, bf16[512,256]{1,0:T(8,128)(2,1)S(1)}, u32[]{:S(2)}) copy-start(bf16[512,256]{1,0:T(8,128)(2,1)S(1)} %slice.45.q_ref) | copy-start | bytes 786436
  67.3 17.7 %copy-start.1 = (bf16[512,512]{1,0:T(8,128)(2,1)}, bf16[512,512]{1,0:T(8,128)(2,1)S(1)}, u32[]{:S(2)}) copy-start(bf16[512,512]{1,0:T(8,128)(2,1)S(1)} %slice.44.q_ref) | copy-start | bytes 1572868
  72.8 0.8 copy-start.11
  73.6 0.8 copy-start.13
  74.4 0.9 copy-start.15
  85.0 1.0 copy-start.5
  85.9 1.0 copy-start.7
  87.0 1.0 copy-start.9
  87.9 28.3 %collective-permute-start.2 = (bf16[512,512]{1,0:T(8,128)(2,1)}, bf16[512,512]{1,0:T(8,128)(2,1)S(1)}, u32[]{:S(2)}, u32[]{:S(2)}) collective-permute-start(bf16[512,512]{1,0:T(8,128)(2,1)} %pad_maximum_fusion.1.k0_ref.v0_ref), channel_id=1, source_target_pairs={{0,2},{1,3},{2,4},{3,5},{4,6},{5,7},{6,8},{7,9},{8,10},{9,11},{10,... | collective-permute-start | bytes 1572872 | tf_op jit(solution)/shard_map/ppermute | solution.py:208
  90.4 25.8 %collective-permute-start.3 = (bf16[512,512]{1,0:T(8,128)(2,1)}, bf16[512,512]{1,0:T(8,128)(2,1)S(1)}, u32[]{:S(2)}, u32[]{:S(2)}) collective-permute-start(bf16[512,512]{1,0:T(8,128)(2,1)} %pad_maximum_fusion.1.k0_ref.v0_ref), channel_id=1, source_target_pairs={{2,0},{3,1},{4,2},{5,3},{6,4},{7,5},{8,6},{9,7},{10,8},{11,9},{12,... | collective-permute-start | bytes 1572872 | tf_op jit(solution)/shard_map/ppermute | solution.py:208
  97.7 1.0 copy-start.2
  98.7 1.2 copy-start.6
  99.9 1.2 copy-start.8
  101.2 1.2 copy-start.10
  102.4 15.9 %copy-start.4 = (bf16[512,256]{1,0:T(8,128)(2,1)S(1)}, bf16[512,256]{1,0:T(8,128)(2,1)}, u32[]{:S(2)}) copy-start(bf16[512,256]{1,0:T(8,128)(2,1)} %copy-done.3) | copy-start | bytes 786436
  102.4 15.9 %copy-start.12 = (f32[512,256]{1,0:T(8,128)S(1)}, f32[512,256]{1,0:T(8,128)}, u32[]{:S(2)}) copy-start(f32[512,256]{1,0:T(8,128)} %copy-done.11) | copy-start | bytes 1572868
  102.4 15.9 %copy-start.14 = (f32[512,256]{1,0:T(8,128)S(1)}, f32[512,256]{1,0:T(8,128)}, u32[]{:S(2)}) copy-start(f32[512,256]{1,0:T(8,128)} %copy-done.13) | copy-start | bytes 1572868
  102.4 15.9 %copy-start.16 = (f32[512,256]{1,0:T(8,128)S(1)}, f32[512,256]{1,0:T(8,128)}, u32[]{:S(2)}) copy-start(f32[512,256]{1,0:T(8,128)} %copy-done.15) | copy-start | bytes 1572868
  116.2 9.0 %copy-start.19 = (bf16[512,1536]{1,0:T(8,128)(2,1)S(1)}, bf16[512,1536]{1,0:T(8,128)(2,1)}, u32[]{:S(2)}) copy-start(bf16[512,1536]{1,0:T(8,128)(2,1)} %param.5) | copy-start | bytes 4718596
  116.2 10.9 %slice-start = ((s8[9437184]{0:T(1024)(128)(4,1)}), s8[4194304]{0:T(1024)(128)(4,1)S(1)}, s32[]{:S(2)}) async-start(s8[9437184]{0:T(1024)(128)(4,1)} %bitcast.10), calls=%async_computation | async-start | bytes 8388608
  116.3 2.0 %collective-permute-start.7 = (bf16[512,512]{1,0:T(8,128)(2,1)S(1)}, bf16[512,512]{1,0:T(8,128)(2,1)S(1)}, u32[]{:S(2)}, u32[]{:S(2)}) collective-permute-start(bf16[512,512]{1,0:T(8,128)(2,1)S(1)} %broadcast_select_fusion.1), channel_id=1, source_target_pairs={{0,1},{1,0},{2,3},{3,2},{4,5},{5,4},{6,7},{7,6},{8,9},{9,8},{10,11... | collective-permute-start | bytes 1572872 | tf_op jit(solution)/shard_map/ppermute | solution.py:211
  118.3 8.8 %slice-start.1 = ((s8[9437184]{0:T(1024)(128)(4,1)}), s8[4194304]{0:T(1024)(128)(4,1)S(1)}, s32[]{:S(2)}) async-start(s8[9437184]{0:T(1024)(128)(4,1)} %bitcast.10), calls=%async_computation.1 | async-start | bytes 8388608
  125.1 2.0 %slice-start.2 = ((s8[9437184]{0:T(1024)(128)(4,1)}), s8[1048576]{0:T(1024)(128)(4,1)S(1)}, s32[]{:S(2)}) async-start(s8[9437184]{0:T(1024)(128)(4,1)} %bitcast.10), calls=%async_computation.2 | async-start | bytes 2097152
  132.2 11.8 %copy-start.17 = (f32[31,1536]{1,0:T(8,128)S(1)}, f32[31,1536]{1,0:T(8,128)}, u32[]{:S(2)}) copy-start(f32[31,1536]{1,0:T(8,128)} %taps_ref.1) | copy-start | bytes 571396
  133.1 9.2 %collective-permute-start.8 = (bf16[16,1536]{1,0:T(8,128)(2,1)S(1)}, bf16[16,1536]{1,0:T(8,128)(2,1)S(1)}, u32[]{:S(2)}, u32[]{:S(2)}) collective-permute-start(bf16[16,1536]{1,0:T(8,128)(2,1)S(1)} %get-tuple-element.30), channel_id=1, source_target_pairs={{0,1},{1,2},{2,3},{3,4},{4,5},{5,6},{6,7},{7,8},{8,9},{9,10},{10,1... | collective-permute-start | bytes 147464 | tf_op jit(solution)/shard_map/ppermute | solution.py:208
  135.2 8.9 %collective-permute-start.9 = (bf16[16,1536]{1,0:T(8,128)(2,1)S(1)}, bf16[16,1536]{1,0:T(8,128)(2,1)S(1)}, u32[]{:S(2)}, u32[]{:S(2)}) collective-permute-start(bf16[16,1536]{1,0:T(8,128)(2,1)S(1)} %get-tuple-element.29), channel_id=1, source_target_pairs={{1,0},{2,1},{3,2},{4,3},{5,4},{6,5},{7,6},{8,7},{9,8},{10,9},{11,1... | collective-permute-start | bytes 147464 | tf_op jit(solution)/shard_map/ppermute | solution.py:208

commit v5 on v3

--- a/solution.py
+++ b/solution.py
@@ -105,31 +105,79 @@
 
 
 def conv_kernel_body(
-    rows, gated_ref, left_ref, right_ref, after_ref, taps_ref, out_ref, wide_ref, sum_ref
+    rows, halo, inner, total, gated_ref, after_ref, taps_ref, out_ref,
+    wide_ref, sum_ref, edge_ref, got_ref, send_sem, recv_sem,
 ):
     count = gated_ref.shape[0]
-    halo = left_ref.shape[0]
     step = pl.program_id(0)
+    steps = count // rows
     blocks = D // LANES
+    me = lax.axis_index("outer") * inner + lax.axis_index("inner")
+    has_before, has_after = me > 0, me < total - 1
+    before, after = lax.rem(me + total - 1, total), lax.rem(me + 1, total)
+    before = (lax.div(before, inner), lax.rem(before, inner))
+    after = (lax.div(after, inner), lax.rem(after, inner))
+    sides = ((has_before, before), (has_after, after))
+    barrier = pltpu.get_barrier_semaphore()
+
+    def sending(side, device):
+        return pltpu.make_async_remote_copy(
+            src_ref=edge_ref.at[side],
+            dst_ref=got_ref.at[1 - side],
+            send_sem=send_sem.at[side],
+            recv_sem=recv_sem.at[1 - side],
+            device_id=device,
+            device_id_type=pl.DeviceIdType.MESH,
+        )
 
     @pl.when(step == 0)
     def _():
+        for present, device in sides:
+            @pl.when(present)
+            def _():
+                pl.semaphore_signal(
+                    barrier, inc=1, device_id=device, device_id_type=pl.DeviceIdType.MESH
+                )
+
+        edge_ref[0, :, :] = gated_ref[pl.ds(0, halo), :]
+        edge_ref[1, :, :] = gated_ref[pl.ds(count - halo, halo), :]
         for block in range(blocks):
             cols = pl.ds(block * LANES, LANES)
-            wide_ref[block, :halo, :] = left_ref[:, cols].astype(jnp.float32)
             wide_ref[block, pl.ds(halo, count), :] = gated_ref[:, cols].astype(jnp.float32)
-            wide_ref[block, pl.ds(halo + count, halo), :] = right_ref[:, cols].astype(jnp.float32)
-
-    first = pl.multiple_of(step * rows, rows)
+        pl.semaphore_wait(barrier, has_before.astype(jnp.int32) + has_after.astype(jnp.int32))
+        for side, (present, device) in enumerate(sides):
+            @pl.when(present)
+            def _():
+                sending(side, device).start()
+
+    @pl.when(step == steps - 2)
+    def _():
+        for side, (present, device) in enumerate(sides):
+            place = pl.ds(side * (halo + count), halo)
+
+            @pl.when(present)
+            def _():
+                sending(side, device).wait_send()
+                sending(1 - side, device).wait_recv()
+                for block in range(blocks):
+                    cols = pl.ds(block * LANES, LANES)
+                    wide_ref[block, place, :] = got_ref[side, :, cols].astype(jnp.float32)
+
+            @pl.when(jnp.logical_not(present))
+            def _():
+                for block in range(blocks):
+                    wide_ref[block, place, :] = jnp.zeros((halo, LANES), jnp.float32)
+
+    first = pl.multiple_of(lax.rem(step + 1, steps) * rows, rows)
     lead = halo - (KW - 1) // 2
     for block in range(blocks):
         cols = pl.ds(block * LANES, LANES)
-        total = jnp.zeros((rows, LANES), jnp.float32)
+        total_sum = jnp.zeros((rows, LANES), jnp.float32)
         for tap in range(KW):
-            total = total + taps_ref[pl.ds(tap, 1), cols] * (
+            total_sum = total_sum + taps_ref[pl.ds(tap, 1), cols] * (
                 wide_ref[block, pl.ds(first + (lead + tap), rows), :]
             )
-        sum_ref[:, cols] = total
+        sum_ref[:, cols] = total_sum
     normed = layer_norm(sum_ref[...])
     out_ref[...] = (after_ref[...] + normed / (1.0 + jnp.exp(-normed))).astype(jnp.bfloat16)
 
@@ -178,25 +226,33 @@
     )(limits, queries, a, b, c, a, b, c, *state)
 
 
-def call_conv(gated, left, right, after, taps):
+def call_conv(gated, after, taps):
     count = gated.shape[0]
-    halo = left.shape[0]
+    halo = 16
     rows = 64
+    steps = count // rows
+    inner = lax.axis_size("inner")
     whole = lambda array: pl.BlockSpec(array.shape, lambda i: (0, 0))
-    block = pl.BlockSpec((rows, D), lambda i: (i, 0))
+    block = pl.BlockSpec((rows, D), lambda i: (lax.rem(i + 1, steps), 0))
     return pl.pallas_call(
-        functools.partial(conv_kernel_body, rows),
-        grid=(count // rows,),
-        in_specs=[whole(gated), whole(left), whole(right), block, whole(taps)],
+        functools.partial(conv_kernel_body, rows, halo, inner, inner * lax.axis_size("outer")),
+        grid=(steps,),
+        in_specs=[whole(gated), block, whole(taps)],
         out_specs=block,
         out_shape=jax.ShapeDtypeStruct((count, D), jnp.bfloat16),
         scratch_shapes=[
             pltpu.VMEM((D // LANES, count + 2 * halo, LANES), jnp.float32),
             pltpu.VMEM((rows, D), jnp.float32),
+            pltpu.VMEM((2, halo, D), jnp.bfloat16),
+            pltpu.VMEM((2, halo, D), jnp.bfloat16),
+            pltpu.SemaphoreType.DMA((2,)),
+            pltpu.SemaphoreType.DMA((2,)),
         ],
-        compiler_params=pltpu.CompilerParams(vmem_limit_bytes=40 << 20),
+        compiler_params=pltpu.CompilerParams(
+            vmem_limit_bytes=40 << 20, collective_id=0, has_side_effects=True
+        ),
         name="conv_tail",
-    )(gated, left, right, after, taps)
+    )(gated, after, taps)
 
 
 def on_device(frames, w_qkv, w_out, w_point, conv_kernel):
@@ -259,9 +315,7 @@
     normed_again = layer_norm(after_attention).astype(jnp.bfloat16)
     projected = jnp.dot(normed_again, w_point, preferred_element_type=jnp.float32)
     gated = (projected[:, :D] * jax.nn.sigmoid(projected[:, D:])).astype(jnp.bfloat16)
-    left = shifted(gated[-16:], 1)
-    right = shifted(gated[:16], -1)
-    return call_conv(gated, left, right, after_attention, conv_kernel)
+    return call_conv(gated, after_attention, conv_kernel)
 
 
 def solution(mesh):

time: 138 us -> 127 us (0.920)
  waiting for transfers between devices: 25.6 us -> 18.6 us
  starting transfers between devices: 25.2 us -> 18.3 us
  Pallas kernels: 47 us -> 49.4 us
    ppermute x6 -> x4, waiting for transfers between devices: 23.7 us -> 16.7 us  [shifted(): return lax.ppermute(array, AXES, pairs)]
    ppermute x6 -> x4, starting transfers between devices: 24.9 us -> 17.9 us  [shifted(): return lax.ppermute(array, AXES, pairs)]
    pallas_call x1, Pallas kernels: 11.5 us -> 13.8 us  [call_conv(): pl.pallas_call(functools.partial(conv_kernel_body, rows, halo, inner, inn...]
    unnamed x48 -> x49, local copies, waits for them, and re-layouts: 9.23 us -> 10.4 us
  transfers between devices with their start and end apart: 10 -> 8, of which waited for: 5 -> 3; matrix products, arithmetic and copies ran while one was open for 7% -> 7% of each run, Pallas kernels for 21% -> 23%
where the time goes in v5:
time: 127 us; the launch traced here: 126 us
  Pallas kernels  49.4 us (39%)
  matrix products  18.8 us (15%)
  waiting for transfers between devices  18.6 us (15%)
  starting transfers between devices  18.3 us (14%)
  local copies, waits for them, and re-layouts  12.1 us (10%)
  other arithmetic  8.96 us (7%)
    pallas_call x2, Pallas kernels, call_far(): pl.pallas_call(functools.partial(far_kernel, count // 2), grid=(pairs,),...  20.6 us
    ppermute x4, starting transfers between devices, shifted(): return lax.ppermute(array, AXES, pairs)  17.9 us
    ppermute x4, waiting for transfers between devices, shifted(): return lax.ppermute(array, AXES, pairs)  16.7 us
    pallas_call x2, Pallas kernels, call_near(): pl.pallas_call(functools.partial(near_kernel, count // 2), grid=(pairs,),...  15 us
    pallas_call x1, Pallas kernels, call_conv(): pl.pallas_call(functools.partial(conv_kernel_body, rows, halo, inner, inn...  13.8 us
    dot_general x5, matrix products, project(): jnp.dot(normed, w_qkv[:, start:stop], preferred_element_type=jnp.float32)  12.3 us
    unnamed x49, local copies, waits for them, and re-layouts  10.4 us
    dot_general x1, matrix products, on_device(): jnp.dot(normed_again, w_point, preferred_element_type=jnp.float32)  5.1 us
  transfers between devices with their start and end apart: 8, of which 3 were waited for; matrix products, arithmetic and copies ran while one was open for 7% of the time, Pallas kernels for 23%

profile of v5, /device:TPU:4, one launch (start us, length us, event | category | flops | bytes accessed | tf_op | source)
XLA Modules:
  0.0 126.5 jit_solution(4112726040372599802)
XLA Ops:
  0.0 1.8 %convert_reduce_fusion = f32[512]{0:T(512)S(1)} fusion(bf16[512,1536]{1,0:T(8,128)(2,1)} %param.5), kind=kLoop, calls=%fused_computation.2 | loop fusion | flops 1572352 | bytes 1574912 | tf_op jit(solution)/shard_map/reduce_sum | solution.py:22
  1.9 2.0 %fusion.2 = f32[512]{0:T(512)S(1)} fusion(bf16[512,1536]{1,0:T(8,128)(2,1)} %param.5, f32[512]{0:T(512)S(1)} %broadcast_multiply_fusion.1), kind=kLoop, calls=%fused_computation.5 | loop fusion | flops 3145216 | bytes 1576960 | tf_op jit(solution)/shard_map/reduce_sum | solution.py:24
  3.8 0.4 fusion.3
  4.3 0.0 copy-start.20
  4.3 3.0 %fusion.24 = bf16[512,512]{1,0:T(8,128)(2,1)S(1)} fusion(bf16[512,1536]{1,0:T(8,128)(2,1)S(1)} %fusion.3, bf16[1536,2304]{1,0:T(8,128)(2,1)} %param.6), kind=kOutput, calls=%fused_computation.26 | convolution fusion | flops 805568512 | bytes 3670016 | tf_op jit(solution)/shard_map/dot_general | solution.py:272
  7.2 2.4 %fusion.21 = bf16[512,512]{1,0:T(8,128)(2,1)S(1)} fusion(bf16[512,1536]{1,0:T(8,128)(2,1)S(1)} %fusion.3, bf16[1536,2304]{1,0:T(8,128)(2,1)} %param.6), kind=kOutput, calls=%fused_computation.25 | convolution fusion | flops 805568512 | bytes 3670016 | tf_op jit(solution)/shard_map/dot_general | solution.py:272
  9.6 0.1 pad_maximum_fusion.k0_ref.v0_ref
  9.8 0.1 collective-permute-start.2
  9.8 6.4 %collective-permute-start.1 = (bf16[512,1024]{1,0:T(8,128)(2,1)S(1)}, bf16[512,1024]{1,0:T(8,128)(2,1)}, u32[]{:S(2)}, u32[]{:S(2)}) collective-permute-start(bf16[512,1024]{1,0:T(8,128)(2,1)S(1)} %pad_maximum_fusion.k0_ref.v0_ref), channel_id=1, source_target_pairs={{2,0},{3,1},{4,2},{5,3},{6,4},{7,5},{8,6},{9,7},{10,8},{11,9},{12,... | collective-permute-start | bytes 3145736 | tf_op jit(solution)/shard_map/ppermute | solution.py:264
  16.2 1.9 %collective-permute-start = (bf16[512,1024]{1,0:T(8,128)(2,1)S(1)}, bf16[512,1024]{1,0:T(8,128)(2,1)}, u32[]{:S(2)}, u32[]{:S(2)}) collective-permute-start(bf16[512,1024]{1,0:T(8,128)(2,1)S(1)} %pad_maximum_fusion.k0_ref.v0_ref), channel_id=1, source_target_pairs={{0,2},{1,3},{2,4},{3,5},{4,6},{5,7},{6,8},{7,9},{8,10},{9,11},{10,... | collective-permute-start | bytes 3145736 | tf_op jit(solution)/shard_map/ppermute | solution.py:264
  18.2 1.7 %convolution_convert_fusion = bf16[512,256]{1,0:T(8,128)(2,1)S(1)} fusion(bf16[512,1536]{1,0:T(8,128)(2,1)S(1)} %fusion.3, bf16[1536,2304]{1,0:T(8,128)(2,1)} %param.6), kind=kOutput, calls=%fused_computation.27 | convolution fusion | flops 402784256 | bytes 2621440 | tf_op jit(solution)/shard_map/dot_general | solution.py:272
  19.9 1.7 %convolution_convert_fusion.1 = bf16[512,256]{1,0:T(8,128)(2,1)S(1)} fusion(bf16[512,1536]{1,0:T(8,128)(2,1)S(1)} %fusion.3, bf16[1536,2304]{1,0:T(8,128)(2,1)} %param.6), kind=kOutput, calls=%fused_computation.28 | convolution fusion | flops 402784256 | bytes 2621440 | tf_op jit(solution)/shard_map/dot_general | solution.py:272
  21.6 0.8 pad_maximum_fusion.1.k0_ref.v0_ref
  22.4 0.2 collective-permute-start.3
  22.6 3.5 %fusion.18 = bf16[512,768]{1,0:T(8,128)(2,1)S(1)} fusion(bf16[512,1536]{1,0:T(8,128)(2,1)} %copy-done.20, bf16[1536,2304]{1,0:T(8,128)(2,1)} %param.6), kind=kOutput, calls=%fused_computation.24 | convolution fusion | flops 1208352768 | bytes 4718592 | tf_op jit(solution)/shard_map/dot_general | solution.py:272
  26.2 0.7 slice.37.q_ref
  26.9 0.9 slice.36.q_ref
  27.8 0.9 copy-done.3
  28.7 5.3 %near_attention.3 = (f32[512,256]{1,0:T(8,128)S(1)}, f32[512,256]{1,0:T(8,128)S(1)}, f32[512,256]{1,0:T(8,128)S(1)}) custom-call(bf16[512,256]{1,0:T(8,128)(2,1)S(1)} %copy-done.3, bf16[512,512]{1,0:T(8,128)(2,1)} %pad_maximum_fusion.1.k0_ref.v0_ref, bf16[512,512]{1,0:T(8,128)(2,1)} %collective-permute-done.3.k1_ref.v1_ref, ...), custom_call_target="tpu_custom_call" | custom-call | flops 1048576 | bytes 1048576 | tf_op jit(solution)/shard_map/near_attention/pallas_call | solution.py:191
  34.0 0.8 copy-done.11
  34.8 0.8 copy-done.13
  35.6 0.9 copy-done.15
  36.5 1.0 copy-done.1
  37.5 9.7 %near_attention.2 = (f32[512,512]{1,0:T(8,128)S(1)}, f32[512,512]{1,0:T(8,128)S(1)}, f32[512,512]{1,0:T(8,128)S(1)}) custom-call(bf16[512,512]{1,0:T(8,128)(2,1)S(1)} %copy-done.1, bf16[512,1024]{1,0:T(8,128)(2,1)S(1)} %pad_maximum_fusion.k0_ref.v0_ref, bf16[512,1024]{1,0:T(8,128)(2,1)} %collective-permute-done.2.k1_ref.v1_ref, ...), custom_call_target="tpu_custom_call" | custom-call | flops 2097152 | bytes 1048576 | tf_op jit(solution)/shard_map/near_attention/pallas_call | solution.py:191
  47.3 15.5 %collective-permute-done.ka_ref.va_ref = bf16[512,1024]{1,0:T(8,128)(2,1)} collective-permute-done((bf16[512,1024]{1,0:T(8,128)(2,1)S(1)}, bf16[512,1024]{1,0:T(8,128)(2,1)}, u32[]{:S(2)}, u32[]{:S(2)}) %collective-permute-start) | collective-permute-done | bytes 1048608 | tf_op jit(solution)/shard_map/ppermute | solution.py:264
  62.8 2.3 %broadcast_select_fusion = bf16[512,1024]{1,0:T(8,128)(2,1)} fusion(bf16[512,1024]{1,0:T(8,128)(2,1)} %collective-permute-done.1.kc_ref.vc_ref, bf16[512,1024]{1,0:T(8,128)(2,1)} %collective-permute-done.ka_ref.va_ref, pred[]{:T(512)S(6)} %eq.5), kind=kLoop, calls=%fused_computation.30 | loop fusion | flops 524288 | bytes 3145729 | tf_op jit(solution)/shard_map/jit(_where)/select_n | solution.py:304
  65.1 3.5 %collective-permute-start.4 = (bf16[512,512]{1,0:T(8,128)(2,1)}, bf16[512,512]{1,0:T(8,128)(2,1)S(1)}, u32[]{:S(2)}, u32[]{:S(2)}) collective-permute-start(bf16[512,512]{1,0:T(8,128)(2,1)} %pad_maximum_fusion.1.k0_ref.v0_ref), channel_id=1, source_target_pairs={{0,2},{1,3},{2,4},{3,5},{4,6},{5,7},{6,8},{7,9},{8,10},{9,11},{10,... | collective-permute-start | bytes 1572872 | tf_op jit(solution)/shard_map/ppermute | solution.py:264
  68.6 6.1 %collective-permute-start.5 = (bf16[512,512]{1,0:T(8,128)(2,1)}, bf16[512,512]{1,0:T(8,128)(2,1)S(1)}, u32[]{:S(2)}, u32[]{:S(2)}) collective-permute-start(bf16[512,512]{1,0:T(8,128)(2,1)} %pad_maximum_fusion.1.k0_ref.v0_ref), channel_id=1, source_target_pairs={{2,0},{3,1},{4,2},{5,3},{6,4},{7,5},{8,6},{9,7},{10,8},{11,9},{12,... | collective-permute-start | bytes 1572872 | tf_op jit(solution)/shard_map/ppermute | solution.py:264
  74.7 0.1 pad_add_fusion.lim_ref
  74.8 1.0 copy-done.2
  75.9 1.2 copy-done.6
  77.1 1.2 copy-done.8
  78.3 1.2 copy-done.10
  79.5 13.8 %far_attention.2 = bf16[512,512]{1,0:T(8,128)(2,1)S(1)} custom-call(s32[3]{0:T(128)S(1)} %pad_add_fusion.lim_ref, bf16[512,512]{1,0:T(8,128)(2,1)S(1)} %copy-done.2, bf16[512,1024]{1,0:T(8,128)(2,1)} %collective-permute-done.ka_ref.va_ref, bf16[512,1024]{1,0:T(8,128)(2,1)} %collective-permute-done.6.kb_ref.vb_ref, ...), custom_call_target="tpu_custom_call" | custom-call | flops 3145728 | bytes 1048576 | tf_op jit(solution)/shard_map/far_attention/pallas_call | solution.py:212
  93.3 1.2 collective-permute-done.5.kc_ref.vc_ref
  94.6 0.1 broadcast_select_fusion.1
  94.6 0.1 collective-permute-start.7
  94.7 1.9 %collective-permute-done.7.kb_ref.vb_ref = bf16[512,512]{1,0:T(8,128)(2,1)S(1)} collective-permute-done((bf16[512,512]{1,0:T(8,128)(2,1)S(1)}, bf16[512,512]{1,0:T(8,128)(2,1)S(1)}, u32[]{:S(2)}, u32[]{:S(2)}) %collective-permute-start.7) | collective-permute-done | bytes 524320 | tf_op jit(solution)/shard_map/ppermute | solution.py:267
  96.6 0.0 slice-start.1
  96.6 6.8 %far_attention.3 = bf16[512,256]{1,0:T(8,128)(2,1)S(1)} custom-call(s32[3]{0:T(128)S(1)} %pad_add_fusion.lim_ref, bf16[512,256]{1,0:T(8,128)(2,1)S(1)} %copy-done.4, bf16[512,512]{1,0:T(8,128)(2,1)S(1)} %collective-permute-done.4.ka_ref.va_ref, bf16[512,512]{1,0:T(8,128)(2,1)S(1)} %collective-permute-done.7.kb_ref.vb_ref, ...), custom_call_target="tpu_custom_call" | custom-call | flops 1572864 | bytes 1048576 | tf_op jit(solution)/shard_map/far_attention/pallas_call | solution.py:212
  103.5 0.0 slice-start.2
  103.5 1.5 %fusion.33 = (f32[512]{0:T(512)S(1)}, f32[512,1536]{1,0:T(8,128)S(1)}) fusion(bf16[768,1536]{1,0:T(8,128)(2,1)S(1)} %copy-done, bf16[512,256]{1,0:T(8,128)(2,1)S(1)} %far_attention.3, bf16[512,512]{1,0:T(8,128)(2,1)S(1)} %far_attention.2, bf16[512,1536]{1,0:T(8,128)(2,1)S(1)} %copy-done.19), kind=kOutput, calls=%fused_computation.44 | convolution fusion | flops 1211891200 | bytes 7866368 | tf_op jit(solution)/shard_map/dot_general | solution.py:314
  105.0 0.5 multiply_reduce_fusion
  105.5 5.1 %fusion.11 = f32[512,3072]{1,0:T(8,128)S(1)} fusion(bf16[1536,3072]{1,0:T(8,128)(2,1)S(1)} %bitcast.11, f32[512,1536]{1,0:T(8,128)S(1)} %get-tuple-element.38.after_ref, f32[512]{0:T(512)S(1)} %add_rsqrt_fusion, f32[512]{0:T(512)S(1)} %broadcast_multiply_fusion), kind=kOutput, calls=%fused_computation.17 | convolution fusion | flops 4834197504 | bytes 18878464 | tf_op jit(solution)/shard_map/dot_general | solution.py:316
  110.6 0.8 fusion.8.gated_ref
  111.4 0.1 copy-done.17
  111.5 13.8 %conv_tail.1 = bf16[512,1536]{1,0:T(8,128)(2,1)S(1)} custom-call(bf16[512,1536]{1,0:T(8,128)(2,1)S(1)} %fusion.8.gated_ref, f32[512,1536]{1,0:T(8,128)S(1)} %get-tuple-element.38.after_ref, f32[31,1536]{1,0:T(8,128)S(1)} %copy-done.17), custom_call_target="tpu_custom_call" | custom-call | tf_op jit(solution)/shard_map/conv_tail/pallas_call | solution.py:237
  125.3 1.1 copy.15
  (46 shorter events, 0.1 us)
Async XLA Ops:
  0.0 103.5 %copy-start = (bf16[768,1536]{1,0:T(8,128)(2,1)S(1)}, bf16[768,1536]{1,0:T(8,128)(2,1)}, u32[]{:S(2)}) copy-start(bf16[768,1536]{1,0:T(8,128)(2,1)} %param.7) | copy-start | bytes 7077892
  0.0 3.8 %copy-start.18 = (bf16[512,1536]{1,0:T(8,128)(2,1)S(1)}, bf16[512,1536]{1,0:T(8,128)(2,1)}, u32[]{:S(2)}) copy-start(bf16[512,1536]{1,0:T(8,128)(2,1)} %param.5) | copy-start | bytes 4718596
  4.3 15.6 %copy-start.20 = (bf16[512,1536]{1,0:T(8,128)(2,1)}, bf16[512,1536]{1,0:T(8,128)(2,1)S(1)}, u32[]{:S(2)}) copy-start(bf16[512,1536]{1,0:T(8,128)(2,1)S(1)} %fusion.3) | copy-start | bytes 4718596
  9.8 26.7 %collective-permute-start.2 = (bf16[512,1024]{1,0:T(8,128)(2,1)S(1)}, bf16[512,1024]{1,0:T(8,128)(2,1)}, u32[]{:S(2)}, u32[]{:S(2)}) collective-permute-start(bf16[512,1024]{1,0:T(8,128)(2,1)S(1)} %pad_maximum_fusion.k0_ref.v0_ref), channel_id=1, source_target_pairs={{0,1},{1,0},{2,3},{3,2},{4,5},{5,4},{6,7},{7,6},{8,9},{9,8},{10,11... | collective-permute-start | bytes 3145736 | tf_op jit(solution)/shard_map/ppermute | solution.py:267
  9.8 37.4 %collective-permute-start.1 = (bf16[512,1024]{1,0:T(8,128)(2,1)S(1)}, bf16[512,1024]{1,0:T(8,128)(2,1)}, u32[]{:S(2)}, u32[]{:S(2)}) collective-permute-start(bf16[512,1024]{1,0:T(8,128)(2,1)S(1)} %pad_maximum_fusion.k0_ref.v0_ref), channel_id=1, source_target_pairs={{2,0},{3,1},{4,2},{5,3},{6,4},{7,5},{8,6},{9,7},{10,8},{11,9},{12,... | collective-permute-start | bytes 3145736 | tf_op jit(solution)/shard_map/ppermute | solution.py:264
  16.2 46.5 %collective-permute-start = (bf16[512,1024]{1,0:T(8,128)(2,1)S(1)}, bf16[512,1024]{1,0:T(8,128)(2,1)}, u32[]{:S(2)}, u32[]{:S(2)}) collective-permute-start(bf16[512,1024]{1,0:T(8,128)(2,1)S(1)} %pad_maximum_fusion.k0_ref.v0_ref), channel_id=1, source_target_pairs={{0,2},{1,3},{2,4},{3,5},{4,6},{5,7},{6,8},{7,9},{8,10},{9,11},{10,... | collective-permute-start | bytes 3145736 | tf_op jit(solution)/shard_map/ppermute | solution.py:264
  22.4 5.4 %collective-permute-start.3 = (bf16[512,512]{1,0:T(8,128)(2,1)}, bf16[512,512]{1,0:T(8,128)(2,1)}, u32[]{:S(2)}, u32[]{:S(2)}) collective-permute-start(bf16[512,512]{1,0:T(8,128)(2,1)} %pad_maximum_fusion.1.k0_ref.v0_ref), channel_id=1, source_target_pairs={{0,1},{1,0},{2,3},{3,2},{4,5},{5,4},{6,7},{7,6},{8,9},{9,8},{10,11... | collective-permute-start | bytes 1572872 | tf_op jit(solution)/shard_map/ppermute | solution.py:267
  27.8 1.0 copy-start.3
  34.0 0.8 copy-start.11
  34.8 0.8 copy-start.13
  35.6 0.9 copy-start.15
  36.5 1.0 copy-start.1
  47.2 17.8 %copy-start.5 = (f32[512,512]{1,0:T(8,128)}, f32[512,512]{1,0:T(8,128)S(1)}, u32[]{:S(2)}) copy-start(f32[512,512]{1,0:T(8,128)S(1)} %get-tuple-element.28.acc_ref) | copy-start | bytes 3145732
  47.2 21.4 %copy-start.7 = (f32[512,512]{1,0:T(8,128)}, f32[512,512]{1,0:T(8,128)S(1)}, u32[]{:S(2)}) copy-start(f32[512,512]{1,0:T(8,128)S(1)} %get-tuple-element.29.high_ref) | copy-start | bytes 3145732
  47.2 21.4 %copy-start.9 = (f32[512,512]{1,0:T(8,128)}, f32[512,512]{1,0:T(8,128)S(1)}, u32[]{:S(2)}) copy-start(f32[512,512]{1,0:T(8,128)S(1)} %get-tuple-element.30.total_ref) | copy-start | bytes 3145732
  65.1 9.8 %collective-permute-start.6 = (bf16[512,1024]{1,0:T(8,128)(2,1)}, bf16[512,1024]{1,0:T(8,128)(2,1)}, u32[]{:S(2)}, u32[]{:S(2)}) collective-permute-start(bf16[512,1024]{1,0:T(8,128)(2,1)} %broadcast_select_fusion), channel_id=1, source_target_pairs={{0,1},{1,0},{2,3},{3,2},{4,5},{5,4},{6,7},{7,6},{8,9},{9,8},{10,11... | collective-permute-start | bytes 3145736 | tf_op jit(solution)/shard_map/ppermute | solution.py:267
  65.1 28.3 %collective-permute-start.4 = (bf16[512,512]{1,0:T(8,128)(2,1)}, bf16[512,512]{1,0:T(8,128)(2,1)S(1)}, u32[]{:S(2)}, u32[]{:S(2)}) collective-permute-start(bf16[512,512]{1,0:T(8,128)(2,1)} %pad_maximum_fusion.1.k0_ref.v0_ref), channel_id=1, source_target_pairs={{0,2},{1,3},{2,4},{3,5},{4,6},{5,7},{6,8},{7,9},{8,10},{9,11},{10,... | collective-permute-start | bytes 1572872 | tf_op jit(solution)/shard_map/ppermute | solution.py:264
  68.6 25.9 %collective-permute-start.5 = (bf16[512,512]{1,0:T(8,128)(2,1)}, bf16[512,512]{1,0:T(8,128)(2,1)S(1)}, u32[]{:S(2)}, u32[]{:S(2)}) collective-permute-start(bf16[512,512]{1,0:T(8,128)(2,1)} %pad_maximum_fusion.1.k0_ref.v0_ref), channel_id=1, source_target_pairs={{2,0},{3,1},{4,2},{5,3},{6,4},{7,5},{8,6},{9,7},{10,8},{11,9},{12,... | collective-permute-start | bytes 1572872 | tf_op jit(solution)/shard_map/ppermute | solution.py:264
  74.8 1.0 copy-start.2
  75.9 1.2 copy-start.6
  77.1 1.2 copy-start.8
  78.3 1.2 copy-start.10
  79.5 17.1 %copy-start.4 = (bf16[512,256]{1,0:T(8,128)(2,1)S(1)}, bf16[512,256]{1,0:T(8,128)(2,1)}, u32[]{:S(2)}) copy-start(bf16[512,256]{1,0:T(8,128)(2,1)} %slice.37.q_ref) | copy-start | bytes 786436
  79.5 17.1 %copy-start.12 = (f32[512,256]{1,0:T(8,128)S(1)}, f32[512,256]{1,0:T(8,128)}, u32[]{:S(2)}) copy-start(f32[512,256]{1,0:T(8,128)} %copy-done.11) | copy-start | bytes 1572868
  79.5 17.1 %copy-start.14 = (f32[512,256]{1,0:T(8,128)S(1)}, f32[512,256]{1,0:T(8,128)}, u32[]{:S(2)}) copy-start(f32[512,256]{1,0:T(8,128)} %copy-done.13) | copy-start | bytes 1572868
  79.5 17.1 %copy-start.16 = (f32[512,256]{1,0:T(8,128)S(1)}, f32[512,256]{1,0:T(8,128)}, u32[]{:S(2)}) copy-start(f32[512,256]{1,0:T(8,128)} %copy-done.15) | copy-start | bytes 1572868
  93.3 10.1 %copy-start.19 = (bf16[512,1536]{1,0:T(8,128)(2,1)S(1)}, bf16[512,1536]{1,0:T(8,128)(2,1)}, u32[]{:S(2)}) copy-start(bf16[512,1536]{1,0:T(8,128)(2,1)} %param.5) | copy-start | bytes 4718596
  94.6 10.9 %slice-start = ((s8[9437184]{0:T(1024)(128)(4,1)}), s8[4194304]{0:T(1024)(128)(4,1)S(1)}, s32[]{:S(2)}) async-start(s8[9437184]{0:T(1024)(128)(4,1)} %bitcast.10), calls=%async_computation | async-start | bytes 8388608
  94.6 2.0 %collective-permute-start.7 = (bf16[512,512]{1,0:T(8,128)(2,1)S(1)}, bf16[512,512]{1,0:T(8,128)(2,1)S(1)}, u32[]{:S(2)}, u32[]{:S(2)}) collective-permute-start(bf16[512,512]{1,0:T(8,128)(2,1)S(1)} %broadcast_select_fusion.1), channel_id=1, source_target_pairs={{0,1},{1,0},{2,3},{3,2},{4,5},{5,4},{6,7},{7,6},{8,9},{9,8},{10,11... | collective-permute-start | bytes 1572872 | tf_op jit(solution)/shard_map/ppermute | solution.py:267
  96.6 8.8 %slice-start.1 = ((s8[9437184]{0:T(1024)(128)(4,1)}), s8[4194304]{0:T(1024)(128)(4,1)S(1)}, s32[]{:S(2)}) async-start(s8[9437184]{0:T(1024)(128)(4,1)} %bitcast.10), calls=%async_computation.1 | async-start | bytes 8388608
  103.5 2.0 %slice-start.2 = ((s8[9437184]{0:T(1024)(128)(4,1)}), s8[1048576]{0:T(1024)(128)(4,1)S(1)}, s32[]{:S(2)}) async-start(s8[9437184]{0:T(1024)(128)(4,1)} %bitcast.10), calls=%async_computation.2 | async-start | bytes 2097152
  110.6 0.9 copy-start.17

commit v6 on v5

--- a/solution.py
+++ b/solution.py
@@ -229,7 +229,7 @@
 def call_conv(gated, after, taps):
     count = gated.shape[0]
     halo = 16
-    rows = 64
+    rows = 128
     steps = count // rows
     inner = lax.axis_size("inner")
     whole = lambda array: pl.BlockSpec(array.shape, lambda i: (0, 0))

time: 127 us -> 127 us (level)
  transfers between devices with their start and end apart: 8 -> 8, of which waited for: 3 -> 3; matrix products, arithmetic and copies ran while one was open for 7% -> 8% of each run, Pallas kernels for 23% -> 23%
where the time goes in v6:
time: 127 us; the launch traced here: 126 us
  Pallas kernels  49.1 us (39%)
  matrix products  18.8 us (15%)
  waiting for transfers between devices  18.6 us (15%)
  starting transfers between devices  18.3 us (14%)
  local copies, waits for them, and re-layouts  12.1 us (10%)
  other arithmetic  8.96 us (7%)
    pallas_call x2, Pallas kernels, call_far(): pl.pallas_call(functools.partial(far_kernel, count // 2), grid=(pairs,),...  20.6 us
    ppermute x4, starting transfers between devices, shifted(): return lax.ppermute(array, AXES, pairs)  17.9 us
    ppermute x4, waiting for transfers between devices, shifted(): return lax.ppermute(array, AXES, pairs)  16.7 us
    pallas_call x2, Pallas kernels, call_near(): pl.pallas_call(functools.partial(near_kernel, count // 2), grid=(pairs,),...  15 us
    pallas_call x1, Pallas kernels, call_conv(): pl.pallas_call(functools.partial(conv_kernel_body, rows, halo, inner, inn...  13.5 us
    dot_general x5, matrix products, project(): jnp.dot(normed, w_qkv[:, start:stop], preferred_element_type=jnp.float32)  12.3 us
    unnamed x49, local copies, waits for them, and re-layouts  10.4 us
    dot_general x1, matrix products, on_device(): jnp.dot(normed_again, w_point, preferred_element_type=jnp.float32)  5.1 us
  transfers between devices with their start and end apart: 8, of which 3 were waited for; matrix products, arithmetic and copies ran while one was open for 8% of the time, Pallas kernels for 23%

profile of v6, /device:TPU:4, one launch (start us, length us, event | category | flops | bytes accessed | tf_op | source)
XLA Modules:
  0.0 126.2 jit_solution(3103261109032048786)
XLA Ops:
  0.0 1.8 %convert_reduce_fusion = f32[512]{0:T(512)S(1)} fusion(bf16[512,1536]{1,0:T(8,128)(2,1)} %param.5), kind=kLoop, calls=%fused_computation.2 | loop fusion | flops 1572352 | bytes 1574912 | tf_op jit(solution)/shard_map/reduce_sum | solution.py:22
  1.9 2.0 %fusion.2 = f32[512]{0:T(512)S(1)} fusion(bf16[512,1536]{1,0:T(8,128)(2,1)} %param.5, f32[512]{0:T(512)S(1)} %broadcast_multiply_fusion.1), kind=kLoop, calls=%fused_computation.5 | loop fusion | flops 3145216 | bytes 1576960 | tf_op jit(solution)/shard_map/reduce_sum | solution.py:24
  3.8 0.4 fusion.3
  4.3 0.0 copy-start.20
  4.3 3.0 %fusion.24 = bf16[512,512]{1,0:T(8,128)(2,1)S(1)} fusion(bf16[512,1536]{1,0:T(8,128)(2,1)S(1)} %fusion.3, bf16[1536,2304]{1,0:T(8,128)(2,1)} %param.6), kind=kOutput, calls=%fused_computation.26 | convolution fusion | flops 805568512 | bytes 3670016 | tf_op jit(solution)/shard_map/dot_general | solution.py:272
  7.2 2.4 %fusion.21 = bf16[512,512]{1,0:T(8,128)(2,1)S(1)} fusion(bf16[512,1536]{1,0:T(8,128)(2,1)S(1)} %fusion.3, bf16[1536,2304]{1,0:T(8,128)(2,1)} %param.6), kind=kOutput, calls=%fused_computation.25 | convolution fusion | flops 805568512 | bytes 3670016 | tf_op jit(solution)/shard_map/dot_general | solution.py:272
  9.6 0.1 pad_maximum_fusion.k0_ref.v0_ref
  9.8 0.1 collective-permute-start.2
  9.8 6.4 %collective-permute-start.1 = (bf16[512,1024]{1,0:T(8,128)(2,1)S(1)}, bf16[512,1024]{1,0:T(8,128)(2,1)}, u32[]{:S(2)}, u32[]{:S(2)}) collective-permute-start(bf16[512,1024]{1,0:T(8,128)(2,1)S(1)} %pad_maximum_fusion.k0_ref.v0_ref), channel_id=1, source_target_pairs={{2,0},{3,1},{4,2},{5,3},{6,4},{7,5},{8,6},{9,7},{10,8},{11,9},{12,... | collective-permute-start | bytes 3145736 | tf_op jit(solution)/shard_map/ppermute | solution.py:264
  16.2 1.9 %collective-permute-start = (bf16[512,1024]{1,0:T(8,128)(2,1)S(1)}, bf16[512,1024]{1,0:T(8,128)(2,1)}, u32[]{:S(2)}, u32[]{:S(2)}) collective-permute-start(bf16[512,1024]{1,0:T(8,128)(2,1)S(1)} %pad_maximum_fusion.k0_ref.v0_ref), channel_id=1, source_target_pairs={{0,2},{1,3},{2,4},{3,5},{4,6},{5,7},{6,8},{7,9},{8,10},{9,11},{10,... | collective-permute-start | bytes 3145736 | tf_op jit(solution)/shard_map/ppermute | solution.py:264
  18.2 1.7 %convolution_convert_fusion = bf16[512,256]{1,0:T(8,128)(2,1)S(1)} fusion(bf16[512,1536]{1,0:T(8,128)(2,1)S(1)} %fusion.3, bf16[1536,2304]{1,0:T(8,128)(2,1)} %param.6), kind=kOutput, calls=%fused_computation.27 | convolution fusion | flops 402784256 | bytes 2621440 | tf_op jit(solution)/shard_map/dot_general | solution.py:272
  19.9 1.7 %convolution_convert_fusion.1 = bf16[512,256]{1,0:T(8,128)(2,1)S(1)} fusion(bf16[512,1536]{1,0:T(8,128)(2,1)S(1)} %fusion.3, bf16[1536,2304]{1,0:T(8,128)(2,1)} %param.6), kind=kOutput, calls=%fused_computation.28 | convolution fusion | flops 402784256 | bytes 2621440 | tf_op jit(solution)/shard_map/dot_general | solution.py:272
  21.6 0.8 pad_maximum_fusion.1.k0_ref.v0_ref
  22.4 0.2 collective-permute-start.3
  22.6 3.5 %fusion.18 = bf16[512,768]{1,0:T(8,128)(2,1)S(1)} fusion(bf16[512,1536]{1,0:T(8,128)(2,1)} %copy-done.20, bf16[1536,2304]{1,0:T(8,128)(2,1)} %param.6), kind=kOutput, calls=%fused_computation.24 | convolution fusion | flops 1208352768 | bytes 4718592 | tf_op jit(solution)/shard_map/dot_general | solution.py:272
  26.2 0.7 slice.37.q_ref
  26.9 0.9 slice.36.q_ref
  27.8 0.9 copy-done.3
  28.7 5.3 %near_attention.3 = (f32[512,256]{1,0:T(8,128)S(1)}, f32[512,256]{1,0:T(8,128)S(1)}, f32[512,256]{1,0:T(8,128)S(1)}) custom-call(bf16[512,256]{1,0:T(8,128)(2,1)S(1)} %copy-done.3, bf16[512,512]{1,0:T(8,128)(2,1)} %pad_maximum_fusion.1.k0_ref.v0_ref, bf16[512,512]{1,0:T(8,128)(2,1)} %collective-permute-done.3.k1_ref.v1_ref, ...), custom_call_target="tpu_custom_call" | custom-call | flops 1048576 | bytes 1048576 | tf_op jit(solution)/shard_map/near_attention/pallas_call | solution.py:191
  34.0 0.8 copy-done.11
  34.8 0.8 copy-done.13
  35.6 0.9 copy-done.15
  36.5 1.0 copy-done.1
  37.5 9.7 %near_attention.2 = (f32[512,512]{1,0:T(8,128)S(1)}, f32[512,512]{1,0:T(8,128)S(1)}, f32[512,512]{1,0:T(8,128)S(1)}) custom-call(bf16[512,512]{1,0:T(8,128)(2,1)S(1)} %copy-done.1, bf16[512,1024]{1,0:T(8,128)(2,1)S(1)} %pad_maximum_fusion.k0_ref.v0_ref, bf16[512,1024]{1,0:T(8,128)(2,1)} %collective-permute-done.2.k1_ref.v1_ref, ...), custom_call_target="tpu_custom_call" | custom-call | flops 2097152 | bytes 1048576 | tf_op jit(solution)/shard_map/near_attention/pallas_call | solution.py:191
  47.3 15.5 %collective-permute-done.ka_ref.va_ref = bf16[512,1024]{1,0:T(8,128)(2,1)} collective-permute-done((bf16[512,1024]{1,0:T(8,128)(2,1)S(1)}, bf16[512,1024]{1,0:T(8,128)(2,1)}, u32[]{:S(2)}, u32[]{:S(2)}) %collective-permute-start) | collective-permute-done | bytes 1048608 | tf_op jit(solution)/shard_map/ppermute | solution.py:264
  62.8 2.3 %broadcast_select_fusion = bf16[512,1024]{1,0:T(8,128)(2,1)} fusion(bf16[512,1024]{1,0:T(8,128)(2,1)} %collective-permute-done.1.kc_ref.vc_ref, bf16[512,1024]{1,0:T(8,128)(2,1)} %collective-permute-done.ka_ref.va_ref, pred[]{:T(512)S(6)} %eq.5), kind=kLoop, calls=%fused_computation.30 | loop fusion | flops 524288 | bytes 3145729 | tf_op jit(solution)/shard_map/jit(_where)/select_n | solution.py:304
  65.1 3.5 %collective-permute-start.4 = (bf16[512,512]{1,0:T(8,128)(2,1)}, bf16[512,512]{1,0:T(8,128)(2,1)S(1)}, u32[]{:S(2)}, u32[]{:S(2)}) collective-permute-start(bf16[512,512]{1,0:T(8,128)(2,1)} %pad_maximum_fusion.1.k0_ref.v0_ref), channel_id=1, source_target_pairs={{0,2},{1,3},{2,4},{3,5},{4,6},{5,7},{6,8},{7,9},{8,10},{9,11},{10,... | collective-permute-start | bytes 1572872 | tf_op jit(solution)/shard_map/ppermute | solution.py:264
  68.6 6.1 %collective-permute-start.5 = (bf16[512,512]{1,0:T(8,128)(2,1)}, bf16[512,512]{1,0:T(8,128)(2,1)S(1)}, u32[]{:S(2)}, u32[]{:S(2)}) collective-permute-start(bf16[512,512]{1,0:T(8,128)(2,1)} %pad_maximum_fusion.1.k0_ref.v0_ref), channel_id=1, source_target_pairs={{2,0},{3,1},{4,2},{5,3},{6,4},{7,5},{8,6},{9,7},{10,8},{11,9},{12,... | collective-permute-start | bytes 1572872 | tf_op jit(solution)/shard_map/ppermute | solution.py:264
  74.7 0.1 pad_add_fusion.lim_ref
  74.8 1.0 copy-done.2
  75.9 1.2 copy-done.6
  77.1 1.2 copy-done.8
  78.3 1.2 copy-done.10
  79.5 13.8 %far_attention.2 = bf16[512,512]{1,0:T(8,128)(2,1)S(1)} custom-call(s32[3]{0:T(128)S(1)} %pad_add_fusion.lim_ref, bf16[512,512]{1,0:T(8,128)(2,1)S(1)} %copy-done.2, bf16[512,1024]{1,0:T(8,128)(2,1)} %collective-permute-done.ka_ref.va_ref, bf16[512,1024]{1,0:T(8,128)(2,1)} %collective-permute-done.6.kb_ref.vb_ref, ...), custom_call_target="tpu_custom_call" | custom-call | flops 3145728 | bytes 1048576 | tf_op jit(solution)/shard_map/far_attention/pallas_call | solution.py:212
  93.3 1.2 collective-permute-done.5.kc_ref.vc_ref
  94.6 0.1 broadcast_select_fusion.1
  94.6 0.1 collective-permute-start.7
  94.7 1.9 %collective-permute-done.7.kb_ref.vb_ref = bf16[512,512]{1,0:T(8,128)(2,1)S(1)} collective-permute-done((bf16[512,512]{1,0:T(8,128)(2,1)S(1)}, bf16[512,512]{1,0:T(8,128)(2,1)S(1)}, u32[]{:S(2)}, u32[]{:S(2)}) %collective-permute-start.7) | collective-permute-done | bytes 524320 | tf_op jit(solution)/shard_map/ppermute | solution.py:267
  96.6 0.0 slice-start.1
  96.6 6.8 %far_attention.3 = bf16[512,256]{1,0:T(8,128)(2,1)S(1)} custom-call(s32[3]{0:T(128)S(1)} %pad_add_fusion.lim_ref, bf16[512,256]{1,0:T(8,128)(2,1)S(1)} %copy-done.4, bf16[512,512]{1,0:T(8,128)(2,1)S(1)} %collective-permute-done.4.ka_ref.va_ref, bf16[512,512]{1,0:T(8,128)(2,1)S(1)} %collective-permute-done.7.kb_ref.vb_ref, ...), custom_call_target="tpu_custom_call" | custom-call | flops 1572864 | bytes 1048576 | tf_op jit(solution)/shard_map/far_attention/pallas_call | solution.py:212
  103.5 0.0 slice-start.2
  103.5 1.5 %fusion.33 = (f32[512]{0:T(512)S(1)}, f32[512,1536]{1,0:T(8,128)S(1)}) fusion(bf16[768,1536]{1,0:T(8,128)(2,1)S(1)} %copy-done, bf16[512,256]{1,0:T(8,128)(2,1)S(1)} %far_attention.3, bf16[512,512]{1,0:T(8,128)(2,1)S(1)} %far_attention.2, bf16[512,1536]{1,0:T(8,128)(2,1)S(1)} %copy-done.19), kind=kOutput, calls=%fused_computation.44 | convolution fusion | flops 1211891200 | bytes 7866368 | tf_op jit(solution)/shard_map/dot_general | solution.py:314
  105.0 0.5 multiply_reduce_fusion
  105.5 5.1 %fusion.11 = f32[512,3072]{1,0:T(8,128)S(1)} fusion(bf16[1536,3072]{1,0:T(8,128)(2,1)S(1)} %bitcast.11, f32[512,1536]{1,0:T(8,128)S(1)} %get-tuple-element.38.after_ref, f32[512]{0:T(512)S(1)} %add_rsqrt_fusion, f32[512]{0:T(512)S(1)} %broadcast_multiply_fusion), kind=kOutput, calls=%fused_computation.17 | convolution fusion | flops 4834197504 | bytes 18878464 | tf_op jit(solution)/shard_map/dot_general | solution.py:316
  110.6 0.8 fusion.8.gated_ref
  111.4 0.1 copy-done.17
  111.5 13.5 %conv_tail.1 = bf16[512,1536]{1,0:T(8,128)(2,1)S(1)} custom-call(bf16[512,1536]{1,0:T(8,128)(2,1)S(1)} %fusion.8.gated_ref, f32[512,1536]{1,0:T(8,128)S(1)} %get-tuple-element.38.after_ref, f32[31,1536]{1,0:T(8,128)S(1)} %copy-done.17), custom_call_target="tpu_custom_call" | custom-call | tf_op jit(solution)/shard_map/conv_tail/pallas_call | solution.py:237
  125.0 1.1 copy.15
  (46 shorter events, 0.1 us)
Async XLA Ops:
  0.0 103.5 %copy-start = (bf16[768,1536]{1,0:T(8,128)(2,1)S(1)}, bf16[768,1536]{1,0:T(8,128)(2,1)}, u32[]{:S(2)}) copy-start(bf16[768,1536]{1,0:T(8,128)(2,1)} %param.7) | copy-start | bytes 7077892
  0.0 3.8 %copy-start.18 = (bf16[512,1536]{1,0:T(8,128)(2,1)S(1)}, bf16[512,1536]{1,0:T(8,128)(2,1)}, u32[]{:S(2)}) copy-start(bf16[512,1536]{1,0:T(8,128)(2,1)} %param.5) | copy-start | bytes 4718596
  4.3 15.6 %copy-start.20 = (bf16[512,1536]{1,0:T(8,128)(2,1)}, bf16[512,1536]{1,0:T(8,128)(2,1)S(1)}, u32[]{:S(2)}) copy-start(bf16[512,1536]{1,0:T(8,128)(2,1)S(1)} %fusion.3) | copy-start | bytes 4718596
  9.8 26.7 %collective-permute-start.2 = (bf16[512,1024]{1,0:T(8,128)(2,1)S(1)}, bf16[512,1024]{1,0:T(8,128)(2,1)}, u32[]{:S(2)}, u32[]{:S(2)}) collective-permute-start(bf16[512,1024]{1,0:T(8,128)(2,1)S(1)} %pad_maximum_fusion.k0_ref.v0_ref), channel_id=1, source_target_pairs={{0,1},{1,0},{2,3},{3,2},{4,5},{5,4},{6,7},{7,6},{8,9},{9,8},{10,11... | collective-permute-start | bytes 3145736 | tf_op jit(solution)/shard_map/ppermute | solution.py:267
  9.8 37.4 %collective-permute-start.1 = (bf16[512,1024]{1,0:T(8,128)(2,1)S(1)}, bf16[512,1024]{1,0:T(8,128)(2,1)}, u32[]{:S(2)}, u32[]{:S(2)}) collective-permute-start(bf16[512,1024]{1,0:T(8,128)(2,1)S(1)} %pad_maximum_fusion.k0_ref.v0_ref), channel_id=1, source_target_pairs={{2,0},{3,1},{4,2},{5,3},{6,4},{7,5},{8,6},{9,7},{10,8},{11,9},{12,... | collective-permute-start | bytes 3145736 | tf_op jit(solution)/shard_map/ppermute | solution.py:264
  16.2 46.5 %collective-permute-start = (bf16[512,1024]{1,0:T(8,128)(2,1)S(1)}, bf16[512,1024]{1,0:T(8,128)(2,1)}, u32[]{:S(2)}, u32[]{:S(2)}) collective-permute-start(bf16[512,1024]{1,0:T(8,128)(2,1)S(1)} %pad_maximum_fusion.k0_ref.v0_ref), channel_id=1, source_target_pairs={{0,2},{1,3},{2,4},{3,5},{4,6},{5,7},{6,8},{7,9},{8,10},{9,11},{10,... | collective-permute-start | bytes 3145736 | tf_op jit(solution)/shard_map/ppermute | solution.py:264
  22.4 5.4 %collective-permute-start.3 = (bf16[512,512]{1,0:T(8,128)(2,1)}, bf16[512,512]{1,0:T(8,128)(2,1)}, u32[]{:S(2)}, u32[]{:S(2)}) collective-permute-start(bf16[512,512]{1,0:T(8,128)(2,1)} %pad_maximum_fusion.1.k0_ref.v0_ref), channel_id=1, source_target_pairs={{0,1},{1,0},{2,3},{3,2},{4,5},{5,4},{6,7},{7,6},{8,9},{9,8},{10,11... | collective-permute-start | bytes 1572872 | tf_op jit(solution)/shard_map/ppermute | solution.py:267
  27.8 1.0 copy-start.3
  34.0 0.8 copy-start.11
  34.8 0.8 copy-start.13
  35.6 0.9 copy-start.15
  36.5 1.0 copy-start.1
  47.2 17.8 %copy-start.5 = (f32[512,512]{1,0:T(8,128)}, f32[512,512]{1,0:T(8,128)S(1)}, u32[]{:S(2)}) copy-start(f32[512,512]{1,0:T(8,128)S(1)} %get-tuple-element.28.acc_ref) | copy-start | bytes 3145732
  47.2 21.4 %copy-start.7 = (f32[512,512]{1,0:T(8,128)}, f32[512,512]{1,0:T(8,128)S(1)}, u32[]{:S(2)}) copy-start(f32[512,512]{1,0:T(8,128)S(1)} %get-tuple-element.29.high_ref) | copy-start | bytes 3145732
  47.2 21.4 %copy-start.9 = (f32[512,512]{1,0:T(8,128)}, f32[512,512]{1,0:T(8,128)S(1)}, u32[]{:S(2)}) copy-start(f32[512,512]{1,0:T(8,128)S(1)} %get-tuple-element.30.total_ref) | copy-start | bytes 3145732
  65.1 9.8 %collective-permute-start.6 = (bf16[512,1024]{1,0:T(8,128)(2,1)}, bf16[512,1024]{1,0:T(8,128)(2,1)}, u32[]{:S(2)}, u32[]{:S(2)}) collective-permute-start(bf16[512,1024]{1,0:T(8,128)(2,1)} %broadcast_select_fusion), channel_id=1, source_target_pairs={{0,1},{1,0},{2,3},{3,2},{4,5},{5,4},{6,7},{7,6},{8,9},{9,8},{10,11... | collective-permute-start | bytes 3145736 | tf_op jit(solution)/shard_map/ppermute | solution.py:267
  65.1 28.3 %collective-permute-start.4 = (bf16[512,512]{1,0:T(8,128)(2,1)}, bf16[512,512]{1,0:T(8,128)(2,1)S(1)}, u32[]{:S(2)}, u32[]{:S(2)}) collective-permute-start(bf16[512,512]{1,0:T(8,128)(2,1)} %pad_maximum_fusion.1.k0_ref.v0_ref), channel_id=1, source_target_pairs={{0,2},{1,3},{2,4},{3,5},{4,6},{5,7},{6,8},{7,9},{8,10},{9,11},{10,... | collective-permute-start | bytes 1572872 | tf_op jit(solution)/shard_map/ppermute | solution.py:264
  68.6 25.9 %collective-permute-start.5 = (bf16[512,512]{1,0:T(8,128)(2,1)}, bf16[512,512]{1,0:T(8,128)(2,1)S(1)}, u32[]{:S(2)}, u32[]{:S(2)}) collective-permute-start(bf16[512,512]{1,0:T(8,128)(2,1)} %pad_maximum_fusion.1.k0_ref.v0_ref), channel_id=1, source_target_pairs={{2,0},{3,1},{4,2},{5,3},{6,4},{7,5},{8,6},{9,7},{10,8},{11,9},{12,... | collective-permute-start | bytes 1572872 | tf_op jit(solution)/shard_map/ppermute | solution.py:264
  74.8 1.0 copy-start.2
  75.9 1.2 copy-start.6
  77.1 1.2 copy-start.8
  78.3 1.2 copy-start.10
  79.5 17.1 %copy-start.4 = (bf16[512,256]{1,0:T(8,128)(2,1)S(1)}, bf16[512,256]{1,0:T(8,128)(2,1)}, u32[]{:S(2)}) copy-start(bf16[512,256]{1,0:T(8,128)(2,1)} %slice.37.q_ref) | copy-start | bytes 786436
  79.5 17.1 %copy-start.12 = (f32[512,256]{1,0:T(8,128)S(1)}, f32[512,256]{1,0:T(8,128)}, u32[]{:S(2)}) copy-start(f32[512,256]{1,0:T(8,128)} %copy-done.11) | copy-start | bytes 1572868
  79.5 17.1 %copy-start.14 = (f32[512,256]{1,0:T(8,128)S(1)}, f32[512,256]{1,0:T(8,128)}, u32[]{:S(2)}) copy-start(f32[512,256]{1,0:T(8,128)} %copy-done.13) | copy-start | bytes 1572868
  79.5 17.1 %copy-start.16 = (f32[512,256]{1,0:T(8,128)S(1)}, f32[512,256]{1,0:T(8,128)}, u32[]{:S(2)}) copy-start(f32[512,256]{1,0:T(8,128)} %copy-done.15) | copy-start | bytes 1572868
  93.3 10.1 %copy-start.19 = (bf16[512,1536]{1,0:T(8,128)(2,1)S(1)}, bf16[512,1536]{1,0:T(8,128)(2,1)}, u32[]{:S(2)}) copy-start(bf16[512,1536]{1,0:T(8,128)(2,1)} %param.5) | copy-start | bytes 4718596
  94.6 10.9 %slice-start = ((s8[9437184]{0:T(1024)(128)(4,1)}), s8[4194304]{0:T(1024)(128)(4,1)S(1)}, s32[]{:S(2)}) async-start(s8[9437184]{0:T(1024)(128)(4,1)} %bitcast.10), calls=%async_computation | async-start | bytes 8388608
  94.6 2.0 %collective-permute-start.7 = (bf16[512,512]{1,0:T(8,128)(2,1)S(1)}, bf16[512,512]{1,0:T(8,128)(2,1)S(1)}, u32[]{:S(2)}, u32[]{:S(2)}) collective-permute-start(bf16[512,512]{1,0:T(8,128)(2,1)S(1)} %broadcast_select_fusion.1), channel_id=1, source_target_pairs={{0,1},{1,0},{2,3},{3,2},{4,5},{5,4},{6,7},{7,6},{8,9},{9,8},{10,11... | collective-permute-start | bytes 1572872 | tf_op jit(solution)/shard_map/ppermute | solution.py:267
  96.6 8.8 %slice-start.1 = ((s8[9437184]{0:T(1024)(128)(4,1)}), s8[4194304]{0:T(1024)(128)(4,1)S(1)}, s32[]{:S(2)}) async-start(s8[9437184]{0:T(1024)(128)(4,1)} %bitcast.10), calls=%async_computation.1 | async-start | bytes 8388608
  103.5 2.0 %slice-start.2 = ((s8[9437184]{0:T(1024)(128)(4,1)}), s8[1048576]{0:T(1024)(128)(4,1)S(1)}, s32[]{:S(2)}) async-start(s8[9437184]{0:T(1024)(128)(4,1)} %bitcast.10), calls=%async_computation.2 | async-start | bytes 2097152
  110.6 0.9 copy-start.17
